TPU v7x, 32 devices: a whole 2x2x4 slice. The times are simulated.
32 devices in a mesh: dp: 4 (over z), fsdp: 8 (over y, x, core).
Axes of the slice: x: 2, y: 2, z: 4, core: 2. Of those that a mesh axis runs over, the one named last changes fastest.
Arguments:
- gate_act: bfloat16 [2048, 14848], P('fsdp', 'dp'), may hold values from -6 to 6
- up_act: bfloat16 [2048, 14848], P('fsdp', 'dp'), may hold values from -6 to 6
- out_grad: bfloat16 [2048, 4096], P('fsdp'), may hold values from -6 to 6
- master_old: float32 [4, 4992, 4096], P('dp', 'fsdp'), may hold values from -0.046875 to 0.046875
- moment1_old: float32 [4, 4992, 4096], P('dp', 'fsdp'), may hold values from -4 to 4
- moment2_old: float32 [4, 4992, 4096], P('dp', 'fsdp'), may hold values from 0.02 to 4
- old_bounds: int32 [4, 9], P('dp'), may hold values from 0 to 3712, as said below
- new_bounds: int32 [4, 8], P('dp'), may hold values from 0 to 3712, as said below
- rank_map: int32 [4, 8], P('dp'), may hold values from 0 to 7, as said below
Outputs:
- mlp_out: float32 [2048, 4096], P('fsdp', 'dp')
- master_new: float32 [4, 4992, 4096], P('dp', 'fsdp')
- moment1_new: float32 [4, 4992, 4096], P('dp', 'fsdp')
- moment2_new: float32 [4, 4992, 4096], P('dp', 'fsdp')
Inputs may be any that keep to these rules, and one draw needn't show every extreme that they name: Each row of old_bounds starts at 0, ends at 3712 and never falls; each position's rows fit its 624 slots. Each row of new_bounds starts at 0, ends at 3712 and never falls; each rank's rows fit 624 slots. In every block a position's new rows lie within its old rows and at most 232 rows of each of its two neighbours. `rank_map`: in each block's row exactly one position, one of the two middle ones, has rank 8 - 1 and owns nothing; the others hold the ranks 0 to 6 in position order.
All inputs are finite; a program needn't handle non-finite values.
Results may differ from a plain program's by a relative error of at most 0.012.
Values may be sent and summed in bfloat16 or wider, within the bound.
No kernel may reach another device: no remote copies, remote signals or barrier semaphores. Data moves between devices by JAX's collectives and lax.ppermute only.
A program may use at most 384 MiB of HBM per device.

v0:
```python
import math

import jax
import jax.numpy as jnp
from jax import lax
from jax.sharding import PartitionSpec as P


def passed_along(value, axis, steps):
    count = lax.axis_size(axis)
    leading, last = (max(0, -steps), min(count, count - steps))
    return lax.ppermute(value, axis, [(source, source + steps) for source in range(leading, last)])


def pick_entry(table, index):
    return jnp.sum(jnp.where(jnp.arange(table.shape[0]) == index, table, jnp.zeros_like(table)))


def migrate(stacked, moved_rows, my_old_start, my_old_count, my_new_start, my_new_count):
    slot_rows = stacked.shape[1]
    prefix = stacked[:, :moved_rows]
    padded = jnp.concatenate(
        [jnp.zeros((3, moved_rows, stacked.shape[2]), stacked.dtype), stacked], axis=1
    )
    suffix = lax.dynamic_slice_in_dim(padded, my_old_count, moved_rows, 1)
    from_right = passed_along(prefix.astype(jnp.bfloat16), "fsdp", -1).astype(prefix.dtype)
    from_left = passed_along(suffix.astype(jnp.bfloat16), "fsdp", 1).astype(suffix.dtype)
    source = jnp.concatenate([from_left, stacked, from_right], axis=1)
    row_index = jnp.arange(slot_rows)
    global_row = my_new_start + row_index
    my_old_end = my_old_start + my_old_count
    index = (
        moved_rows
        + global_row
        - my_old_start
        + jnp.where(global_row >= my_old_end, slot_rows - my_old_count, 0)
    )
    index = jnp.clip(index, 0, 2 * moved_rows + slot_rows - 1)
    chosen = jnp.take(source, index, axis=1)
    return jnp.where((row_index < my_new_count)[None, :, None], chosen, jnp.zeros_like(chosen))


def block_product(hidden, weight_shard, table_start, table_count):
    slot_rows = weight_shard.shape[0]
    padded_hidden = jnp.concatenate(
        [hidden, jnp.zeros((hidden.shape[0], slot_rows), hidden.dtype)], axis=1
    )
    row_index = jnp.arange(slot_rows)[:, None]
    empty = jnp.zeros((hidden.shape[0], weight_shard.shape[1]), jnp.float32)
    piece = lax.all_gather(weight_shard, "fsdp", axis=0, tiled=True)
    shard_count = piece.shape[0] // slot_rows
    blocks = piece.reshape(shard_count, slot_rows, piece.shape[1])

    def one_shard(step, carry):
        start_col = pick_entry(table_start, step)
        live_rows = pick_entry(table_count, step)
        block = lax.dynamic_index_in_dim(blocks, step, 0, keepdims=False)
        block = jnp.where(row_index < live_rows, block, jnp.zeros_like(block))
        columns = lax.dynamic_slice_in_dim(padded_hidden, start_col, slot_rows, 1)
        return carry + jnp.dot(columns, block, preferred_element_type=jnp.float32)

    return lax.fori_loop(0, shard_count, one_shard, empty)


def local(
    gate_act,
    up_act,
    out_grad,
    master_old,
    moment1_old,
    moment2_old,
    old_bounds,
    new_bounds,
    rank_map,
):
    ranks_total = lax.axis_size("fsdp")
    my_position = lax.axis_index("fsdp")
    slot_rows = master_old.shape[1]
    token_rows = gate_act.shape[0]
    block_rows = gate_act.shape[1]
    base_rows = block_rows // ranks_total
    moved_rows = (base_rows + 1) // 2
    grad_scale = 1.0 / math.sqrt(token_rows * ranks_total)
    my_old_bounds = old_bounds[0]
    my_new_bounds = new_bounds[0]
    my_rank_map = rank_map[0]
    old_start = my_old_bounds[:-1]
    old_count = my_old_bounds[1:] - my_old_bounds[:-1]
    extended = jnp.concatenate([my_new_bounds, my_new_bounds[-1:]])
    extended_next = jnp.concatenate([extended[1:], extended[-1:]])
    owner_hit = my_rank_map[:, None] == jnp.arange(ranks_total + 1)[None, :]
    new_start = jnp.sum(jnp.where(owner_hit, extended[None, :], 0), axis=1)
    new_count = jnp.sum(jnp.where(owner_hit, extended_next[None, :], 0), axis=1) - new_start
    hidden = (jax.nn.silu(gate_act.astype(jnp.float32)) * up_act.astype(jnp.float32)).astype(
        jnp.bfloat16
    )
    stacked = jnp.stack([master_old[0], moment1_old[0], moment2_old[0]])
    moved = migrate(
        stacked,
        moved_rows,
        pick_entry(old_start, my_position),
        pick_entry(old_count, my_position),
        pick_entry(new_start, my_position),
        pick_entry(new_count, my_position),
    )
    weight_shard = master_old[0].astype(jnp.bfloat16)
    block_part = block_product(hidden, weight_shard, old_start, old_count)
    mlp_out = lax.psum_scatter(
        block_part.astype(jnp.bfloat16), "dp", scatter_dimension=1, tiled=True
    ).astype(jnp.float32)
    row_index = jnp.arange(slot_rows * lax.axis_size("fsdp"))
    position = row_index // slot_rows
    within = row_index % slot_rows
    hit = position[:, None] == jnp.arange(ranks_total)[None, :]
    start_col = jnp.sum(jnp.where(hit, new_start[None, :], 0), axis=1)
    live_rows = jnp.sum(jnp.where(hit, new_count[None, :], 0), axis=1)
    column = jnp.clip(start_col + within, 0, block_rows - 1)
    chosen = jnp.take(hidden, column, axis=1)
    chosen = jnp.where((within < live_rows)[None, :], chosen, jnp.zeros_like(chosen))
    grad = (
        lax.psum_scatter(
            lax.dot_general(
                chosen, out_grad, (((0,), (0,)), ((), ())), preferred_element_type=jnp.float32
            ).astype(jnp.bfloat16),
            "fsdp",
            scatter_dimension=0,
            tiled=True,
        ).astype(jnp.float32)
        * grad_scale
    )
    first_next = 0.9 * moved[1] + 0.1 * grad
    second_next = 0.95 * moved[2] + 0.05 * grad * grad
    master_next = moved[0] - 0.001 * (first_next / (jnp.sqrt(second_next) + 1e-08) + 0.1 * moved[0])
    return (mlp_out, master_next[None], first_next[None], second_next[None])


def solution(mesh):
    placed = (
        P("fsdp", "dp"),
        P("fsdp", "dp"),
        P("fsdp", None),
        P("dp", "fsdp", None),
        P("dp", "fsdp", None),
        P("dp", "fsdp", None),
        P("dp", None),
        P("dp", None),
        P("dp", None),
    )
    return jax.shard_map(
        local,
        mesh=mesh,
        in_specs=placed,
        out_specs=(
            P("fsdp", "dp"),
            P("dp", "fsdp", None),
            P("dp", "fsdp", None),
            P("dp", "fsdp", None),
        ),
        check_vma=False,
    )
```

profile of v0, /device:TPU:11, one launch (start us, length us, event | category | flops | bytes accessed | tf_op | source)
XLA Modules:
  0.0 662.1 jit_solution(13614917913296723851)
XLA Ops:
  7.2 15.1 %constant_dynamic-update-slice_fusion.2 = (f32[3,624,4096]{2,1,0:T(8,128)}, bf16[1,624,4096]{2,1,0:T(8,128)(2,1)}) fusion(f32[1,624,4096]{2,1,0:T(8,128)} %param.14), kind=kLoop, calls=%fused_computation.77 | loop fusion | flops 2555903 | bytes 25559040
  23.8 3.9 copy.45
  27.7 3.9 copy.46
  33.5 5.4 fusion.24
  38.9 14.9 %gather_fusion.1 = bf16[4992,256]{1,0:T(8,128)(2,1)} fusion(bf16[256,3712]{0,1:T(8,128)(2,1)} %fusion.24, s32[5120]{0:T(1024)S(1)} %pad_clamp_fusion), kind=kCustom, calls=%fused_computation.1 | custom fusion | bytes 5131776 | tf_op jit(solution)/shard_map/jit(_take)/gather | solution.py:118
  53.8 19.3 %convolution_convert_fusion = bf16[4992,4096]{1,0:T(8,128)(2,1)} fusion(bf16[256,4096]{1,0:T(8,128)(2,1)S(1)} %copy-done, bf16[4992,256]{1,0:T(8,128)(2,1)} %gather_fusion.1, pred[4992]{0:T(1024)(128)(4,1)S(1)} %get-tuple-element.213, pred[4992]{0:T(1024)(128)(4,1)S(1)} %get-tuple-element.214), kind=kOutput, calls=%fused_computation.18 | convolution fusion | flops 10491985920 | bytes 45557504 | tf_op jit(solution)/shard_map/dot_general | solution.py:122
  76.4 9.0 %constant_dynamic-update-slice_fusion.1 = f32[3,624,4096]{2,1,0:T(8,128)} fusion(f32[3,624,4096]{2,1,0:T(8,128)} %get-tuple-element.209, f32[1,624,4096]{2,1,0:T(8,128)} %param.15), kind=kLoop, calls=%fused_computation.76 | loop fusion | bytes 20447232
  85.3 9.0 %constant_dynamic-update-slice_fusion = f32[3,624,4096]{2,1,0:T(8,128)} fusion(f32[3,624,4096]{2,1,0:T(8,128)} %constant_dynamic-update-slice_fusion.1, f32[1,624,4096]{2,1,0:T(8,128)} %param.16), kind=kLoop, calls=%fused_computation.75 | loop fusion | bytes 20447232 | tf_op jit(solution)/shard_map/stack | solution.py:97
  94.4 15.4 %fusion.12 = (bf16[3,232,4096]{2,1,0:T(8,128)(2,1)}, bf16[3,232,4096]{2,1,0:T(8,128)(2,1)}) fusion(s32[]{:T(128)S(6)} %select_n.170, f32[3,624,4096]{2,1,0:T(8,128)} %constant_dynamic-update-slice_fusion), kind=kLoop, calls=%fused_computation.25 | loop fusion | bytes 47775748 | tf_op jit(solution)/shard_map/convert_element_type | solution.py:27
  109.8 4.0 collective-permute-start
  113.8 2.1 collective-permute-start.1
  117.8 1.5 concatenate.15
  119.3 1.3 fusion.40
  122.4 209.6 %collective-permute-done = bf16[3,232,4096]{2,1,0:T(8,128)(2,1)} collective-permute-done((bf16[3,232,4096]{2,1,0:T(8,128)(2,1)}, bf16[3,232,4096]{2,1,0:T(8,128)(2,1)}, u32[]{:S(2)}, u32[]{:S(2)}) %collective-permute-start) | collective-permute-done | bytes 5701664 | tf_op jit(solution)/shard_map/ppermute | solution.py:12
  332.0 12.1 %convert_element_type.45 = f32[3,232,4096]{2,1,0:T(8,128)} convert(bf16[3,232,4096]{2,1,0:T(8,128)(2,1)} %collective-permute-done) | non-fusion elementwise | flops 2850816 | bytes 17104896 | tf_op jit(solution)/shard_map/convert_element_type | solution.py:27
  344.1 12.1 %convert_element_type.46 = f32[3,232,4096]{2,1,0:T(8,128)} convert(bf16[3,232,4096]{2,1,0:T(8,128)(2,1)} %collective-permute-done.1) | non-fusion elementwise | flops 2850816 | bytes 17104896 | tf_op jit(solution)/shard_map/convert_element_type | solution.py:26
  356.2 38.2 %pad_maximum_fusion = f32[3,1088,4096]{2,1,0:T(8,128)} fusion(f32[3,232,4096]{2,1,0:T(8,128)} %convert_element_type.46, f32[3,624,4096]{2,1,0:T(8,128)} %constant_dynamic-update-slice_fusion, f32[3,232,4096]{2,1,0:T(8,128)} %convert_element_type.45), kind=kLoop, calls=%fused_computation.16 | loop fusion | flops 26738688 | bytes 106954752 | tf_op jit(solution)/shard_map/concatenate | solution.py:28
  394.4 68.0 %copy.48 = f32[3,1088,4096]{2,0,1:T(4,128)} copy(f32[3,1088,4096]{2,1,0:T(8,128)} %pad_maximum_fusion) | data formatting | bytes 106954752 | tf_op jit(solution)/shard_map/concatenate | solution.py:28
  462.5 40.5 %gather_fusion = f32[624,3,4096]{2,1,0:T(4,128)} fusion(f32[3,1088,4096]{2,0,1:T(4,128)} %copy.48, s32[1024]{0:T(1024)S(1)} %pad_clamp_fusion.1), kind=kCustom, calls=%fused_computation | custom fusion | bytes 61344192 | tf_op jit(solution)/shard_map/jit(_take)/gather | solution.py:39
  503.0 88.8 %while.14 = (s32[]{:T(128)}, f32[256,4096]{1,0:T(8,128)}, s32[8]{0:T(128)S(1)}, bf16[256,4336]{0,1:T(8,128)(2,1)}, s32[8]{0:T(128)S(1)}, /*index=5*/bf16[8,624,4...) while((s32[]{:T(128)}, f32[256,4096]{1,0:T(8,128)}, s32[8]{0:T(128)S(1)}, ...), condition=%wide.region_3.4_spmd.clone, body=%wide.region_0.3_spmd.clone.sunk | while | flops 1313276544 | bytes 13821385 | solution.py:62
  506.2 6.9 %convolution_add_fusion.2 = f32[256,4096]{1,0:T(8,128)} fusion(bf16[8,624,4096]{2,1,0:T(8,128)(2,1)} %get-tuple-element.279, s32[]{:T(128)S(6)} %copy.58, pred[624]{0:T(1024)(128)(4,1)S(1)} %compare_reduce_fusion.2, f32[256,4096]{1,0:T(8,128)} %get-tuple-element.266, pred[]{:T(512)S(6)} %compare.5, bf16[256,4336]{0,1:T(8,128)(2,1)} %get-tuple-element.277, ...), kind=kOutput, calls=%fused_computation.3.clone.1 | convolution fusion | flops 1313275904 | bytes 13820537 | tf_op jit(solution)/shard_map/while/body/eval_jaxpr/dot_general | solution.py:60
  516.5 8.2 %convolution_add_fusion.2 = f32[256,4096]{1,0:T(8,128)} fusion(bf16[8,624,4096]{2,1,0:T(8,128)(2,1)} %get-tuple-element.279, s32[]{:T(128)S(6)} %copy.58, pred[624]{0:T(1024)(128)(4,1)S(1)} %compare_reduce_fusion.2, f32[256,4096]{1,0:T(8,128)} %get-tuple-element.266, pred[]{:T(512)S(6)} %compare.5, bf16[256,4336]{0,1:T(8,128)(2,1)} %get-tuple-element.277, ...), kind=kOutput, calls=%fused_computation.3.clone.1 | convolution fusion | flops 1313275904 | bytes 13820537 | tf_op jit(solution)/shard_map/while/body/eval_jaxpr/dot_general | solution.py:60
  527.9 8.1 %convolution_add_fusion.2 = f32[256,4096]{1,0:T(8,128)} fusion(bf16[8,624,4096]{2,1,0:T(8,128)(2,1)} %get-tuple-element.279, s32[]{:T(128)S(6)} %copy.58, pred[624]{0:T(1024)(128)(4,1)S(1)} %compare_reduce_fusion.2, f32[256,4096]{1,0:T(8,128)} %get-tuple-element.266, pred[]{:T(512)S(6)} %compare.5, bf16[256,4336]{0,1:T(8,128)(2,1)} %get-tuple-element.277, ...), kind=kOutput, calls=%fused_computation.3.clone.1 | convolution fusion | flops 1313275904 | bytes 13820537 | tf_op jit(solution)/shard_map/while/body/eval_jaxpr/dot_general | solution.py:60
  539.2 8.0 %convolution_add_fusion.2 = f32[256,4096]{1,0:T(8,128)} fusion(bf16[8,624,4096]{2,1,0:T(8,128)(2,1)} %get-tuple-element.279, s32[]{:T(128)S(6)} %copy.58, pred[624]{0:T(1024)(128)(4,1)S(1)} %compare_reduce_fusion.2, f32[256,4096]{1,0:T(8,128)} %get-tuple-element.266, pred[]{:T(512)S(6)} %compare.5, bf16[256,4336]{0,1:T(8,128)(2,1)} %get-tuple-element.277, ...), kind=kOutput, calls=%fused_computation.3.clone.1 | convolution fusion | flops 1313275904 | bytes 13820537 | tf_op jit(solution)/shard_map/while/body/eval_jaxpr/dot_general | solution.py:60
  550.4 8.0 %convolution_add_fusion.2 = f32[256,4096]{1,0:T(8,128)} fusion(bf16[8,624,4096]{2,1,0:T(8,128)(2,1)} %get-tuple-element.279, s32[]{:T(128)S(6)} %copy.58, pred[624]{0:T(1024)(128)(4,1)S(1)} %compare_reduce_fusion.2, f32[256,4096]{1,0:T(8,128)} %get-tuple-element.266, pred[]{:T(512)S(6)} %compare.5, bf16[256,4336]{0,1:T(8,128)(2,1)} %get-tuple-element.277, ...), kind=kOutput, calls=%fused_computation.3.clone.1 | convolution fusion | flops 1313275904 | bytes 13820537 | tf_op jit(solution)/shard_map/while/body/eval_jaxpr/dot_general | solution.py:60
  561.7 7.9 %convolution_add_fusion.2 = f32[256,4096]{1,0:T(8,128)} fusion(bf16[8,624,4096]{2,1,0:T(8,128)(2,1)} %get-tuple-element.279, s32[]{:T(128)S(6)} %copy.58, pred[624]{0:T(1024)(128)(4,1)S(1)} %compare_reduce_fusion.2, f32[256,4096]{1,0:T(8,128)} %get-tuple-element.266, pred[]{:T(512)S(6)} %compare.5, bf16[256,4336]{0,1:T(8,128)(2,1)} %get-tuple-element.277, ...), kind=kOutput, calls=%fused_computation.3.clone.1 | convolution fusion | flops 1313275904 | bytes 13820537 | tf_op jit(solution)/shard_map/while/body/eval_jaxpr/dot_general | solution.py:60
  572.8 7.9 %convolution_add_fusion.2 = f32[256,4096]{1,0:T(8,128)} fusion(bf16[8,624,4096]{2,1,0:T(8,128)(2,1)} %get-tuple-element.279, s32[]{:T(128)S(6)} %copy.58, pred[624]{0:T(1024)(128)(4,1)S(1)} %compare_reduce_fusion.2, f32[256,4096]{1,0:T(8,128)} %get-tuple-element.266, pred[]{:T(512)S(6)} %compare.5, bf16[256,4336]{0,1:T(8,128)(2,1)} %get-tuple-element.277, ...), kind=kOutput, calls=%fused_computation.3.clone.1 | convolution fusion | flops 1313275904 | bytes 13820537 | tf_op jit(solution)/shard_map/while/body/eval_jaxpr/dot_general | solution.py:60
  583.9 7.9 %convolution_add_fusion.2 = f32[256,4096]{1,0:T(8,128)} fusion(bf16[8,624,4096]{2,1,0:T(8,128)(2,1)} %get-tuple-element.279, s32[]{:T(128)S(6)} %copy.58, pred[624]{0:T(1024)(128)(4,1)S(1)} %compare_reduce_fusion.2, f32[256,4096]{1,0:T(8,128)} %get-tuple-element.266, pred[]{:T(512)S(6)} %compare.5, bf16[256,4336]{0,1:T(8,128)(2,1)} %get-tuple-element.277, ...), kind=kOutput, calls=%fused_computation.3.clone.1 | convolution fusion | flops 1313275904 | bytes 13820537 | tf_op jit(solution)/shard_map/while/body/eval_jaxpr/dot_general | solution.py:60
  591.7 3.8 convert_element_type.42
  595.6 32.8 %fusion.11 = f32[3,624,4096]{2,1,0:T(8,128)} fusion(f32[624,3,4096]{2,1,0:T(4,128)} %gather_fusion, pred[624]{0:T(1024)(128)(4,1)S(1)} %iota_compare_fusion.2, pred[624]{0:T(1024)(128)(4,1)S(1)} %compare_and_fusion.1), kind=kLoop, calls=%fused_computation.21 | loop fusion | flops 15335424 | bytes 61342944 | tf_op jit(solution)/shard_map/jit(_where)/select_n | solution.py:40
  628.4 25.0 %fusion.19 = (f32[1,624,4096]{2,1,0:T(8,128)}, f32[1,624,4096]{2,1,0:T(8,128)}, f32[1,624,4096]{2,1,0:T(8,128)}) fusion(bf16[624,4096]{1,0:T(8,128)(2,1)} %reduce-scatter.5.cloned.1.call-done, f32[3,624,4096]{2,1,0:T(8,128)} %fusion.11), kind=kLoop, calls=%fused_computation.37 | loop fusion | flops 38338560 | bytes 66453504 | tf_op jit(solution)/shard_map/broadcast_in_dim | solution.py:134
  653.5 2.1 convert_element_type.43
  (55 shorter events, 17.1 us)
Async XLA Ops:
  7.2 46.6 %copy-start = (bf16[256,4096]{1,0:T(8,128)(2,1)S(1)}, bf16[256,4096]{1,0:T(8,128)(2,1)}, u32[]{:S(2)}) copy-start(bf16[256,4096]{1,0:T(8,128)(2,1)} %param.13) | copy-start | bytes 6291460
  7.2 15.2 %copy-start.5 = (s32[1,8]{1,0:T(1,128)S(1)}, s32[1,8]{1,0:T(1,128)}, u32[]{:S(2)}) copy-start(s32[1,8]{1,0:T(1,128)} %param.18) | copy-start | bytes 100
  7.2 495.8 %all-gather.3.cloned.1.call-start = ((), (), s32[]{:S(2)}) async-start(), calls=%async_computation.4 | async-start | bytes 46006272 | tf_op jit(solution)/shard_map/all_gather | solution.py:50
  22.3 10.0 %copy-start.4 = (s32[1,8]{1,0:T(1,128)S(1)}, s32[1,8]{1,0:T(1,128)}, u32[]{:S(2)}) copy-start(s32[1,8]{1,0:T(1,128)} %param.19) | copy-start | bytes 100
  22.4 606.0 %reduce-scatter.5.cloned.1.call-start = ((), (), s32[]{:S(2)}) async-start(), calls=%async_computation.3 | async-start | bytes 46006272 | tf_op jit(solution)/shard_map/reduce_scatter | solution.py:121
  73.1 0.7 copy-start.3
  73.1 580.3 %reduce-scatter.3.cloned.1.call-start = ((), (), s32[]{:S(2)}) async-start(), calls=%async_computation.2 | async-start | bytes 2621440 | tf_op jit(solution)/shard_map/reduce_scatter | solution.py:108
  94.4 23.4 %copy-start.2 = (bf16[256,3712]{0,1:T(8,128)(2,1)S(1)}, bf16[256,3712]{0,1:T(8,128)(2,1)}, u32[]{:S(2)}) copy-start(bf16[256,3712]{0,1:T(8,128)(2,1)} %fusion.24) | copy-start | bytes 5701636
  109.8 222.2 %collective-permute-start = (bf16[3,232,4096]{2,1,0:T(8,128)(2,1)}, bf16[3,232,4096]{2,1,0:T(8,128)(2,1)}, u32[]{:S(2)}, u32[]{:S(2)}) collective-permute-start(bf16[3,232,4096]{2,1,0:T(8,128)(2,1)} %get-tuple-element.207), channel_id=1, source_target_pairs={{0,1},{1,2},{2,3},{3,4},{4,5},{5,6},{6,7},{8,9},{9,10},{10,11},{11... | collective-permute-start | bytes 17104904 | tf_op jit(solution)/shard_map/ppermute | solution.py:12
  113.8 230.3 %collective-permute-start.1 = (bf16[3,232,4096]{2,1,0:T(8,128)(2,1)}, bf16[3,232,4096]{2,1,0:T(8,128)(2,1)}, u32[]{:S(2)}, u32[]{:S(2)}) collective-permute-start(bf16[3,232,4096]{2,1,0:T(8,128)(2,1)} %get-tuple-element.208), channel_id=1, source_target_pairs={{1,0},{2,1},{3,2},{4,3},{5,4},{6,5},{7,6},{9,8},{10,9},{11,10},{12... | collective-permute-start | bytes 17104904 | tf_op jit(solution)/shard_map/ppermute | solution.py:12
  628.4 27.2 %copy-start.1 = (bf16[256,4096]{1,0:T(8,128)(2,1)S(1)}, bf16[256,4096]{1,0:T(8,128)(2,1)}, u32[]{:S(2)}) copy-start(bf16[256,4096]{1,0:T(8,128)(2,1)} %param.13) | copy-start | bytes 6291460
Sparse Core Ops, SparseCore 0:
  22.5 282.9 all-gather.2
  309.2 243.1 reduce-scatter.4
  595.7 42.6 reduce-scatter.2
where the time goes:
time: 665 us; the launch traced here: 662 us
  waiting for transfers between devices  210 us (32%)
  local copies, waits for them, and re-layouts  167 us (25%)
  other arithmetic  164 us (25%)
  matrix products  82 us (12%)
  between operations  17.6 us (3%)
  loops' own time  15.6 us (2%)
    ppermute x2, waiting for transfers between devices, passed_along(): lax.ppermute(value, axis, [(source, source + steps) for source in range(l...  210 us
    concatenate x1, local copies, waits for them, and re-layouts, migrate(): source = jnp.concatenate([from_left, stacked, from_right], axis=1)  68 us
    dot_general x8, matrix products, one_shard(): return carry + jnp.dot(columns, block, preferred_element_type=jnp.float32)  62.7 us
    gather x1, local copies, waits for them, and re-layouts, migrate(): chosen = jnp.take(source, index, axis=1)  40.5 us
    concatenate x1, other arithmetic, migrate(): source = jnp.concatenate([from_left, stacked, from_right], axis=1)  38.2 us
    select_n x1, other arithmetic, migrate(): jnp.where((row_index < my_new_count)[None, :, None], chosen, jnp.zeros_li...  32.8 us
    broadcast_in_dim x1, other arithmetic, local(): return (mlp_out, master_next[None], first_next[None], second_next[None])  25 us
    dot_general x1, matrix products, local(): lax.dot_general(chosen, out_grad, (((0,), (0,)), ((), ())), preferred_ele...  19.3 us
  transfers between devices with their start and end apart: 5, of which 1 were waited for; matrix products, arithmetic and copies ran while one was open for 60% of the time, Pallas kernels for 0%

commit v1 on v0

v1 whole, which is shorter than its diff:
```python
import functools
import math

import jax
import jax.numpy as jnp
from jax import lax
from jax.experimental import pallas as pl
from jax.experimental.pallas import tpu as pltpu
from jax.sharding import PartitionSpec as P

BF16 = jnp.bfloat16
F32 = jnp.float32
VMEM_BYTES = 58 * 1024 * 1024
SMEM = pl.BlockSpec(memory_space=pltpu.SMEM)


def round_up(value, step):
    return -(-value // step) * step


def params():
    return pltpu.CompilerParams(vmem_limit_bytes=VMEM_BYTES)


def cost(flops, moved):
    return pl.CostEstimate(flops=int(flops), bytes_accessed=int(moved), transcendentals=0)


def old_range(tab, n, q):
    return tab[q], tab[q + 1]


def new_range(tab, n, q):
    k = tab[2 * n + 1 + q]
    return tab[n + 1 + jnp.minimum(k, n - 1)], tab[n + 1 + jnp.minimum(k + 1, n - 1)]


def shifted_rows(ref, start, rows):
    base = pl.multiple_of((start // 8) * 8, 8)
    rem = start - base
    x = ref[pl.ds(base, rows + 8), :]
    lanes = x.shape[1]
    y = pltpu.roll(x.reshape(rows // 8 + 1, 8, lanes), (8 - rem) % 8, 1)
    sublane = lax.broadcasted_iota(jnp.int32, (rows // 8, 8, lanes), 1)
    return jnp.where(sublane < 8 - rem, y[:-1], y[1:]).reshape(rows, lanes)


def place_rows(ref, x, start):
    rows, lanes = x.shape
    base = pl.multiple_of((start // 8) * 8, 8)
    rem = start - base
    y = pltpu.roll(x.reshape(rows // 8, 8, lanes), rem, 1)
    before = jnp.concatenate([y[:1], y])
    after = jnp.concatenate([y, y[-1:]])
    sublane = lax.broadcasted_iota(jnp.int32, (rows // 8 + 1, 8, lanes), 1)
    merged = jnp.where(sublane < rem, before, after).reshape(rows + 8, lanes)
    row = lax.broadcasted_iota(jnp.int32, (rows + 8, lanes), 0)
    ref[pl.ds(base, rows + 8), :] = jnp.where(row >= rem, merged, ref[pl.ds(base, rows + 8), :])


def relayout(tab, n, own, left, right, src, dst):
    slot, mv = own.shape[0], left.shape[0]
    q = tab[3 * n + 1]
    old_start, old_end = old_range(tab, n, q)
    new_start, _ = new_range(tab, n, q)
    src[0:mv, :] = left.astype(F32)
    src[mv : mv + slot, :] = own
    start = mv + jnp.clip(new_start - old_start, -mv, slot)
    dst[mv : mv + slot, :] = shifted_rows(src, start, slot)
    place_rows(dst, right.astype(F32), mv + jnp.clip(old_end - new_start, -mv, slot))


def hidden_kernel(n, rows, tab, gate, up, *refs):
    outs, scratch = refs[:-1], refs[-1]
    tokens, width = gate.shape
    for first in range(0, width, 128):
        last = min(first + 128, width)
        g = gate[:, first:last].astype(F32)
        h = g / (1.0 + jnp.exp(-g)) * up[:, first:last].astype(F32)
        scratch[first:last, :] = h.T
    scratch[width:, :] = jnp.zeros((scratch.shape[0] - width, tokens), F32)
    q = tab[3 * n + 1]
    for rel, out in enumerate(outs):
        for other in range(2):
            start, _ = new_range(tab, n, q ^ (2 * rel + other))
            out[other] = shifted_rows(scratch, start, rows).astype(BF16)


def hidden_windows(tab, gate, up, n, rows):
    tokens, width = gate.shape
    shape = jax.ShapeDtypeStruct((2, rows, tokens), BF16)
    return pl.pallas_call(
        functools.partial(hidden_kernel, n, rows),
        out_shape=[shape] * (n // 2),
        in_specs=[SMEM, pl.BlockSpec(memory_space=pltpu.VMEM), pl.BlockSpec(memory_space=pltpu.VMEM)],
        out_specs=[pl.BlockSpec(memory_space=pltpu.VMEM)] * (n // 2),
        scratch_shapes=[pltpu.VMEM((round_up(width, 8) + rows + 8, tokens), F32)],
        compiler_params=params(),
        cost_estimate=cost(0, 25e6),
    )(tab, gate, up)


def edges_kernel(n, mv, count, tab, *refs):
    ins, outs, scratch = refs[:count], refs[count : 3 * count], refs[-1]
    q = tab[3 * n + 1]
    old_start, old_end = old_range(tab, n, q)
    live = old_end - old_start
    slot = ins[0].shape[0]
    base = pl.multiple_of((jnp.clip(live - mv, 0, slot - mv - 8) // 8) * 8, 8)
    for i in range(count):
        outs[2 * i][...] = ins[i][0:mv, :].astype(BF16)
        scratch[mv + 8 : 2 * mv + 16, :] = ins[i][pl.ds(base, mv + 8), :]
        outs[2 * i + 1][...] = shifted_rows(scratch, live + 8 - base, mv).astype(BF16)


def edges(tab, arrays, n, mv):
    slot, width = arrays[0].shape
    block = min(width, 1024)
    count = len(arrays)
    return pl.pallas_call(
        functools.partial(edges_kernel, n, mv, count),
        out_shape=[jax.ShapeDtypeStruct((mv, width), BF16)] * (2 * count),
        grid=(width // block,),
        in_specs=[SMEM] + [pl.BlockSpec((slot, block), lambda i: (0, i))] * count,
        out_specs=[pl.BlockSpec((mv, block), lambda i: (0, i))] * (2 * count),
        scratch_shapes=[pltpu.VMEM((2 * mv + 32, block), F32)],
        compiler_params=params(),
        cost_estimate=cost(0, count * slot * width * 5),
    )(tab, *arrays)


def weights_kernel(n, tab, own, left, right, out, src, dst):
    slot, mv = own.shape[0], left.shape[0]
    relayout(tab, n, own[...], left[...], right[...], src, dst)
    start, end = new_range(tab, n, tab[3 * n + 1])
    row = lax.broadcasted_iota(jnp.int32, own.shape, 0)
    kept = jnp.where(row < end - start, dst[mv : mv + slot, :], 0.0).astype(BF16)
    if out.shape[0] > slot:
        kept = jnp.concatenate([kept, jnp.zeros((out.shape[0] - slot, kept.shape[1]), BF16)])
    out[...] = kept


def new_weights(tab, own, left, right, n, rows):
    slot, width = own.shape
    mv = left.shape[0]
    block = min(width, 512)
    return pl.pallas_call(
        functools.partial(weights_kernel, n),
        out_shape=jax.ShapeDtypeStruct((rows, width), BF16),
        grid=(width // block,),
        in_specs=[SMEM, pl.BlockSpec((slot, block), lambda i: (0, i))]
        + [pl.BlockSpec((mv, block), lambda i: (0, i))] * 2,
        out_specs=pl.BlockSpec((rows, block), lambda i: (0, i)),
        scratch_shapes=[
            pltpu.VMEM((2 * slot + mv + 8, block), F32),
            pltpu.VMEM((slot + 2 * mv + 8, block), F32),
        ],
        compiler_params=params(),
        cost_estimate=cost(0, slot * width * 8),
    )(tab, own, left, right)


def forward_kernel(sent, tab, *refs):
    pieces, (mine, other, send, keep, hid) = refs[:-5], refs[-5:]
    rows, tokens = pieces[0].shape[1:]

    @pl.when(pl.program_id(0) == 0)
    def _():
        for i, piece in enumerate(pieces):
            for e in range(2):
                hid[i * tokens : (i + 1) * tokens, e * rows : (e + 1) * rows] = (
                    piece[e].astype(F32).T.astype(BF16)
                )

    for i in range(len(pieces)):
        block = hid[i * tokens : (i + 1) * tokens, :]
        part = jnp.dot(block[:, :rows], mine[...], preferred_element_type=F32)
        part = part + jnp.dot(block[:, rows:], other[...], preferred_element_type=F32)
        if i < sent:
            send[i, 0] = part.astype(BF16)
        else:
            keep[i - sent, 0] = part.astype(BF16)


def forward_half(tab, pieces, mine, other, sent, n, n_dp, half):
    rows, tokens = pieces[0].shape[1:]
    width = mine.shape[1]
    block = width // (2 * n_dp)
    count = len(pieces)

    def columns(s, tab):
        return 0, lax.rem(tab[3 * n + 2] + s, n_dp) * 2 + half

    def whole(s, tab):
        return 0, 0, 0

    def out_block(s, tab):
        return 0, s, 0, 0

    return pl.pallas_call(
        functools.partial(forward_kernel, sent),
        out_shape=[
            jax.ShapeDtypeStruct((sent, n_dp, tokens, block), BF16),
            jax.ShapeDtypeStruct((count - sent, n_dp, tokens, block), BF16),
        ],
        grid_spec=pltpu.PrefetchScalarGridSpec(
            num_scalar_prefetch=1,
            grid=(n_dp,),
            in_specs=[pl.BlockSpec((2, rows, tokens), whole)] * count
            + [pl.BlockSpec((rows, block), columns)] * 2,
            out_specs=[
                pl.BlockSpec((sent, 1, tokens, block), out_block),
                pl.BlockSpec((count - sent, 1, tokens, block), out_block),
            ],
            scratch_shapes=[pltpu.VMEM((count * tokens, 2 * rows), BF16)],
        ),
        compiler_params=params(),
        cost_estimate=cost(2 * count * tokens * 2 * rows * width // 2, 15e6),
    )(tab, *pieces, mine, other)


def adam_kernel(n, pieces, grads, scale, tab, *refs):
    ht_refs, refs = refs[: pieces + 1], refs[pieces + 1 :]
    og_refs, refs = refs[:grads], refs[grads:]
    own, left, right, outs = refs[0:3], refs[3:6], refs[6:9], refs[9:12]
    src, ht, og, moved = refs[12], refs[13], refs[14], refs[15:18]
    slot, mv = own[0].shape[0], left[0].shape[0]
    tokens = ht_refs[0].shape[2]

    @pl.when(pl.program_id(0) == 0)
    def _():
        for i in range(pieces):
            ht[:, i * tokens : (i + 1) * tokens] = ht_refs[i][0]
            ht[:, (pieces + i) * tokens : (pieces + i + 1) * tokens] = ht_refs[pieces][i]

    first = 0
    for ref in og_refs:
        og[first : first + ref.shape[0], :] = ref[...]
        first += ref.shape[0]
    for i in range(3):
        relayout(tab, n, own[i][...], left[i][...], right[i][...], src, moved[i])
    start, end = new_range(tab, n, tab[3 * n + 1])
    step = slot // 2 if slot % 16 == 0 else slot
    for base in range(0, slot, step):
        grad = jnp.dot(ht[base : base + step, :], og[...], preferred_element_type=F32) * scale
        rows = slice(mv + base, mv + base + step)
        master, first_old, second_old = (ref[rows, :] for ref in moved)
        first_next = 0.9 * first_old + 0.1 * grad
        second_next = 0.95 * second_old + 0.05 * grad * grad
        master_next = master - 0.001 * (first_next / (jnp.sqrt(second_next) + 1e-08) + 0.1 * master)
        live = lax.broadcasted_iota(jnp.int32, grad.shape, 0) + base < end - start
        for out, value in zip(outs, (master_next, first_next, second_next)):
            out[base : base + step, :] = jnp.where(live, value, 0.0)


def adam(tab, pieces, partner, grads, own, left, right, n, scale):
    rows, tokens = pieces[0].shape[1:]
    slot, width = own[0].shape
    mv = left[0].shape[0]
    block = min(width, 512)
    total = sum(g.shape[0] for g in grads)
    count = len(pieces)

    def column(i):
        return 0, i

    return pl.pallas_call(
        functools.partial(adam_kernel, n, count, len(grads), scale),
        out_shape=[jax.ShapeDtypeStruct((slot, width), F32)] * 3,
        grid=(width // block,),
        in_specs=[SMEM]
        + [pl.BlockSpec((1, rows, tokens), lambda i: (0, 0, 0))] * count
        + [pl.BlockSpec((count, rows, tokens), lambda i: (0, 0, 0))]
        + [pl.BlockSpec((g.shape[0], block), column) for g in grads]
        + [pl.BlockSpec((slot, block), column)] * 3
        + [pl.BlockSpec((mv, block), column)] * 6,
        out_specs=[pl.BlockSpec((slot, block), column)] * 3,
        scratch_shapes=[
            pltpu.VMEM((2 * slot + mv + 8, block), F32),
            pltpu.VMEM((rows, total), BF16),
            pltpu.VMEM((total, block), BF16),
        ]
        + [pltpu.VMEM((slot + 2 * mv + 8, block), F32)] * 3,
        compiler_params=params(),
        cost_estimate=cost(2 * total * slot * width, 95e6),
    )(tab, *pieces, partner, *grads, *own, *left, *right)


def swap(value, mask):
    n = lax.axis_size("fsdp")
    return lax.ppermute(value, "fsdp", [(i, i ^ mask) for i in range(n)])


def along(value, steps):
    n = lax.axis_size("fsdp")
    return lax.ppermute(value, "fsdp", [(i, i + steps) for i in range(n) if 0 <= i + steps < n])


def turn(value, steps):
    n = lax.axis_size("dp")
    return lax.ppermute(value, "dp", [(i, (i + steps) % n) for i in range(n)])


def gathered(value, groups):
    if groups != 4:
        return [value] + [swap(value, 2 * rel) for rel in range(1, groups)]
    half = value.shape[0] // 2
    x, y = swap(value, 2), swap(value, 4)
    return [value, x, y, swap(y[:half], 2), swap(x[half:], 4)]


def local(gate, up, out_grad, master_old, moment1_old, moment2_old, old_bounds, new_bounds, rank_map):
    n, n_dp = lax.axis_size("fsdp"), lax.axis_size("dp")
    groups = n // 2
    tokens, block_rows = gate.shape
    slot, width = master_old.shape[1:]
    rows = round_up(slot, 16)
    mv = round_up((block_rows // n + 1) // 2, 16)
    scale = 1.0 / math.sqrt(tokens * n)
    index = jnp.stack([lax.axis_index("fsdp"), lax.axis_index("dp")]).astype(jnp.int32)
    tab = jnp.concatenate([old_bounds[0], new_bounds[0], rank_map[0], index])
    own = [master_old[0], moment1_old[0], moment2_old[0]]

    first, last = edges(tab, own[:1], n, mv)
    master_right, master_left = along(first, -1), along(last, 1)
    windows = hidden_windows(tab, gate, up, n, rows)
    pieces = [windows[0]] + [swap(windows[rel], 2 * rel) for rel in range(1, groups)]
    first1, last1, first2, last2 = edges(tab, own[1:], n, mv)
    right = [master_right, along(first1, -1), along(first2, -1)]
    left = [master_left, along(last1, 1), along(last2, 1)]

    mine = new_weights(tab, own[0], left[0], right[0], n, rows)
    other = swap(mine, 1)
    halves = []
    for half in range(2):
        if groups == 4:
            near, far = (1, 2) if half == 0 else (2, 1)
            order = [pieces[near], pieces[3], pieces[0], pieces[far]]
            send, keep = forward_half(tab, order, mine, other, 2, n, n_dp, half)
            came = swap(send, 2 * near)
            passed = (keep[1].astype(F32) + came[1].astype(F32)).astype(BF16)
            total = keep[0].astype(F32) + came[0].astype(F32) + swap(passed, 2 * far).astype(F32)
        else:
            order = pieces[1:] + pieces[:1]
            send, keep = forward_half(tab, order, mine, other, groups - 1, n, n_dp, half)
            total = keep[0].astype(F32)
            for rel in range(1, groups):
                total = total + swap(send[rel - 1], 2 * rel).astype(F32)
        low = total.astype(BF16)
        out = total[0]
        for steps in range(1, n_dp):
            out = out + turn(low[steps], steps).astype(F32)
        halves.append(out)
    mlp_out = jnp.concatenate(halves, axis=1)

    grads = gathered(out_grad, groups)
    grads = grads + [swap(g, 1) for g in grads]
    partner = swap(jnp.stack([piece[1] for piece in pieces]), 1)
    master, first_next, second_next = adam(tab, pieces, partner, grads, own, left, right, n, scale)
    return mlp_out, master[None], first_next[None], second_next[None]


def solution(mesh):
    placed = (
        P("fsdp", "dp"),
        P("fsdp", "dp"),
        P("fsdp", None),
        P("dp", "fsdp", None),
        P("dp", "fsdp", None),
        P("dp", "fsdp", None),
        P("dp", None),
        P("dp", None),
        P("dp", None),
    )
    return jax.shard_map(
        local,
        mesh=mesh,
        in_specs=placed,
        out_specs=(
            P("fsdp", "dp"),
            P("dp", "fsdp", None),
            P("dp", "fsdp", None),
            P("dp", "fsdp", None),
        ),
        check_vma=False,
    )
```

time: 665 us -> 399 us (0.60)
  local copies, waits for them, and re-layouts: 167 us -> 6.2 us
  other arithmetic: 164 us -> 8.33 us
  Pallas kernels: 0 us -> 94.8 us
  matrix products: 82 us -> 0 us
  starting transfers between devices: 6.19 us -> 47.2 us
  waiting for transfers between devices: 210 us -> 239 us
  between operations: 17.6 us -> 0.99 us
  loops' own time: 15.6 us -> 0 us
    pallas_call x0 -> x7, Pallas kernels: none -> 94.8 us  [the longest x1 37.8 us: adam(): pl.pallas_call(functools.partial(adam_kernel, n, count, len(grads), scale...]
    dot_general x9 -> x0, matrix products: 82 us -> none  [the longest x8 62.7 us: one_shard(): return carry + jnp.dot(columns, block, preferred_element_type=jnp.float32)]
    concatenate x2 -> x1, local copies, waits for them, and re-layouts: 69.5 us -> 1.29 us  [local(): tab = jnp.concatenate([old_bounds[0], new_bounds[0], rank_map[0], index])]
    gather x2 -> x0, local copies, waits for them, and re-layouts: 55.3 us -> none  [the longest x1 40.5 us: migrate(): chosen = jnp.take(source, index, axis=1)]
    ppermute x2 -> x30, starting transfers between devices: 6.07 us -> 47.2 us  [the longest x18 22.1 us: swap(): return lax.ppermute(value, 'fsdp', [(i, i ^ mask) for i in range(n)])]
    concatenate x3 -> x1, other arithmetic: 39.7 us -> 1.06 us  [local(): mlp_out = jnp.concatenate(halves, axis=1)]
    select_n x4 -> x0, other arithmetic: 34.3 us -> none  [the longest x1 32.8 us: migrate(): jnp.where((row_index < my_new_count)[None, :, None], chosen, jnp.zeros_li...]
    ppermute x2 -> x30, waiting for transfers between devices: 210 us -> 239 us  [the longest x6 130 us: along(): lax.ppermute(value, 'fsdp', [(i, i + steps) for i in range(n) if 0 <= i +...]
  transfers between devices with their start and end apart: 5 -> 30, of which waited for: 1 -> 14; matrix products, arithmetic and copies ran while one was open for 60% -> 2% of each run, Pallas kernels for 0% -> 20%
where the time goes in v1:
time: 399 us; the launch traced here: 396 us
  waiting for transfers between devices  239 us (60%)
  Pallas kernels  94.8 us (24%)
  starting transfers between devices  47.2 us (12%)
  other arithmetic  8.33 us (2%)
  local copies, waits for them, and re-layouts  6.2 us (2%)
    ppermute x6, waiting for transfers between devices, along(): lax.ppermute(value, 'fsdp', [(i, i + steps) for i in range(n) if 0 <= i +...  130 us
    ppermute x18, waiting for transfers between devices, swap(): return lax.ppermute(value, 'fsdp', [(i, i ^ mask) for i in range(n)])  70 us
    ppermute x6, waiting for transfers between devices, turn(): return lax.ppermute(value, 'dp', [(i, (i + steps) % n) for i in range(n)])  38.7 us
    pallas_call x1, Pallas kernels, adam(): pl.pallas_call(functools.partial(adam_kernel, n, count, len(grads), scale...  37.8 us
    pallas_call x2, Pallas kernels, forward_half(): pl.pallas_call(functools.partial(forward_kernel, sent), out_shape=[jax.Sh...  24.9 us
    ppermute x18, starting transfers between devices, swap(): return lax.ppermute(value, 'fsdp', [(i, i ^ mask) for i in range(n)])  22.1 us
    ppermute x6, starting transfers between devices, along(): lax.ppermute(value, 'fsdp', [(i, i + steps) for i in range(n) if 0 <= i +...  17.6 us
    pallas_call x2, Pallas kernels, edges(): pl.pallas_call(functools.partial(edges_kernel, n, mv, count), out_shape=[...  16.7 us
  transfers between devices with their start and end apart: 30, of which 14 were waited for; matrix products, arithmetic and copies ran while one was open for 2% of the time, Pallas kernels for 20%

profile of v1, /device:TPU:11, one launch (start us, length us, event | category | flops | bytes accessed | tf_op | source)
XLA Modules:
  0.0 396.5 jit_solution(9910305986206092517)
XLA Ops:
  1.9 6.1 %shard_map.121 = (bf16[240,4096]{1,0:T(8,128)(2,1)}, bf16[240,4096]{1,0:T(8,128)(2,1)}) custom-call(s32[27]{0:T(128)} %concatenate.6.tab, f32[624,4096]{1,0:T(8,128)} %bitcast.49), custom_call_target="tpu_custom_call" | custom-call | bytes 12779520 | tf_op jit(solution)/shard_map/pallas_call | solution.py:120
  8.1 3.7 collective-permute-start.3
  11.7 1.9 collective-permute-start.4
  13.7 38.2 %collective-permute-done.3.left.refs_18_ = bf16[240,4096]{1,0:T(8,128)(2,1)S(1)} collective-permute-done((bf16[240,4096]{1,0:T(8,128)(2,1)}, bf16[240,4096]{1,0:T(8,128)(2,1)S(1)}, u32[]{:S(2)}, u32[]{:S(2)}) %collective-permute-start.3) | collective-permute-done | bytes 1966112 | tf_op jit(solution)/shard_map/ppermute | solution.py:296
  51.9 4.4 %collective-permute-done.4.right.refs_21_ = bf16[240,4096]{1,0:T(8,128)(2,1)S(1)} collective-permute-done((bf16[240,4096]{1,0:T(8,128)(2,1)}, bf16[240,4096]{1,0:T(8,128)(2,1)S(1)}, u32[]{:S(2)}, u32[]{:S(2)}) %collective-permute-start.4) | collective-permute-done | bytes 1966112 | tf_op jit(solution)/shard_map/ppermute | solution.py:296
  57.5 10.5 %shard_map.122.refs_4_ = bf16[624,4096]{1,0:T(8,128)(2,1)} custom-call(s32[27]{0:T(128)} %concatenate.6.tab, f32[624,4096]{1,0:T(8,128)} %bitcast.50, bf16[240,4096]{1,0:T(8,128)(2,1)} %copy-done, bf16[240,4096]{1,0:T(8,128)(2,1)} %copy-done.1), custom_call_target="tpu_custom_call" | custom-call | bytes 20447232 | tf_op jit(solution)/shard_map/pallas_call | solution.py:147
  68.0 4.9 %shard_map.120 = (bf16[2,624,256]{2,1,0:T(8,128)(2,1)}, bf16[2,624,256]{2,1,0:T(8,128)(2,1)}, bf16[2,624,256]{2,1,0:T(8,128)(2,1)}, bf16[2,624,256]{2,1,0:T(8,128)(2,1)}) custom-call(s32[27]{0:T(128)} %concatenate.6.tab, bf16[256,3712]{1,0:T(8,128)(2,1)} %gate.1, bf16[256,3712]{1,0:T(8,128)(2,1)} %up.1), custom_call_target="tpu_custom_call" | custom-call | bytes 25000000 | tf_op jit(solution)/shard_map/pallas_call | solution.py:92
  73.5 2.0 collective-permute-start.1
  75.5 10.6 %shard_map.125 = (bf16[240,4096]{1,0:T(8,128)(2,1)}, bf16[240,4096]{1,0:T(8,128)(2,1)}, bf16[240,4096]{1,0:T(8,128)(2,1)}, bf16[240,4096]{1,0:T(8,128)(2,1)}) custom-call(s32[27]{0:T(128)} %concatenate.6.tab, f32[624,4096]{1,0:T(8,128)} %bitcast.52, f32[624,4096]{1,0:T(8,128)} %bitcast.54), custom_call_target="tpu_custom_call" | custom-call | bytes 25559040 | tf_op jit(solution)/shard_map/pallas_call | solution.py:120
  86.1 3.0 collective-permute-start.26
  89.3 12.7 %collective-permute-done.1.refs_1_.refs_3_ = bf16[2,624,256]{2,1,0:T(8,128)(2,1)S(1)} collective-permute-done((bf16[2,624,256]{2,1,0:T(8,128)(2,1)}, bf16[2,624,256]{2,1,0:T(8,128)(2,1)S(1)}, u32[]{:S(2)}, u32[]{:S(2)}) %collective-permute-start.1) | collective-permute-done | bytes 639008 | tf_op jit(solution)/shard_map/ppermute | solution.py:291
  102.2 2.0 collective-permute-start.16
  104.2 4.2 %collective-permute-start.27 = (bf16[240,4096]{1,0:T(8,128)(2,1)S(1)}, bf16[240,4096]{1,0:T(8,128)(2,1)}, u32[]{:S(2)}, u32[]{:S(2)}) collective-permute-start(bf16[240,4096]{1,0:T(8,128)(2,1)S(1)} %copy-done.20), channel_id=1, source_target_pairs={{0,1},{1,2},{2,3},{3,4},{4,5},{5,6},{6,7},{8,9},{9,10},{10,11},{11... | collective-permute-start | bytes 5898248 | tf_op jit(solution)/shard_map/ppermute | solution.py:296
  108.5 2.3 collective-permute-start.28
  110.8 20.9 %collective-permute-done.26.refs_19_ = bf16[240,4096]{1,0:T(8,128)(2,1)S(1)} collective-permute-done((bf16[240,4096]{1,0:T(8,128)(2,1)}, bf16[240,4096]{1,0:T(8,128)(2,1)S(1)}, u32[]{:S(2)}, u32[]{:S(2)}) %collective-permute-start.26) | collective-permute-done | bytes 1966112 | tf_op jit(solution)/shard_map/ppermute | solution.py:296
  131.7 42.0 %collective-permute-done.27.refs_20_ = bf16[240,4096]{1,0:T(8,128)(2,1)} collective-permute-done((bf16[240,4096]{1,0:T(8,128)(2,1)S(1)}, bf16[240,4096]{1,0:T(8,128)(2,1)}, u32[]{:S(2)}, u32[]{:S(2)}) %collective-permute-start.27) | collective-permute-done | bytes 1966112 | tf_op jit(solution)/shard_map/ppermute | solution.py:296
  173.7 2.6 collective-permute-start.29
  176.3 12.4 %shard_map.123 = (bf16[2,4,256,512]{3,2,1,0:T(8,128)(2,1)}, bf16[2,4,256,512]{3,2,1,0:T(8,128)(2,1)}) custom-call(s32[27]{0:T(128)} %concatenate.6.tab, bf16[2,624,256]{2,1,0:T(8,128)(2,1)} %copy-done.12, bf16[2,624,256]{2,1,0:T(8,128)(2,1)} %copy-done.14, bf16[2,624,256]{2,1,0:T(8,128)(2,1)} %get-tuple-element.23.refs_2_.refs_0_, ...), custom_call_target="tpu_custom_call" | custom-call | flops 5234491392 | bytes 15000000 | tf_op jit(solution)/shard_map/pallas_call | solution.py:200
  191.4 12.4 %shard_map.124 = (bf16[2,4,256,512]{3,2,1,0:T(8,128)(2,1)}, bf16[2,4,256,512]{3,2,1,0:T(8,128)(2,1)}) custom-call(s32[27]{0:T(128)} %concatenate.6.tab, bf16[2,624,256]{2,1,0:T(8,128)(2,1)} %copy-done.13, bf16[2,624,256]{2,1,0:T(8,128)(2,1)} %copy-done.14, bf16[2,624,256]{2,1,0:T(8,128)(2,1)} %get-tuple-element.23.refs_2_.refs_0_, ...), custom_call_target="tpu_custom_call" | custom-call | flops 5234491392 | bytes 15000000 | tf_op jit(solution)/shard_map/pallas_call | solution.py:200
  203.8 15.0 %collective-permute-done.17.refs_6_ = bf16[256,4096]{1,0:T(8,128)(2,1)S(1)} collective-permute-done((bf16[256,4096]{1,0:T(8,128)(2,1)}, bf16[256,4096]{1,0:T(8,128)(2,1)S(1)}, u32[]{:S(2)}, u32[]{:S(2)}) %collective-permute-start.17) | collective-permute-done | bytes 2097184 | tf_op jit(solution)/shard_map/ppermute | solution.py:291
  219.0 24.8 %collective-permute-done.29.refs_23_ = bf16[240,4096]{1,0:T(8,128)(2,1)} collective-permute-done((bf16[240,4096]{1,0:T(8,128)(2,1)}, bf16[240,4096]{1,0:T(8,128)(2,1)}, u32[]{:S(2)}, u32[]{:S(2)}) %collective-permute-start.29) | collective-permute-done | bytes 1966112 | tf_op jit(solution)/shard_map/ppermute | solution.py:296
  243.8 42.3 %collective-permute-done.19.refs_8_ = bf16[128,4096]{1,0:T(8,128)(2,1)S(1)} collective-permute-done((bf16[128,4096]{1,0:T(8,128)(2,1)}, bf16[128,4096]{1,0:T(8,128)(2,1)S(1)}, u32[]{:S(2)}, u32[]{:S(2)}) %collective-permute-start.19) | collective-permute-done | bytes 1048608 | tf_op jit(solution)/shard_map/ppermute | solution.py:291
  286.2 12.2 %collective-permute-start.23 = (bf16[256,4096]{1,0:T(8,128)(2,1)S(1)}, bf16[256,4096]{1,0:T(8,128)(2,1)}, u32[]{:S(2)}, u32[]{:S(2)}) collective-permute-start(bf16[256,4096]{1,0:T(8,128)(2,1)S(1)} %collective-permute-done.18.refs_7_), channel_id=1, source_target_pairs={{0,1},{1,0},{2,3},{3,2},{4,5},{5,4},{6,7},{7,6},{8,9},{9,8},{10,11... | collective-permute-start | bytes 6291464 | tf_op jit(solution)/shard_map/ppermute | solution.py:291
  298.9 2.5 fusion
  303.9 1.8 collective-permute-start.12
  307.9 37.8 %shard_map.126 = (f32[624,4096]{1,0:T(8,128)}, f32[624,4096]{1,0:T(8,128)}, f32[624,4096]{1,0:T(8,128)}) custom-call(s32[27]{0:T(128)} %concatenate.6.tab, bf16[2,624,256]{2,1,0:T(8,128)(2,1)} %get-tuple-element.23.refs_2_.refs_0_, bf16[2,624,256]{2,1,0:T(8,128)(2,1)} %copy-done.12, bf16[2,624,256]{2,1,0:T(8,128)(2,1)} %copy-done.13, ...), custom_call_target="tpu_custom_call" | custom-call | flops 10468982784 | bytes 95000000 | tf_op jit(solution)/shard_map/pallas_call | solution.py:267
  345.8 2.5 fusion.8
  349.9 4.1 %collective-permute-start.9 = (bf16[256,512]{1,0:T(8,128)(2,1)S(1)}, bf16[256,512]{1,0:T(8,128)(2,1)S(1)}, u32[]{:S(2)}, u32[]{:S(2)}) collective-permute-start(bf16[256,512]{1,0:T(8,128)(2,1)S(1)} %get-tuple-element.44), channel_id=1, source_target_pairs={{0,16},{8,24},{16,0},{24,8},{1,17},{9,25},{17,1},{25,9},{2,18},{10... | collective-permute-start | bytes 786440 | tf_op jit(solution)/shard_map/ppermute | solution.py:301
  357.3 6.4 %collective-permute-done.8 = bf16[256,512]{1,0:T(8,128)(2,1)S(1)} collective-permute-done((bf16[256,512]{1,0:T(8,128)(2,1)S(1)}, bf16[256,512]{1,0:T(8,128)(2,1)S(1)}, u32[]{:S(2)}, u32[]{:S(2)}) %collective-permute-start.8) | collective-permute-done | bytes 262176 | tf_op jit(solution)/shard_map/ppermute | solution.py:301
  363.6 8.1 %collective-permute-done.9 = bf16[256,512]{1,0:T(8,128)(2,1)S(1)} collective-permute-done((bf16[256,512]{1,0:T(8,128)(2,1)S(1)}, bf16[256,512]{1,0:T(8,128)(2,1)S(1)}, u32[]{:S(2)}, u32[]{:S(2)}) %collective-permute-start.9) | collective-permute-done | bytes 262176 | tf_op jit(solution)/shard_map/ppermute | solution.py:301
  371.9 16.7 %collective-permute-done.13 = bf16[256,512]{1,0:T(8,128)(2,1)S(1)} collective-permute-done((bf16[256,512]{1,0:T(8,128)(2,1)S(1)}, bf16[256,512]{1,0:T(8,128)(2,1)S(1)}, u32[]{:S(2)}, u32[]{:S(2)}) %collective-permute-start.13) | collective-permute-done | bytes 262176 | tf_op jit(solution)/shard_map/ppermute | solution.py:301
  388.6 5.6 %collective-permute-done.14 = bf16[256,512]{1,0:T(8,128)(2,1)S(1)} collective-permute-done((bf16[256,512]{1,0:T(8,128)(2,1)S(1)}, bf16[256,512]{1,0:T(8,128)(2,1)S(1)}, u32[]{:S(2)}, u32[]{:S(2)}) %collective-permute-start.14) | collective-permute-done | bytes 262176 | tf_op jit(solution)/shard_map/ppermute | solution.py:301
  (94 shorter events, 18.8 us)
Async XLA Ops:
  8.1 43.8 %collective-permute-start.3 = (bf16[240,4096]{1,0:T(8,128)(2,1)}, bf16[240,4096]{1,0:T(8,128)(2,1)S(1)}, u32[]{:S(2)}, u32[]{:S(2)}) collective-permute-start(bf16[240,4096]{1,0:T(8,128)(2,1)} %get-tuple-element.25), channel_id=1, source_target_pairs={{0,1},{1,2},{2,3},{3,4},{4,5},{5,6},{6,7},{8,9},{9,10},{10,11},{11... | collective-permute-start | bytes 5898248 | tf_op jit(solution)/shard_map/ppermute | solution.py:296
  11.7 44.5 %collective-permute-start.4 = (bf16[240,4096]{1,0:T(8,128)(2,1)}, bf16[240,4096]{1,0:T(8,128)(2,1)S(1)}, u32[]{:S(2)}, u32[]{:S(2)}) collective-permute-start(bf16[240,4096]{1,0:T(8,128)(2,1)} %get-tuple-element.26), channel_id=1, source_target_pairs={{1,0},{2,1},{3,2},{4,3},{5,4},{6,5},{7,6},{9,8},{10,9},{11,10},{12... | collective-permute-start | bytes 5898248 | tf_op jit(solution)/shard_map/ppermute | solution.py:296
  68.0 105.7 %collective-permute-start.5 = (bf16[624,4096]{1,0:T(8,128)(2,1)}, bf16[624,4096]{1,0:T(8,128)(2,1)}, u32[]{:S(2)}, u32[]{:S(2)}) collective-permute-start(bf16[624,4096]{1,0:T(8,128)(2,1)} %shard_map.122.refs_4_), channel_id=1, source_target_pairs={{0,1},{1,0},{2,3},{3,2},{4,5},{5,4},{6,7},{7,6},{8,9},{9,8},{10,11... | collective-permute-start | bytes 15335432 | tf_op jit(solution)/shard_map/ppermute | solution.py:291
  72.9 16.3 %collective-permute-start = (bf16[2,624,256]{2,1,0:T(8,128)(2,1)}, bf16[2,624,256]{2,1,0:T(8,128)(2,1)S(1)}, u32[]{:S(2)}, u32[]{:S(2)}) collective-permute-start(bf16[2,624,256]{2,1,0:T(8,128)(2,1)} %get-tuple-element.21), channel_id=1, source_target_pairs={{0,2},{1,3},{2,0},{3,1},{4,6},{5,7},{6,4},{7,5},{8,10},{9,11},{10,... | collective-permute-start | bytes 1916936 | tf_op jit(solution)/shard_map/ppermute | solution.py:291
  73.1 16.1 %collective-permute-start.2 = (bf16[2,624,256]{2,1,0:T(8,128)(2,1)}, bf16[2,624,256]{2,1,0:T(8,128)(2,1)S(1)}, u32[]{:S(2)}, u32[]{:S(2)}) collective-permute-start(bf16[2,624,256]{2,1,0:T(8,128)(2,1)} %get-tuple-element.24), channel_id=1, source_target_pairs={{0,4},{1,5},{2,6},{3,7},{4,0},{5,1},{6,2},{7,3},{8,12},{9,13},{10,... | collective-permute-start | bytes 1916936 | tf_op jit(solution)/shard_map/ppermute | solution.py:291
  73.5 28.4 %collective-permute-start.1 = (bf16[2,624,256]{2,1,0:T(8,128)(2,1)}, bf16[2,624,256]{2,1,0:T(8,128)(2,1)S(1)}, u32[]{:S(2)}, u32[]{:S(2)}) collective-permute-start(bf16[2,624,256]{2,1,0:T(8,128)(2,1)} %get-tuple-element.22), channel_id=1, source_target_pairs={{0,6},{1,7},{2,4},{3,5},{4,2},{5,3},{6,0},{7,1},{8,14},{9,15},{10,... | collective-permute-start | bytes 1916936 | tf_op jit(solution)/shard_map/ppermute | solution.py:291
  86.1 45.6 %collective-permute-start.26 = (bf16[240,4096]{1,0:T(8,128)(2,1)}, bf16[240,4096]{1,0:T(8,128)(2,1)S(1)}, u32[]{:S(2)}, u32[]{:S(2)}) collective-permute-start(bf16[240,4096]{1,0:T(8,128)(2,1)} %get-tuple-element.31), channel_id=1, source_target_pairs={{0,1},{1,2},{2,3},{3,4},{4,5},{5,6},{6,7},{8,9},{9,10},{10,11},{11... | collective-permute-start | bytes 5898248 | tf_op jit(solution)/shard_map/ppermute | solution.py:296
  102.2 6.3 %collective-permute-start.16 = (bf16[4,624,256]{2,1,0:T(8,128)(2,1)S(1)}, bf16[4,624,256]{2,1,0:T(8,128)(2,1)S(1)}, u32[]{:S(2)}, u32[]{:S(2)}) collective-permute-start(bf16[4,624,256]{2,1,0:T(8,128)(2,1)S(1)} %pad_maximum_fusion), channel_id=1, source_target_pairs={{0,1},{1,0},{2,3},{3,2},{4,5},{5,4},{6,7},{7,6},{8,9},{9,8},{10,11... | collective-permute-start | bytes 3833864 | tf_op jit(solution)/shard_map/ppermute | solution.py:291
  104.2 69.5 %collective-permute-start.27 = (bf16[240,4096]{1,0:T(8,128)(2,1)S(1)}, bf16[240,4096]{1,0:T(8,128)(2,1)}, u32[]{:S(2)}, u32[]{:S(2)}) collective-permute-start(bf16[240,4096]{1,0:T(8,128)(2,1)S(1)} %copy-done.20), channel_id=1, source_target_pairs={{0,1},{1,2},{2,3},{3,4},{4,5},{5,6},{6,7},{8,9},{9,10},{10,11},{11... | collective-permute-start | bytes 5898248 | tf_op jit(solution)/shard_map/ppermute | solution.py:296
  108.4 80.4 %collective-permute-start.18 = (bf16[256,4096]{1,0:T(8,128)(2,1)}, bf16[256,4096]{1,0:T(8,128)(2,1)S(1)}, u32[]{:S(2)}, u32[]{:S(2)}) collective-permute-start(bf16[256,4096]{1,0:T(8,128)(2,1)} %refs_5_.1), channel_id=1, source_target_pairs={{0,4},{1,5},{2,6},{3,7},{4,0},{5,1},{6,2},{7,3},{8,12},{9,13},{10,... | collective-permute-start | bytes 6291464 | tf_op jit(solution)/shard_map/ppermute | solution.py:291
  108.5 82.3 %collective-permute-start.28 = (bf16[240,4096]{1,0:T(8,128)(2,1)}, bf16[240,4096]{1,0:T(8,128)(2,1)}, u32[]{:S(2)}, u32[]{:S(2)}) collective-permute-start(bf16[240,4096]{1,0:T(8,128)(2,1)} %get-tuple-element.33), channel_id=1, source_target_pairs={{1,0},{2,1},{3,2},{4,3},{5,4},{6,5},{7,6},{9,8},{10,9},{11,10},{12... | collective-permute-start | bytes 5898248 | tf_op jit(solution)/shard_map/ppermute | solution.py:296
  131.7 87.1 %collective-permute-start.17 = (bf16[256,4096]{1,0:T(8,128)(2,1)}, bf16[256,4096]{1,0:T(8,128)(2,1)S(1)}, u32[]{:S(2)}, u32[]{:S(2)}) collective-permute-start(bf16[256,4096]{1,0:T(8,128)(2,1)} %refs_5_.1), channel_id=1, source_target_pairs={{0,2},{1,3},{2,0},{3,1},{4,6},{5,7},{6,4},{7,5},{8,10},{9,11},{10,... | collective-permute-start | bytes 6291464 | tf_op jit(solution)/shard_map/ppermute | solution.py:291
  173.7 70.1 %collective-permute-start.21 = (bf16[256,4096]{1,0:T(8,128)(2,1)}, bf16[256,4096]{1,0:T(8,128)(2,1)}, u32[]{:S(2)}, u32[]{:S(2)}) collective-permute-start(bf16[256,4096]{1,0:T(8,128)(2,1)} %refs_5_.1), channel_id=1, source_target_pairs={{0,1},{1,0},{2,3},{3,2},{4,5},{5,4},{6,7},{7,6},{8,9},{9,8},{10,11... | collective-permute-start | bytes 6291464 | tf_op jit(solution)/shard_map/ppermute | solution.py:291
  173.7 70.1 %collective-permute-start.29 = (bf16[240,4096]{1,0:T(8,128)(2,1)}, bf16[240,4096]{1,0:T(8,128)(2,1)}, u32[]{:S(2)}, u32[]{:S(2)}) collective-permute-start(bf16[240,4096]{1,0:T(8,128)(2,1)} %get-tuple-element.34), channel_id=1, source_target_pairs={{1,0},{2,1},{3,2},{4,3},{5,4},{6,5},{7,6},{9,8},{10,9},{11,10},{12... | collective-permute-start | bytes 5898248 | tf_op jit(solution)/shard_map/ppermute | solution.py:296
  188.8 97.4 %copy-start.2 = (bf16[256,4096]{1,0:T(8,128)(2,1)}, bf16[256,4096]{1,0:T(8,128)(2,1)S(1)}, u32[]{:S(2)}) copy-start(bf16[256,4096]{1,0:T(8,128)(2,1)S(1)} %collective-permute-done.18.refs_7_) | copy-start | bytes 6291460
  188.8 109.7 %collective-permute-start.6 = (bf16[2,4,256,512]{3,2,1,0:T(8,128)(2,1)}, bf16[2,4,256,512]{3,2,1,0:T(8,128)(2,1)}, u32[]{:S(2)}, u32[]{:S(2)}) collective-permute-start(bf16[2,4,256,512]{3,2,1,0:T(8,128)(2,1)} %get-tuple-element.28), channel_id=1, source_target_pairs={{0,2},{1,3},{2,0},{3,1},{4,6},{5,7},{6,4},{7,5},{8,10},{9,11},{10,... | collective-permute-start | bytes 6291464 | tf_op jit(solution)/shard_map/ppermute | solution.py:291
  190.8 95.4 %collective-permute-start.19 = (bf16[128,4096]{1,0:T(8,128)(2,1)}, bf16[128,4096]{1,0:T(8,128)(2,1)S(1)}, u32[]{:S(2)}, u32[]{:S(2)}) collective-permute-start(bf16[128,4096]{1,0:T(8,128)(2,1)} %slice.103), channel_id=1, source_target_pairs={{0,2},{1,3},{2,0},{3,1},{4,6},{5,7},{6,4},{7,5},{8,10},{9,11},{10,... | collective-permute-start | bytes 3145736 | tf_op jit(solution)/shard_map/ppermute | solution.py:291
  203.8 95.1 %copy-start.9 = (bf16[2,4,256,512]{3,2,1,0:T(8,128)(2,1)S(1)}, bf16[2,4,256,512]{3,2,1,0:T(8,128)(2,1)}, u32[]{:S(2)}) copy-start(bf16[2,4,256,512]{3,2,1,0:T(8,128)(2,1)} %get-tuple-element.27) | copy-start | bytes 6291460
  218.8 82.7 %collective-permute-start.11 = (bf16[2,4,256,512]{3,2,1,0:T(8,128)(2,1)}, bf16[2,4,256,512]{3,2,1,0:T(8,128)(2,1)S(1)}, u32[]{:S(2)}, u32[]{:S(2)}) collective-permute-start(bf16[2,4,256,512]{3,2,1,0:T(8,128)(2,1)} %get-tuple-element.30), channel_id=1, source_target_pairs={{0,4},{1,5},{2,6},{3,7},{4,0},{5,1},{6,2},{7,3},{8,12},{9,13},{10,... | collective-permute-start | bytes 6291464 | tf_op jit(solution)/shard_map/ppermute | solution.py:291
  243.8 54.6 %collective-permute-start.20 = (bf16[128,4096]{1,0:T(8,128)(2,1)S(1)}, bf16[128,4096]{1,0:T(8,128)(2,1)S(1)}, u32[]{:S(2)}, u32[]{:S(2)}) collective-permute-start(bf16[128,4096]{1,0:T(8,128)(2,1)S(1)} %slice.104), channel_id=1, source_target_pairs={{0,4},{1,5},{2,6},{3,7},{4,0},{5,1},{6,2},{7,3},{8,12},{9,13},{10,... | collective-permute-start | bytes 3145736 | tf_op jit(solution)/shard_map/ppermute | solution.py:291
  243.8 61.8 %collective-permute-start.22 = (bf16[256,4096]{1,0:T(8,128)(2,1)S(1)}, bf16[256,4096]{1,0:T(8,128)(2,1)S(1)}, u32[]{:S(2)}, u32[]{:S(2)}) collective-permute-start(bf16[256,4096]{1,0:T(8,128)(2,1)S(1)} %collective-permute-done.17.refs_6_), channel_id=1, source_target_pairs={{0,1},{1,0},{2,3},{3,2},{4,5},{5,4},{6,7},{7,6},{8,9},{9,8},{10,11... | collective-permute-start | bytes 6291464 | tf_op jit(solution)/shard_map/ppermute | solution.py:291
  286.2 21.8 %collective-permute-start.23 = (bf16[256,4096]{1,0:T(8,128)(2,1)S(1)}, bf16[256,4096]{1,0:T(8,128)(2,1)}, u32[]{:S(2)}, u32[]{:S(2)}) collective-permute-start(bf16[256,4096]{1,0:T(8,128)(2,1)S(1)} %collective-permute-done.18.refs_7_), channel_id=1, source_target_pairs={{0,1},{1,0},{2,3},{3,2},{4,5},{5,4},{6,7},{7,6},{8,9},{9,8},{10,11... | collective-permute-start | bytes 6291464 | tf_op jit(solution)/shard_map/ppermute | solution.py:291
  298.4 5.4 %collective-permute-start.24 = (bf16[128,4096]{1,0:T(8,128)(2,1)S(1)}, bf16[128,4096]{1,0:T(8,128)(2,1)S(1)}, u32[]{:S(2)}, u32[]{:S(2)}) collective-permute-start(bf16[128,4096]{1,0:T(8,128)(2,1)S(1)} %collective-permute-done.19.refs_8_), channel_id=1, source_target_pairs={{0,1},{1,0},{2,3},{3,2},{4,5},{5,4},{6,7},{7,6},{8,9},{9,8},{10,11... | collective-permute-start | bytes 3145736 | tf_op jit(solution)/shard_map/ppermute | solution.py:291
  298.5 7.2 %collective-permute-start.25 = (bf16[128,4096]{1,0:T(8,128)(2,1)S(1)}, bf16[128,4096]{1,0:T(8,128)(2,1)S(1)}, u32[]{:S(2)}, u32[]{:S(2)}) collective-permute-start(bf16[128,4096]{1,0:T(8,128)(2,1)S(1)} %collective-permute-done.20.refs_9_), channel_id=1, source_target_pairs={{0,1},{1,0},{2,3},{3,2},{4,5},{5,4},{6,7},{7,6},{8,9},{9,8},{10,11... | collective-permute-start | bytes 3145736 | tf_op jit(solution)/shard_map/ppermute | solution.py:291
  301.4 44.3 %collective-permute-start.7 = (bf16[4,256,512]{2,1,0:T(8,128)(2,1)}, bf16[4,256,512]{2,1,0:T(8,128)(2,1)}, u32[]{:S(2)}, u32[]{:S(2)}) collective-permute-start(bf16[4,256,512]{2,1,0:T(8,128)(2,1)} %fusion), channel_id=1, source_target_pairs={{0,4},{1,5},{2,6},{3,7},{4,0},{5,1},{6,2},{7,3},{8,12},{9,13},{10,... | collective-permute-start | bytes 3145736 | tf_op jit(solution)/shard_map/ppermute | solution.py:291
  303.9 50.2 %collective-permute-start.12 = (bf16[4,256,512]{2,1,0:T(8,128)(2,1)}, bf16[4,256,512]{2,1,0:T(8,128)(2,1)S(1)}, u32[]{:S(2)}, u32[]{:S(2)}) collective-permute-start(bf16[4,256,512]{2,1,0:T(8,128)(2,1)} %fusion.1), channel_id=1, source_target_pairs={{0,2},{1,3},{2,0},{3,1},{4,6},{5,7},{6,4},{7,5},{8,10},{9,11},{10,... | collective-permute-start | bytes 3145736 | tf_op jit(solution)/shard_map/ppermute | solution.py:291
  348.4 7.5 %collective-permute-start.10 = (bf16[256,512]{1,0:T(8,128)(2,1)S(1)}, bf16[256,512]{1,0:T(8,128)(2,1)S(1)}, u32[]{:S(2)}, u32[]{:S(2)}) collective-permute-start(bf16[256,512]{1,0:T(8,128)(2,1)S(1)} %get-tuple-element.43), channel_id=1, source_target_pairs={{0,24},{8,0},{16,8},{24,16},{1,25},{9,1},{17,9},{25,17},{2,26},{10... | collective-permute-start | bytes 786440 | tf_op jit(solution)/shard_map/ppermute | solution.py:301
  348.6 15.0 %collective-permute-start.8 = (bf16[256,512]{1,0:T(8,128)(2,1)S(1)}, bf16[256,512]{1,0:T(8,128)(2,1)S(1)}, u32[]{:S(2)}, u32[]{:S(2)}) collective-permute-start(bf16[256,512]{1,0:T(8,128)(2,1)S(1)} %get-tuple-element.42), channel_id=1, source_target_pairs={{0,8},{8,16},{16,24},{24,0},{1,9},{9,17},{17,25},{25,1},{2,10},{10... | collective-permute-start | bytes 786440 | tf_op jit(solution)/shard_map/ppermute | solution.py:301
  349.9 21.8 %collective-permute-start.9 = (bf16[256,512]{1,0:T(8,128)(2,1)S(1)}, bf16[256,512]{1,0:T(8,128)(2,1)S(1)}, u32[]{:S(2)}, u32[]{:S(2)}) collective-permute-start(bf16[256,512]{1,0:T(8,128)(2,1)S(1)} %get-tuple-element.44), channel_id=1, source_target_pairs={{0,16},{8,24},{16,0},{24,8},{1,17},{9,25},{17,1},{25,9},{2,18},{10... | collective-permute-start | bytes 786440 | tf_op jit(solution)/shard_map/ppermute | solution.py:301
  354.6 34.0 %collective-permute-start.13 = (bf16[256,512]{1,0:T(8,128)(2,1)S(1)}, bf16[256,512]{1,0:T(8,128)(2,1)S(1)}, u32[]{:S(2)}, u32[]{:S(2)}) collective-permute-start(bf16[256,512]{1,0:T(8,128)(2,1)S(1)} %get-tuple-element.45), channel_id=1, source_target_pairs={{0,8},{8,16},{16,24},{24,0},{1,9},{9,17},{17,25},{25,1},{2,10},{10... | collective-permute-start | bytes 786440 | tf_op jit(solution)/shard_map/ppermute | solution.py:301
  354.7 39.5 %collective-permute-start.14 = (bf16[256,512]{1,0:T(8,128)(2,1)S(1)}, bf16[256,512]{1,0:T(8,128)(2,1)S(1)}, u32[]{:S(2)}, u32[]{:S(2)}) collective-permute-start(bf16[256,512]{1,0:T(8,128)(2,1)S(1)} %get-tuple-element.47), channel_id=1, source_target_pairs={{0,16},{8,24},{16,0},{24,8},{1,17},{9,25},{17,1},{25,9},{2,18},{10... | collective-permute-start | bytes 786440 | tf_op jit(solution)/shard_map/ppermute | solution.py:301
  355.9 39.4 %collective-permute-start.15 = (bf16[256,512]{1,0:T(8,128)(2,1)S(1)}, bf16[256,512]{1,0:T(8,128)(2,1)S(1)}, u32[]{:S(2)}, u32[]{:S(2)}) collective-permute-start(bf16[256,512]{1,0:T(8,128)(2,1)S(1)} %get-tuple-element.46), channel_id=1, source_target_pairs={{0,24},{8,0},{16,8},{24,16},{1,25},{9,1},{17,9},{25,17},{2,26},{10... | collective-permute-start | bytes 786440 | tf_op jit(solution)/shard_map/ppermute | solution.py:301
  (19 other events, 337.9 us)

commit v2 on v1

v2 whole, which is shorter than its diff:
```python
import functools
import math

import jax
import jax.numpy as jnp
from jax import lax
from jax.experimental import pallas as pl
from jax.experimental.pallas import tpu as pltpu
from jax.sharding import PartitionSpec as P

BF16 = jnp.bfloat16
F32 = jnp.float32
VMEM_BYTES = 58 * 1024 * 1024
SMEM = pl.BlockSpec(memory_space=pltpu.SMEM)


def round_up(value, step):
    return -(-value // step) * step


def params():
    return pltpu.CompilerParams(vmem_limit_bytes=VMEM_BYTES)


def cost():
    return pl.CostEstimate(flops=1, bytes_accessed=1, transcendentals=0)


def old_range(tab, n, q):
    return tab[q], tab[q + 1]


def new_range(tab, n, q):
    k = tab[2 * n + 1 + q]
    return tab[n + 1 + jnp.minimum(k, n - 1)], tab[n + 1 + jnp.minimum(k + 1, n - 1)]


def shifted_rows(ref, start, rows):
    base = pl.multiple_of((start // 8) * 8, 8)
    rem = start - base
    x = ref[pl.ds(base, rows + 8), :]
    lanes = x.shape[1]
    y = pltpu.roll(x.reshape(rows // 8 + 1, 8, lanes), (8 - rem) % 8, 1)
    sublane = lax.broadcasted_iota(jnp.int32, (rows // 8, 8, lanes), 1)
    return jnp.where(sublane < 8 - rem, y[:-1], y[1:]).reshape(rows, lanes)


def place_groups(y, rem):
    before = jnp.concatenate([y[:1], y])
    here = jnp.concatenate([y, y[-1:]])
    sublane = lax.broadcasted_iota(jnp.int32, (1, 8, y.shape[2]), 1)
    return jnp.where(sublane < rem, before, here)


def rolled(x, rem):
    return pltpu.roll(x.reshape(x.shape[0] // 8, 8, x.shape[1]), rem, 1)


def relayout(tab, n, own, inner, outer, dst):
    slot, mv = own.shape[0], inner.shape[0]
    lanes = own.shape[1]
    q = tab[3 * n + 1]
    odd = lax.rem(q, 2) == 1
    old_start, old_end = old_range(tab, n, q)
    new_start, _ = new_range(tab, n, q)
    start = slot + jnp.clip(old_start - new_start, -slot, mv)
    base = pl.multiple_of((start // 8) * 8, 8)
    rem = start - base
    left = jnp.where(odd, inner, outer).astype(F32)
    y = jnp.concatenate([rolled(left, rem), rolled(own, rem)])
    dst[pl.ds(base, mv + slot + 8), :] = place_groups(y, rem).reshape(mv + slot + 8, lanes)
    start = mv + slot + jnp.clip(old_end - new_start, -mv, slot)
    base = pl.multiple_of((start // 8) * 8, 8)
    rem = start - base
    right = place_groups(rolled(jnp.where(odd, outer, inner).astype(F32), rem), rem).reshape(mv + 8, lanes)
    row = lax.broadcasted_iota(jnp.int32, (mv + 8, lanes), 0)
    dst[pl.ds(base, mv + 8), :] = jnp.where(row >= rem, right, dst[pl.ds(base, mv + 8), :])


def relayout_rows(slot, mv):
    return 2 * slot + 2 * mv + 16


def hidden_kernel(n, rows, tab, gate, up, *refs):
    outs, scratch = refs[:-1], refs[-1]
    tokens, width = gate.shape
    for first in range(0, width, 128):
        last = min(first + 128, width)
        g = gate[:, first:last].astype(F32)
        h = g / (1.0 + jnp.exp(-g)) * up[:, first:last].astype(F32)
        scratch[first:last, :] = h.T
    scratch[width:, :] = jnp.zeros((scratch.shape[0] - width, tokens), F32)
    q = tab[3 * n + 1]
    for rel, out in enumerate(outs):
        for other in range(2):
            start, _ = new_range(tab, n, q ^ (2 * rel + other))
            out[other] = shifted_rows(scratch, start, rows).astype(BF16)


def hidden_windows(tab, gate, up, n, rows):
    tokens, width = gate.shape
    shape = jax.ShapeDtypeStruct((2, rows, tokens), BF16)
    return pl.pallas_call(
        functools.partial(hidden_kernel, n, rows),
        out_shape=[shape] * (n // 2),
        in_specs=[SMEM, pl.BlockSpec(memory_space=pltpu.VMEM), pl.BlockSpec(memory_space=pltpu.VMEM)],
        out_specs=[pl.BlockSpec(memory_space=pltpu.VMEM)] * (n // 2),
        scratch_shapes=[pltpu.VMEM((round_up(width, 8) + rows + 8, tokens), F32)],
        compiler_params=params(),
        cost_estimate=cost(),
    )(tab, gate, up)


def edges_kernel(n, mv, count, block, starts, tab, *refs):
    ins, inner, outers, (head, tail, sems) = refs[:count], refs[count], refs[count + 1 : -3], refs[-3:]
    q = tab[3 * n + 1]
    odd = lax.rem(q, 2) == 1
    old_start, old_end = old_range(tab, n, q)
    live = old_end - old_start
    slot, width = ins[0].shape
    base = pl.multiple_of((jnp.clip(live - mv, 0, slot - mv - 8) // 8) * 8, 8)
    copies = []
    for i in range(count):
        copies.append(pltpu.make_async_copy(ins[i].at[pl.ds(0, mv)], head.at[i], sems.at[i, 0]))
        copies.append(
            pltpu.make_async_copy(ins[i].at[pl.ds(base, mv + 8)], tail.at[i, pl.ds(mv + 8, mv + 8)], sems.at[i, 1])
        )
    for copy in copies:
        copy.start()
    size = len(starts[0]) * count * block
    for i in range(count):
        copies[2 * i].wait()
        copies[2 * i + 1].wait()
        for part, blocks in enumerate(starts):
            for at, start in enumerate(blocks):
                columns = slice(start, start + block)
                first = head[i, :, columns].astype(BF16)
                last = shifted_rows(tail.at[i, :, columns], live + 8 - base, mv).astype(BF16)
                place = (at * count + i) * block
                outers[part][:, place : place + block] = jnp.where(odd, last, first)
                place += part * size
                inner[:, place : place + block] = jnp.where(odd, first, last)


def edges(tab, arrays, n, mv, block, starts):
    width = arrays[0].shape[1]
    count = len(arrays)
    return pl.pallas_call(
        functools.partial(edges_kernel, n, mv, count, block, starts),
        out_shape=[jax.ShapeDtypeStruct((mv, count * width), BF16)]
        + [jax.ShapeDtypeStruct((mv, count * width // len(starts)), BF16)] * len(starts),
        in_specs=[SMEM] + [pl.BlockSpec(memory_space=pl.ANY)] * count,
        out_specs=[pl.BlockSpec(memory_space=pltpu.VMEM)] * (1 + len(starts)),
        scratch_shapes=[
            pltpu.VMEM((count, mv, width), F32),
            pltpu.VMEM((count, 2 * mv + 32, width), F32),
            pltpu.SemaphoreType.DMA((count, 2)),
        ],
        compiler_params=params(),
        cost_estimate=cost(),
    )(tab, *arrays)


def weights_kernel(n, tab, own, inner, outer, out, dst):
    slot, mv = own.shape[0], inner.shape[0]
    relayout(tab, n, own[...], inner[...], outer[...], dst)
    start, end = new_range(tab, n, tab[3 * n + 1])
    row = lax.broadcasted_iota(jnp.int32, own.shape, 0)
    kept = jnp.where(row < end - start, dst[mv + slot : mv + 2 * slot, :], 0.0).astype(BF16)
    if out.shape[1] > slot:
        kept = jnp.concatenate([kept, jnp.zeros((out.shape[1] - slot, kept.shape[1]), BF16)])
    block = out.shape[2]
    for i in range(out.shape[0]):
        out[i] = kept[:, i * block : (i + 1) * block]


def new_weights(tab, own, inner, outer, n, n_dp, rows, half):
    slot, width = own.shape
    mv = inner.shape[0]
    block = width // (2 * n_dp)

    def group(s, tab):
        return lax.rem(tab[3 * n + 2] + s, n_dp)

    return pl.pallas_call(
        functools.partial(weights_kernel, n),
        out_shape=jax.ShapeDtypeStruct((2, rows, width // 4), BF16),
        grid_spec=pltpu.PrefetchScalarGridSpec(
            num_scalar_prefetch=1,
            grid=(n_dp,),
            in_specs=[
                pl.BlockSpec((slot, block), lambda s, tab: (0, 2 * group(s, tab) + half)),
                pl.BlockSpec((mv, block), lambda s, tab: (0, half * n_dp + group(s, tab))),
                pl.BlockSpec((mv, block), lambda s, tab: (0, group(s, tab))),
            ],
            out_specs=pl.BlockSpec((2, rows, block // 2), lambda s, tab: (0, 0, s)),
            scratch_shapes=[pltpu.VMEM((relayout_rows(slot, mv), block), F32)],
        ),
        compiler_params=params(),
        cost_estimate=cost(),
    )(tab, own, inner, outer)


def turned_kernel(piece, out):
    rows = piece.shape[1]
    for e in range(2):
        out[:, e * rows : (e + 1) * rows] = piece[e].astype(F32).T.astype(BF16)


def turned(piece):
    return pl.pallas_call(
        turned_kernel,
        out_shape=jax.ShapeDtypeStruct((piece.shape[2], 2 * piece.shape[1]), BF16),
        in_specs=[pl.BlockSpec(memory_space=pltpu.VMEM)],
        out_specs=pl.BlockSpec(memory_space=pltpu.VMEM),
        compiler_params=params(),
        cost_estimate=cost(),
    )(piece)


def forward_kernel(sent, tab, *refs):
    pieces, (mine, other, send, keep, hid, weights) = refs[:-6], refs[-6:]
    rows = mine.shape[1]
    tokens = send.shape[2]

    @pl.when(pl.program_id(0) == 0)
    def _():
        for i, piece in enumerate(pieces):
            hid[i * tokens : (i + 1) * tokens, :] = piece[...]

    weights[:rows, :] = mine[0]
    weights[rows:, :] = other[0]
    part = jnp.dot(hid[...], weights[...], preferred_element_type=F32).astype(BF16)
    for i in range(len(pieces)):
        block = part[i * tokens : (i + 1) * tokens, :]
        if i < sent:
            send[i, 0] = block
        else:
            keep[i - sent, 0] = block


def forward_chunk(tab, pieces, mine, other, sent, n_dp, at):
    tokens = pieces[0].shape[0]
    rows = mine.shape[1]
    block = mine.shape[2] // n_dp
    kept = len(pieces) - sent

    def out_block(s):
        return 0, s, 0, 0

    return pl.pallas_call(
        functools.partial(forward_kernel, sent),
        out_shape=[
            jax.ShapeDtypeStruct((sent, n_dp, tokens, block), BF16),
            jax.ShapeDtypeStruct((kept, n_dp, tokens, block), BF16),
        ],
        grid=(n_dp,),
        in_specs=[SMEM]
        + [pl.BlockSpec(pieces[0].shape, lambda s: (0, 0))] * len(pieces)
        + [pl.BlockSpec((1, rows, block), lambda s: (at, 0, s))] * 2,
        out_specs=[
            pl.BlockSpec((sent, 1, tokens, block), out_block),
            pl.BlockSpec((kept, 1, tokens, block), out_block),
        ],
        scratch_shapes=[
            pltpu.VMEM((len(pieces) * tokens, 2 * rows), BF16),
            pltpu.VMEM((2 * rows, block), BF16),
        ],
        compiler_params=params(),
        cost_estimate=cost(),
    )(tab, *pieces, mine, other)


def fill_tokens(ht_refs, ht):
    tokens = ht_refs[0].shape[2]
    for i, ref in enumerate(ht_refs):
        ht[:, i * tokens : (i + 1) * tokens] = ref[0]


def fill_grads(parity, og_refs, places, og):
    for ref, (at, flip, count, *more) in zip(og_refs, places):
        rows = ref.shape[0]
        if flip is None:
            og[at : at + rows, :] = ref[...]
        else:
            shift = (parity if flip == 0 else 1 - parity) * count + more[0]
            og[pl.ds(pl.multiple_of(at + shift, rows), rows), :] = ref[...]


def partner_kernel(n, pieces, places, tab, *refs):
    ht_refs, og_refs, (out, ht, og) = refs[:pieces], refs[pieces:-3], refs[-3:]

    @pl.when(pl.program_id(0) == 0)
    def _():
        fill_tokens(ht_refs, ht)

    fill_grads(lax.rem(tab[3 * n + 2], 2), og_refs, places, og)
    out[...] = jnp.dot(ht[...], og[...], preferred_element_type=F32).astype(BF16)


def partner_grad(tab, pieces, grads, places, n, part, parts):
    rows, tokens = pieces[0].shape[1:]
    width = grads[0].shape[1]
    block = min(width // parts, 512)
    steps = width // parts // block
    total = sum(g.shape[0] for g in grads)
    return pl.pallas_call(
        functools.partial(partner_kernel, n, len(pieces), places),
        out_shape=jax.ShapeDtypeStruct((rows, width // parts), BF16),
        grid=(steps,),
        in_specs=[SMEM]
        + [pl.BlockSpec((1, rows, tokens), lambda i: (1, 0, 0))] * len(pieces)
        + [pl.BlockSpec((g.shape[0], block), lambda i: (0, part * steps + i)) for g in grads],
        out_specs=pl.BlockSpec((rows, block), lambda i: (0, i)),
        scratch_shapes=[pltpu.VMEM((rows, total), BF16), pltpu.VMEM((total, block), BF16)],
        compiler_params=params(),
        cost_estimate=cost(),
    )(tab, *pieces, *grads)


def adam_kernel(n, pieces, places, scale, aliased, relayed, tab, *refs):
    ht_refs, refs = refs[:pieces], refs[pieces:]
    og_refs, refs = refs[: len(places)], refs[len(places) :]
    rest, own, (inner0, inner1, outer0, outer1, inner_both, outer_both) = refs[0], refs[1:4], refs[4:10]
    refs = refs[10:]
    relay, refs = refs[:relayed], refs[relayed + aliased :]
    outs, ht, og, moved = refs[0:3], refs[3], refs[4], refs[5:8]
    slot, mv = own[0].shape[0], inner0.shape[0]
    block = og.shape[1]
    even = lax.rem(pl.program_id(0), 2) == 0

    @pl.when(pl.program_id(0) == 0)
    def _():
        fill_tokens(ht_refs, ht)

    fill_grads(lax.rem(tab[3 * n + 2], 2), og_refs, places, og)
    inner = jnp.where(even, inner0[...], inner1[...])
    outer = jnp.where(even, outer0[...], outer1[...])
    relayout(tab, n, own[0][...], inner, outer, moved[0])
    for i in range(2):
        columns = slice(i * block, (i + 1) * block)
        outer = outer_both[:, columns]
        for ref in relay:
            outer = outer + ref[:, columns]
        relayout(tab, n, own[i + 1][...], inner_both[:, columns], outer, moved[i + 1])
    start, end = new_range(tab, n, tab[3 * n + 1])
    step = slot // 2 if slot % 16 == 0 else slot
    for base in range(0, slot, step):
        grad = jnp.dot(ht[base : base + step, :], og[...], preferred_element_type=F32)
        grad = (grad + rest[base : base + step, :].astype(F32)) * scale
        rows = slice(mv + slot + base, mv + slot + base + step)
        master, first_old, second_old = (ref[rows, :] for ref in moved)
        first_next = 0.9 * first_old + 0.1 * grad
        second_next = 0.95 * second_old + 0.05 * grad * grad
        master_next = master - 0.001 * (first_next / (jnp.sqrt(second_next) + 1e-08) + 0.1 * master)
        live = lax.broadcasted_iota(jnp.int32, grad.shape, 0) + base < end - start
        for out, value in zip(outs, (master_next, first_next, second_next)):
            out[base : base + step, :] = jnp.where(live, value, 0.0)


def adam_part(tab, pieces, grads, places, rest, own, edge, both, outs, n, n_dp, scale, part, parts):
    rows, tokens = pieces[0].shape[1:]
    slot, width = own[0].shape
    mv = both[0].shape[0]
    block = width // (2 * n_dp)
    steps = width // parts // block
    total = sum(g.shape[0] for g in grads)
    inner, outers = edge
    split = parts // (width // rest.shape[1])

    def column(i):
        return 0, part * steps + i

    def first(i):
        return 0, (part * steps + i) // 2

    def second(i):
        return 0, n_dp + (part * steps + i) // 2

    def inner_both(i):
        return 0, part * steps + i

    operands = [tab, *pieces, *grads, rest, *own, inner, inner, *outers, *both, *outs]
    return pl.pallas_call(
        functools.partial(adam_kernel, n, len(pieces), places, scale, len(outs), len(both) - 2),
        out_shape=[jax.ShapeDtypeStruct((slot, width), F32)] * 3,
        grid=(steps,),
        in_specs=[SMEM]
        + [pl.BlockSpec((1, rows, tokens), lambda i: (0, 0, 0))] * len(pieces)
        + [pl.BlockSpec((g.shape[0], block), column) for g in grads]
        + [pl.BlockSpec((rows, block), lambda i: (0, part % split * steps + i))]
        + [pl.BlockSpec((slot, block), column)] * 3
        + [pl.BlockSpec((mv, block), first), pl.BlockSpec((mv, block), second)]
        + [pl.BlockSpec((mv, block), first)] * 2
        + [pl.BlockSpec((mv, 2 * block), inner_both)]
        + [pl.BlockSpec((mv, 2 * block), lambda i: (0, i))] * (len(both) - 1)
        + [pl.BlockSpec(memory_space=pl.ANY)] * len(outs),
        out_specs=[pl.BlockSpec((slot, block), column)] * 3,
        scratch_shapes=[
            pltpu.VMEM((rows, total), BF16),
            pltpu.VMEM((total, block), BF16),
        ]
        + [pltpu.VMEM((relayout_rows(slot, mv), block), F32)] * 3,
        input_output_aliases={len(operands) - 3 + i: i for i in range(3)} if outs else {},
        compiler_params=params(),
        cost_estimate=cost(),
    )(*operands)


def swap(value, mask):
    n = lax.axis_size("fsdp")
    return lax.ppermute(value, "fsdp", [(i, i ^ mask) for i in range(n)])


def swap_outer(value, middle=True):
    n = lax.axis_size("fsdp")
    pairs = [(i, i + 1 if i % 2 else i - 1) for i in range(1, n - 1)]
    return lax.ppermute(value, "fsdp", [(i, j) for i, j in pairs if middle or {i, j} != {3, 4}])


def relay_first(value):
    return lax.ppermute(value, "fsdp", [(3, 7), (4, 0)])


def relay_second(value):
    return lax.ppermute(value, "fsdp", [(7, 4), (0, 3)])


def turn(value, steps):
    n = lax.axis_size("dp")
    return lax.ppermute(value, "dp", [(i, (i + steps) % n) for i in range(n)])


def stage(*values):
    return lax.optimization_barrier(values)


def add(a, b):
    return (a.astype(F32) + b.astype(F32)).astype(BF16)


def local(gate, up, out_grad, master_old, moment1_old, moment2_old, old_bounds, new_bounds, rank_map):
    n, n_dp = lax.axis_size("fsdp"), lax.axis_size("dp")
    groups = n // 2
    square = groups == 4
    chunks, parts = 4, 4
    tokens, block_rows = gate.shape
    slot, width = master_old.shape[1:]
    rows = round_up(slot, 16)
    mv = round_up((block_rows // n + 1) // 2, 16)
    scale = 1.0 / math.sqrt(tokens * n)
    index = jnp.stack([lax.axis_index("fsdp"), lax.axis_index("dp")]).astype(jnp.int32)
    tab = jnp.concatenate([old_bounds[0], new_bounds[0], rank_map[0], index])
    own = [master_old[0], moment1_old[0], moment2_old[0]]
    half = tokens // 2
    parity = lax.rem(lax.axis_index("dp"), 2)
    mine_grad = lax.dynamic_slice_in_dim(out_grad, parity * half, half, 0)

    block = width // (2 * n_dp)
    steps = width // parts // block
    halves = 2
    order = [2, 3, 0, 1] if square else list(range(1, groups)) + [0]
    sent = 2 if square else groups - 1

    def flip(value):
        return lax.ppermute(value, "dp", [(i, i ^ 1) for i in range(n_dp)])

    def forward(chunk):
        mine, other = weights[chunk // 2]
        return forward_chunk(tab, [tokens_first[i] for i in order], mine, other, sent, n_dp, chunk % 2)

    def first_sum(chunk):
        send = sends[chunk]
        if square:
            return [swap(send, 4)]
        return [swap(send[rel - 1], 2 * rel) for rel in range(1, groups)]

    def second_sum(chunk):
        total = keeps[chunk][0].astype(F32)
        if square:
            passed = swap(add(keeps[chunk][1], came[chunk][0][1]), 2)
            return total + came[chunk][0][0].astype(F32) + passed.astype(F32)
        for value in came[chunk]:
            total = total + value.astype(F32)
        return total

    def over_dp(chunk):
        low = totals[chunk].astype(BF16)
        out = totals[chunk][0]
        for turned_by in range(1, n_dp):
            out = out + turn(low[turned_by], turned_by).astype(F32)
        return out

    def step(part, outs):
        moved = (moving_inner, *moved_outer[part])
        value = partner[part // (parts // halves)]
        return list(
            adam_part(tab, pieces, grads, places, value, own, (inner, outers), moved, outs, n, n_dp, scale, part, parts)
        )

    inner, *outers = edges(
        tab, own[:1], n, mv, block, [[(2 * j + h) * block for j in range(n_dp)] for h in range(2)]
    )
    tab, inner, outers, mine_grad = stage(tab, inner, outers, mine_grad)
    outers = list(outers)
    inner, outers[0] = swap(inner, 1), swap_outer(outers[0])
    windows = list(hidden_windows(tab, gate, up, n, rows))
    moving = list(
        edges(
            tab,
            own[1:],
            n,
            mv,
            block,
            [[(part * steps + i) * block for i in range(steps)] for part in range(parts)],
        )
    )
    quarter = half // 2
    grad_y = [swap(mine_grad[:quarter], 4)] if square else []
    tab, inner, outers, mine_grad, grad_y, windows, moving = stage(
        tab, inner, outers, mine_grad, grad_y, windows, moving
    )

    outers, moving, grad_y = list(outers), list(moving), list(grad_y)
    outers[1] = swap_outer(outers[1])
    flips_y = []
    if square:
        grad_y.append(swap(mine_grad[quarter:], 4))
        flips_y.append(flip(grad_y[0]))
    moving_inner = swap(moving[0], 1)
    mine = new_weights(tab, own[0], inner, outers[0], n, n_dp, rows, 0)
    tab, outers, mine_grad, grad_y, flips_y, windows, moving, moving_inner, mine = stage(
        tab, outers, mine_grad, grad_y, flips_y, windows, moving, moving_inner, mine
    )

    pieces, flips_y = list(windows), list(flips_y)
    for rel in range(1, groups):
        pieces[rel] = swap(pieces[rel], 2 * rel)
    weights = [(mine, swap(mine, 1))]
    if square:
        flips_y.append(flip(grad_y[1]))
    mine = new_weights(tab, own[0], inner, outers[1], n, n_dp, rows, 1)
    tokens_first = [turned(pieces[0])]
    tab, mine_grad, flips_y, moving, pieces, weights, mine, tokens_first = stage(
        tab, mine_grad, flips_y, moving, pieces, weights, mine, tokens_first
    )

    weights = list(weights) + [(mine, swap(mine, 1))]
    tokens_first = list(tokens_first) + [turned(piece) for piece in pieces[1:]]
    sends, keeps, came, totals = [None] * chunks, [None] * chunks, [None] * chunks, [None] * chunks
    sends[0], keeps[0] = forward(0)
    grad_x = swap(mine_grad, 2) if square else mine_grad
    relays = [relay_first(moving[2]), relay_first(moving[4])] if square else []
    tab, grad_x, moving, weights, sends, keeps, tokens_first, relays = stage(
        tab, grad_x, moving, weights, sends, keeps, tokens_first, relays
    )

    sends, keeps, relays = list(sends), list(keeps), list(relays)
    moved_outer = [(swap_outer(moving[1]),)]
    if square:
        relays[0] = relay_second(relays[0])
        grad_g, flip_x = swap(grad_x, 4), flip(grad_x)
    else:
        grad_g, flip_x = grad_x, grad_x
    sends[1], keeps[1] = forward(1)
    tab, grad_x, grad_g, flip_x, moving, moved_outer, sends, keeps, relays = stage(
        tab, grad_x, grad_g, flip_x, moving, moved_outer, sends, keeps, relays
    )

    sends, keeps, moved_outer = list(sends), list(keeps), list(moved_outer)
    moved_outer.append((swap_outer(moving[2], not square), *relays[:1]))
    came[0] = first_sum(0)
    flip_g = flip(grad_g) if square else grad_g
    sends[2], keeps[2] = forward(2)
    sends[3], keeps[3] = forward(3)
    tab, flip_g, moving, moved_outer, sends, keeps, came, relays = stage(
        tab, flip_g, moving, moved_outer, sends, keeps, came, relays
    )

    keeps, came, moved_outer, relays = list(keeps), list(came), list(moved_outer), list(relays)
    if square:
        grads = [out_grad, grad_x, *grad_y, grad_g, flip_x, *flips_y, flip_g]
        places = [(0, None, tokens)]
        for which in range(2):
            places += [(tokens, which, half, 0), (2 * tokens, which, half, 0), (2 * tokens, which, half, quarter)]
            places += [(3 * tokens, which, half, 0)]
    else:
        grads = [out_grad] + [swap(out_grad, 2 * rel) for rel in range(1, groups)]
        places = [(i * tokens, None, tokens) for i in range(groups)]
    moved_outer.append((swap_outer(moving[3]),))
    if square:
        relays[1] = relay_second(relays[1])
    came[1] = first_sum(1)
    totals[0] = second_sum(0)
    partner = [partner_grad(tab, pieces, grads, places, n, i, halves) for i in range(halves)]
    tab, moving, moved_outer, sends, came, totals, partner, relays = stage(
        tab, moving, moved_outer, sends, came, totals, partner, relays
    )

    came, totals, moved_outer = list(came), list(totals), list(moved_outer)
    moved_outer.append((swap_outer(moving[4], not square), *relays[1:]))
    came[2] = first_sum(2)
    totals[1] = second_sum(1)
    partner = [swap(value, 1) for value in partner]
    outs = step(1, step(0, []))
    tab, moved_outer, sends, came, totals, partner, outs = stage(
        tab, moved_outer, sends, came, totals, partner, outs
    )

    came, totals = list(came), list(totals)
    came[3] = first_sum(3)
    totals[2] = second_sum(2)
    results = [over_dp(0), over_dp(1)]
    outs = step(3, step(2, list(outs)))
    tab, came, totals, outs = stage(tab, came, totals, list(outs))

    totals = list(totals)
    totals[3] = second_sum(3)
    results.append(over_dp(2))
    results.append(over_dp(3))
    mlp_out = jnp.concatenate(results, axis=1)
    return mlp_out, outs[0][None], outs[1][None], outs[2][None]


def solution(mesh):
    placed = (
        P("fsdp", "dp"),
        P("fsdp", "dp"),
        P("fsdp", None),
        P("dp", "fsdp", None),
        P("dp", "fsdp", None),
        P("dp", "fsdp", None),
        P("dp", None),
        P("dp", None),
        P("dp", None),
    )
    return jax.shard_map(
        local,
        mesh=mesh,
        in_specs=placed,
        out_specs=(
            P("fsdp", "dp"),
            P("dp", "fsdp", None),
            P("dp", "fsdp", None),
            P("dp", "fsdp", None),
        ),
        check_vma=False,
    )
```

time: 399 us -> 361 us (0.905)
  waiting for transfers between devices: 239 us -> 146 us
  Pallas kernels: 94.8 us -> 132 us
  starting transfers between devices: 47.2 us -> 55.3 us
  local copies, waits for them, and re-layouts: 6.2 us -> 11.6 us
    ppermute x6 -> x14, waiting for transfers between devices: 130 us -> 29.5 us  [the longest x6 12.5 us: swap_outer(): lax.ppermute(value, 'fsdp', [(i, j) for i, j in pairs if middle or {i, j}...]
    pallas_call x5 -> x16, Pallas kernels: 79.4 us -> 115 us  [the longest x4 47.8 us: adam_part(): pl.pallas_call(functools.partial(adam_kernel, n, len(pieces), places, sca...]
    ppermute x18 -> x21, waiting for transfers between devices: 70 us -> 89.6 us  [swap(): return lax.ppermute(value, 'fsdp', [(i, i ^ mask) for i in range(n)])]
    ppermute x6 -> x12, waiting for transfers between devices: 38.7 us -> 26.4 us  [turn(): return lax.ppermute(value, 'dp', [(i, (i + steps) % n) for i in range(n)])]
    ppermute x6 -> x14, starting transfers between devices: 17.6 us -> 24.9 us  [the longest x6 15.7 us: swap_outer(): lax.ppermute(value, 'fsdp', [(i, j) for i, j in pairs if middle or {i, j}...]
    ppermute x6 -> x12, starting transfers between devices: 7.45 us -> 13.5 us  [turn(): return lax.ppermute(value, 'dp', [(i, (i + steps) % n) for i in range(n)])]
    add x2 -> x7, other arithmetic: 0.26 us -> 6.03 us  [the longest x3 4.78 us: second_sum(): return total + came[chunk][0][0].astype(F32) + passed.astype(F32)]
    ppermute x18 -> x21, starting transfers between devices: 22.1 us -> 16.9 us  [swap(): return lax.ppermute(value, 'fsdp', [(i, i ^ mask) for i in range(n)])]
  transfers between devices with their start and end apart: 30 -> 47, of which waited for: 14 -> 21; matrix products, arithmetic and copies ran while one was open for 2% -> 4% of each run, Pallas kernels for 20% -> 35%
where the time goes in v2:
time: 361 us; the launch traced here: 358 us
  waiting for transfers between devices  146 us (40%)
  Pallas kernels  132 us (37%)
  starting transfers between devices  55.3 us (15%)
  other arithmetic  12 us (3%)
  local copies, waits for them, and re-layouts  11.6 us (3%)
    ppermute x21, waiting for transfers between devices, swap(): return lax.ppermute(value, 'fsdp', [(i, i ^ mask) for i in range(n)])  89.6 us
    pallas_call x4, Pallas kernels, adam_part(): pl.pallas_call(functools.partial(adam_kernel, n, len(pieces), places, sca...  47.8 us
    pallas_call x4, Pallas kernels, forward_chunk(): pl.pallas_call(functools.partial(forward_kernel, sent), out_shape=[jax.Sh...  27.6 us
    ppermute x12, waiting for transfers between devices, turn(): return lax.ppermute(value, 'dp', [(i, (i + steps) % n) for i in range(n)])  26.4 us
    ppermute x21, starting transfers between devices, swap(): return lax.ppermute(value, 'fsdp', [(i, i ^ mask) for i in range(n)])  16.9 us
    pallas_call x2, Pallas kernels, edges(): pl.pallas_call(functools.partial(edges_kernel, n, mv, count, block, start...  16.1 us
    ppermute x6, starting transfers between devices, swap_outer(): lax.ppermute(value, 'fsdp', [(i, j) for i, j in pairs if middle or {i, j}...  15.7 us
    pallas_call x2, Pallas kernels, partner_grad(): pl.pallas_call(functools.partial(partner_kernel, n, len(pieces), places),...  14.1 us
  transfers between devices with their start and end apart: 47, of which 21 were waited for; matrix products, arithmetic and copies ran while one was open for 4% of the time, Pallas kernels for 35%

profile of v2, /device:TPU:11, one launch (start us, length us, event | category | flops | bytes accessed | tf_op | source)
XLA Modules:
  0.0 358.0 jit_solution(11313722188309898776)
XLA Ops:
  3.4 6.4 %shard_map.120 = (bf16[240,4096]{1,0:T(8,128)(2,1)}, bf16[240,2048]{1,0:T(8,128)(2,1)}, bf16[240,2048]{1,0:T(8,128)(2,1)}) custom-call(s32[27]{0:T(128)} %concatenate.6.tab, f32[624,4096]{1,0:T(8,128)} %bitcast.78), custom_call_target="tpu_custom_call" | custom-call | flops 1 | bytes 1 | tf_op jit(solution)/shard_map/pallas_call | solution.py:148
  10.5 3.0 collective-permute-start.1
  13.7 9.7 %shard_map.122 = (bf16[240,8192]{1,0:T(8,128)(2,1)}, bf16[240,2048]{1,0:T(8,128)(2,1)}, bf16[240,2048]{1,0:T(8,128)(2,1)}, bf16[240,2048]{1,0:T(8,128)(2,1)}, bf16[240,2048]{1,0:T(8,128)(2,1)}) custom-call(s32[27]{0:T(128)} %concatenate.6.tab, f32[624,4096]{1,0:T(8,128)} %bitcast.85, f32[624,4096]{1,0:T(8,128)} %bitcast.90), custom_call_target="tpu_custom_call" | custom-call | flops 1 | bytes 1 | tf_op jit(solution)/shard_map/pallas_call | solution.py:148
  23.4 5.0 %shard_map.121 = (bf16[2,624,256]{2,1,0:T(8,128)(2,1)}, bf16[2,624,256]{2,1,0:T(8,128)(2,1)}, bf16[2,624,256]{2,1,0:T(8,128)(2,1)}, bf16[2,624,256]{2,1,0:T(8,128)(2,1)}) custom-call(s32[27]{0:T(128)} %concatenate.6.tab, bf16[256,3712]{1,0:T(8,128)(2,1)} %gate.1, bf16[256,3712]{1,0:T(8,128)(2,1)} %up.1), custom_call_target="tpu_custom_call" | custom-call | flops 1 | bytes 1 | tf_op jit(solution)/shard_map/pallas_call | solution.py:103
  28.3 9.8 %collective-permute-done.2.refs_6_ = bf16[64,4096]{1,0:T(8,128)(2,1)S(1)} collective-permute-done((bf16[64,4096]{1,0:T(8,128)(2,1)S(1)}, bf16[64,4096]{1,0:T(8,128)(2,1)S(1)}, u32[]{:S(2)}, u32[]{:S(2)}) %collective-permute-start.2) | collective-permute-done | bytes 524320 | tf_op jit(solution)/shard_map/ppermute | solution.py:412
  44.6 6.4 %shard_map.123.refs_4_ = bf16[2,624,1024]{2,1,0:T(8,128)(2,1)} custom-call(s32[27]{0:T(128)} %concatenate.6.tab, f32[624,4096]{1,0:T(8,128)} %bitcast.79, bf16[240,4096]{1,0:T(8,128)(2,1)} %copy-done, bf16[240,2048]{1,0:T(8,128)(2,1)} %copy-done.8), custom_call_target="tpu_custom_call" | custom-call | flops 1 | bytes 1 | tf_op jit(solution)/shard_map/pallas_call | solution.py:185
  51.0 17.1 %collective-permute-done.4.refs_7_ = bf16[64,4096]{1,0:T(8,128)(2,1)} collective-permute-done((bf16[64,4096]{1,0:T(8,128)(2,1)}, bf16[64,4096]{1,0:T(8,128)(2,1)}, u32[]{:S(2)}, u32[]{:S(2)}) %collective-permute-start.4) | collective-permute-done | bytes 524320 | tf_op jit(solution)/shard_map/ppermute | solution.py:412
  73.5 6.4 %shard_map.124.refs_4_ = bf16[2,624,1024]{2,1,0:T(8,128)(2,1)} custom-call(s32[27]{0:T(128)} %concatenate.6.tab, f32[624,4096]{1,0:T(8,128)} %bitcast.80, bf16[240,4096]{1,0:T(8,128)(2,1)} %copy-done, bf16[240,2048]{1,0:T(8,128)(2,1)} %collective-permute-done.3.outer.refs_20_), custom_call_target="tpu_custom_call" | custom-call | flops 1 | bytes 1 | tf_op jit(solution)/shard_map/pallas_call | solution.py:185
  79.9 4.0 %collective-permute-done.7.refs_11_ = bf16[64,4096]{1,0:T(8,128)(2,1)} collective-permute-done((bf16[64,4096]{1,0:T(8,128)(2,1)}, bf16[64,4096]{1,0:T(8,128)(2,1)}, u32[]{:S(2)}, u32[]{:S(2)}) %collective-permute-start.7) | collective-permute-done | bytes 524320 | tf_op jit(solution)/shard_map/ppermute | solution.py:466
  85.6 11.7 %collective-permute-done.8.piece.refs_1_ = bf16[2,624,256]{2,1,0:T(8,128)(2,1)S(1)} collective-permute-done((bf16[2,624,256]{2,1,0:T(8,128)(2,1)}, bf16[2,624,256]{2,1,0:T(8,128)(2,1)S(1)}, u32[]{:S(2)}, u32[]{:S(2)}) %collective-permute-start.8) | collective-permute-done | bytes 639008 | tf_op jit(solution)/shard_map/ppermute | solution.py:412
  100.9 3.4 collective-permute-start.14
  113.4 6.9 %shard_map.129 = (bf16[2,4,256,256]{3,2,1,0:T(8,128)(2,1)}, bf16[2,4,256,256]{3,2,1,0:T(8,128)(2,1)}) custom-call(s32[27]{0:T(128)} %concatenate.6.tab, bf16[256,1248]{1,0:T(8,128)(2,1)} %shard_map.126.refs_0_, bf16[256,1248]{1,0:T(8,128)(2,1)} %shard_map.127.refs_1_, bf16[256,1248]{1,0:T(8,128)(2,1)} %shard_map.125.refs_2_, ...), custom_call_target="tpu_custom_call" | custom-call | flops 1 | bytes 1 | tf_op jit(solution)/shard_map/pallas_call | solution.py:251
  120.3 4.8 %collective-permute-done.15 = bf16[240,2048]{1,0:T(8,128)(2,1)} collective-permute-done((bf16[240,2048]{1,0:T(8,128)(2,1)}, bf16[240,2048]{1,0:T(8,128)(2,1)}, u32[]{:S(2)}, u32[]{:S(2)}) %collective-permute-start.15) | collective-permute-done | bytes 983072 | tf_op jit(solution)/shard_map/ppermute | solution.py:422
  128.6 5.1 %collective-permute-start.18 = (bf16[240,2048]{1,0:T(8,128)(2,1)S(1)}, bf16[240,2048]{1,0:T(8,128)(2,1)S(1)}, u32[]{:S(2)}, u32[]{:S(2)}) collective-permute-start(bf16[240,2048]{1,0:T(8,128)(2,1)S(1)} %copy-done.24), channel_id=1, source_target_pairs={{1,2},{2,1},{3,4},{4,3},{5,6},{6,5},{9,10},{10,9},{11,12},{12,11},... | collective-permute-start | bytes 2949128 | tf_op jit(solution)/shard_map/ppermute | solution.py:418
  135.0 6.9 %shard_map.130 = (bf16[2,4,256,256]{3,2,1,0:T(8,128)(2,1)}, bf16[2,4,256,256]{3,2,1,0:T(8,128)(2,1)}) custom-call(s32[27]{0:T(128)} %concatenate.6.tab, bf16[256,1248]{1,0:T(8,128)(2,1)} %shard_map.126.refs_0_, bf16[256,1248]{1,0:T(8,128)(2,1)} %shard_map.127.refs_1_, bf16[256,1248]{1,0:T(8,128)(2,1)} %shard_map.125.refs_2_, ...), custom_call_target="tpu_custom_call" | custom-call | flops 1 | bytes 1 | tf_op jit(solution)/shard_map/pallas_call | solution.py:251
  141.9 12.5 %collective-permute-done.18.refs_22_ = bf16[240,2048]{1,0:T(8,128)(2,1)S(1)} collective-permute-done((bf16[240,2048]{1,0:T(8,128)(2,1)S(1)}, bf16[240,2048]{1,0:T(8,128)(2,1)S(1)}, u32[]{:S(2)}, u32[]{:S(2)}) %collective-permute-start.18) | collective-permute-done | bytes 983072 | tf_op jit(solution)/shard_map/ppermute | solution.py:418
  154.5 7.4 %collective-permute-done.16.refs_8_ = bf16[128,4096]{1,0:T(8,128)(2,1)S(1)} collective-permute-done((bf16[128,4096]{1,0:T(8,128)(2,1)S(1)}, bf16[128,4096]{1,0:T(8,128)(2,1)S(1)}, u32[]{:S(2)}, u32[]{:S(2)}) %collective-permute-start.16) | collective-permute-done | bytes 1048608 | tf_op jit(solution)/shard_map/ppermute | solution.py:412
  163.5 6.8 %shard_map.132 = (bf16[2,4,256,256]{3,2,1,0:T(8,128)(2,1)}, bf16[2,4,256,256]{3,2,1,0:T(8,128)(2,1)}) custom-call(s32[27]{0:T(128)} %concatenate.6.tab, bf16[256,1248]{1,0:T(8,128)(2,1)} %shard_map.126.refs_0_, bf16[256,1248]{1,0:T(8,128)(2,1)} %shard_map.127.refs_1_, bf16[256,1248]{1,0:T(8,128)(2,1)} %shard_map.125.refs_2_, ...), custom_call_target="tpu_custom_call" | custom-call | flops 1 | bytes 1 | tf_op jit(solution)/shard_map/pallas_call | solution.py:251
  170.4 6.9 %shard_map.131 = (bf16[2,4,256,256]{3,2,1,0:T(8,128)(2,1)}, bf16[2,4,256,256]{3,2,1,0:T(8,128)(2,1)}) custom-call(s32[27]{0:T(128)} %concatenate.6.tab, bf16[256,1248]{1,0:T(8,128)(2,1)} %shard_map.126.refs_0_, bf16[256,1248]{1,0:T(8,128)(2,1)} %shard_map.127.refs_1_, bf16[256,1248]{1,0:T(8,128)(2,1)} %shard_map.125.refs_2_, ...), custom_call_target="tpu_custom_call" | custom-call | flops 1 | bytes 1 | tf_op jit(solution)/shard_map/pallas_call | solution.py:251
  177.4 8.0 %collective-permute-done.20.refs_12_ = bf16[128,4096]{1,0:T(8,128)(2,1)S(1)} collective-permute-done((bf16[128,4096]{1,0:T(8,128)(2,1)S(1)}, bf16[128,4096]{1,0:T(8,128)(2,1)S(1)}, u32[]{:S(2)}, u32[]{:S(2)}) %collective-permute-start.20) | collective-permute-done | bytes 1048608 | tf_op jit(solution)/shard_map/ppermute | solution.py:466
  194.0 7.0 %shard_map.134 = bf16[624,2048]{1,0:T(8,128)(2,1)} custom-call(s32[27]{0:T(128)} %concatenate.6.tab, bf16[2,624,256]{2,1,0:T(8,128)(2,1)} %get-tuple-element.275.piece.refs_0_, bf16[2,624,256]{2,1,0:T(8,128)(2,1)} %copy-done.7, bf16[2,624,256]{2,1,0:T(8,128)(2,1)} %collective-permute-done.9.piece.refs_2_, bf16[2,624,256]{2,1,0:T(8,128)(2,1)} %copy-done.6, ...), custom_call_target="tpu_custom_call" | custom-call | flops 1 | bytes 1 | tf_op jit(solution)/shard_map/pallas_call | solution.py:307
  201.1 7.0 %shard_map.133 = bf16[624,2048]{1,0:T(8,128)(2,1)} custom-call(s32[27]{0:T(128)} %concatenate.6.tab, bf16[2,624,256]{2,1,0:T(8,128)(2,1)} %get-tuple-element.275.piece.refs_0_, bf16[2,624,256]{2,1,0:T(8,128)(2,1)} %copy-done.7, bf16[2,624,256]{2,1,0:T(8,128)(2,1)} %collective-permute-done.9.piece.refs_2_, bf16[2,624,256]{2,1,0:T(8,128)(2,1)} %copy-done.6, ...), custom_call_target="tpu_custom_call" | custom-call | flops 1 | bytes 1 | tf_op jit(solution)/shard_map/pallas_call | solution.py:307
  208.1 16.7 %collective-permute-done.25 = bf16[4,256,256]{2,1,0:T(8,128)(2,1)} collective-permute-done((bf16[4,256,256]{2,1,0:T(8,128)(2,1)S(1)}, bf16[4,256,256]{2,1,0:T(8,128)(2,1)}, u32[]{:S(2)}, u32[]{:S(2)}) %collective-permute-start.25) | collective-permute-done | bytes 524320 | tf_op jit(solution)/shard_map/ppermute | solution.py:412
  234.8 21.5 %collective-permute-done.29 = bf16[4,256,256]{2,1,0:T(8,128)(2,1)S(1)} collective-permute-done((bf16[4,256,256]{2,1,0:T(8,128)(2,1)S(1)}, bf16[4,256,256]{2,1,0:T(8,128)(2,1)S(1)}, u32[]{:S(2)}, u32[]{:S(2)}) %collective-permute-start.29) | collective-permute-done | bytes 524320 | tf_op jit(solution)/shard_map/ppermute | solution.py:412
  260.0 11.8 %shard_map.135 = (f32[624,4096]{1,0:T(8,128)}, f32[624,4096]{1,0:T(8,128)}, f32[624,4096]{1,0:T(8,128)}) custom-call(s32[27]{0:T(128)} %concatenate.6.tab, bf16[2,624,256]{2,1,0:T(8,128)(2,1)} %get-tuple-element.275.piece.refs_0_, bf16[2,624,256]{2,1,0:T(8,128)(2,1)} %copy-done.7, bf16[2,624,256]{2,1,0:T(8,128)(2,1)} %collective-permute-done.9.piece.refs_2_, ...), custom_call_target="tpu_custom_call" | custom-call | flops 1 | bytes 1 | tf_op jit(solution)/shard_map/pallas_call | solution.py:384
  271.8 12.1 %shard_map.136 = (f32[624,4096]{1,0:T(8,128)}, f32[624,4096]{1,0:T(8,128)}, f32[624,4096]{1,0:T(8,128)}) custom-call(s32[27]{0:T(128)} %concatenate.6.tab, bf16[2,624,256]{2,1,0:T(8,128)(2,1)} %get-tuple-element.275.piece.refs_0_, bf16[2,624,256]{2,1,0:T(8,128)(2,1)} %copy-done.7, ...), custom_call_target="tpu_custom_call", output_to_operand_aliasing={{0}: (25, {}), {1}: (26, {}), {2}: (27, {})} | custom-call | flops 1 | bytes 1 | tf_op jit(solution)/shard_map/pallas_call | solution.py:384
  291.7 11.8 %shard_map.137 = (f32[624,4096]{1,0:T(8,128)}, f32[624,4096]{1,0:T(8,128)}, f32[624,4096]{1,0:T(8,128)}) custom-call(s32[27]{0:T(128)} %concatenate.6.tab, bf16[2,624,256]{2,1,0:T(8,128)(2,1)} %get-tuple-element.275.piece.refs_0_, bf16[2,624,256]{2,1,0:T(8,128)(2,1)} %copy-done.7, ...), custom_call_target="tpu_custom_call", output_to_operand_aliasing={{0}: (24, {}), {1}: (25, {}), {2}: (26, {})} | custom-call | flops 1 | bytes 1 | tf_op jit(solution)/shard_map/pallas_call | solution.py:384
  303.5 12.1 %shard_map.138 = (f32[624,4096]{1,0:T(8,128)}, f32[624,4096]{1,0:T(8,128)}, f32[624,4096]{1,0:T(8,128)}) custom-call(s32[27]{0:T(128)} %concatenate.6.tab, bf16[2,624,256]{2,1,0:T(8,128)(2,1)} %get-tuple-element.275.piece.refs_0_, bf16[2,624,256]{2,1,0:T(8,128)(2,1)} %copy-done.7, ...), custom_call_target="tpu_custom_call", output_to_operand_aliasing={{0}: (25, {}), {1}: (26, {}), {2}: (27, {})} | custom-call | flops 1 | bytes 1 | tf_op jit(solution)/shard_map/pallas_call | solution.py:384
  318.2 3.2 collective-permute-start.36
  324.2 4.8 %collective-permute-done.36 = bf16[256,256]{1,0:T(8,128)(2,1)S(1)} collective-permute-done((bf16[256,256]{1,0:T(8,128)(2,1)S(1)}, bf16[256,256]{1,0:T(8,128)(2,1)S(1)}, u32[]{:S(2)}, u32[]{:S(2)}) %collective-permute-start.36) | collective-permute-done | bytes 131104 | tf_op jit(solution)/shard_map/ppermute | solution.py:431
  335.1 3.1 collective-permute-start.45
  341.0 10.2 %collective-permute-done.42 = bf16[256,256]{1,0:T(8,128)(2,1)S(1)} collective-permute-done((bf16[256,256]{1,0:T(8,128)(2,1)S(1)}, bf16[256,256]{1,0:T(8,128)(2,1)S(1)}, u32[]{:S(2)}, u32[]{:S(2)}) %collective-permute-start.42) | collective-permute-done | bytes 131104 | tf_op jit(solution)/shard_map/ppermute | solution.py:431
  (155 shorter events, 87.4 us)
Async XLA Ops:
  9.8 28.3 %collective-permute-start = (bf16[240,4096]{1,0:T(8,128)(2,1)}, bf16[240,4096]{1,0:T(8,128)(2,1)S(1)}, u32[]{:S(2)}, u32[]{:S(2)}) collective-permute-start(bf16[240,4096]{1,0:T(8,128)(2,1)} %get-tuple-element.171), channel_id=1, source_target_pairs={{0,1},{1,0},{2,3},{3,2},{4,5},{5,4},{6,7},{7,6},{8,9},{9,8},{10,11... | collective-permute-start | bytes 5898248 | tf_op jit(solution)/shard_map/ppermute | solution.py:412
  10.5 27.6 %collective-permute-start.1 = (bf16[240,2048]{1,0:T(8,128)(2,1)}, bf16[240,2048]{1,0:T(8,128)(2,1)S(1)}, u32[]{:S(2)}, u32[]{:S(2)}) collective-permute-start(bf16[240,2048]{1,0:T(8,128)(2,1)} %get-tuple-element.172), channel_id=1, source_target_pairs={{1,2},{2,1},{3,4},{4,3},{5,6},{6,5},{9,10},{10,9},{11,12},{12,11},... | collective-permute-start | bytes 2949128 | tf_op jit(solution)/shard_map/ppermute | solution.py:418
  13.6 24.5 %collective-permute-start.2 = (bf16[64,4096]{1,0:T(8,128)(2,1)S(1)}, bf16[64,4096]{1,0:T(8,128)(2,1)S(1)}, u32[]{:S(2)}, u32[]{:S(2)}) collective-permute-start(bf16[64,4096]{1,0:T(8,128)(2,1)S(1)} %slice.102), channel_id=1, source_target_pairs={{0,4},{1,5},{2,6},{3,7},{4,0},{5,1},{6,2},{7,3},{8,12},{9,13},{10,... | collective-permute-start | bytes 1572872 | tf_op jit(solution)/shard_map/ppermute | solution.py:412
  39.2 28.9 %collective-permute-start.6 = (bf16[240,8192]{1,0:T(8,128)(2,1)}, bf16[240,8192]{1,0:T(8,128)(2,1)S(1)}, u32[]{:S(2)}, u32[]{:S(2)}) collective-permute-start(bf16[240,8192]{1,0:T(8,128)(2,1)} %get-tuple-element.193), channel_id=1, source_target_pairs={{0,1},{1,0},{2,3},{3,2},{4,5},{5,4},{6,7},{7,6},{8,9},{9,8},{10,11... | collective-permute-start | bytes 11796488 | tf_op jit(solution)/shard_map/ppermute | solution.py:412
  39.6 28.5 %collective-permute-start.3 = (bf16[240,2048]{1,0:T(8,128)(2,1)}, bf16[240,2048]{1,0:T(8,128)(2,1)}, u32[]{:S(2)}, u32[]{:S(2)}) collective-permute-start(bf16[240,2048]{1,0:T(8,128)(2,1)} %get-tuple-element.186), channel_id=1, source_target_pairs={{1,2},{2,1},{3,4},{4,3},{5,6},{6,5},{9,10},{10,9},{11,12},{12,11},... | collective-permute-start | bytes 2949128 | tf_op jit(solution)/shard_map/ppermute | solution.py:418
  44.4 23.7 %collective-permute-start.4 = (bf16[64,4096]{1,0:T(8,128)(2,1)}, bf16[64,4096]{1,0:T(8,128)(2,1)}, u32[]{:S(2)}, u32[]{:S(2)}) collective-permute-start(bf16[64,4096]{1,0:T(8,128)(2,1)} %slice.103), channel_id=1, source_target_pairs={{0,4},{1,5},{2,6},{3,7},{4,0},{5,1},{6,2},{7,3},{8,12},{9,13},{10,... | collective-permute-start | bytes 1572872 | tf_op jit(solution)/shard_map/ppermute | solution.py:412
  44.4 23.7 %collective-permute-start.5 = (bf16[64,4096]{1,0:T(8,128)(2,1)}, bf16[64,4096]{1,0:T(8,128)(2,1)}, u32[]{:S(2)}, u32[]{:S(2)}) collective-permute-start(bf16[64,4096]{1,0:T(8,128)(2,1)} %copy-done.9), channel_id=1, source_target_pairs={{0,8},{8,0},{16,24},{24,16},{1,9},{9,1},{17,25},{25,17},{2,10},{10... | collective-permute-start | bytes 1572872 | tf_op jit(solution)/shard_map/ppermute | solution.py:466
  68.1 31.7 %collective-permute-start.11 = (bf16[2,624,1024]{2,1,0:T(8,128)(2,1)}, bf16[2,624,1024]{2,1,0:T(8,128)(2,1)}, u32[]{:S(2)}, u32[]{:S(2)}) collective-permute-start(bf16[2,624,1024]{2,1,0:T(8,128)(2,1)} %shard_map.123.refs_4_), channel_id=1, source_target_pairs={{0,1},{1,0},{2,3},{3,2},{4,5},{5,4},{6,7},{7,6},{8,9},{9,8},{10,11... | collective-permute-start | bytes 7667720 | tf_op jit(solution)/shard_map/ppermute | solution.py:412
  69.3 28.0 %collective-permute-start.8 = (bf16[2,624,256]{2,1,0:T(8,128)(2,1)}, bf16[2,624,256]{2,1,0:T(8,128)(2,1)S(1)}, u32[]{:S(2)}, u32[]{:S(2)}) collective-permute-start(bf16[2,624,256]{2,1,0:T(8,128)(2,1)} %get-tuple-element.208), channel_id=1, source_target_pairs={{0,2},{1,3},{2,0},{3,1},{4,6},{5,7},{6,4},{7,5},{8,10},{9,11},{10,... | collective-permute-start | bytes 1916936 | tf_op jit(solution)/shard_map/ppermute | solution.py:412
  69.3 30.5 %collective-permute-start.9 = (bf16[2,624,256]{2,1,0:T(8,128)(2,1)}, bf16[2,624,256]{2,1,0:T(8,128)(2,1)}, u32[]{:S(2)}, u32[]{:S(2)}) collective-permute-start(bf16[2,624,256]{2,1,0:T(8,128)(2,1)} %get-tuple-element.209), channel_id=1, source_target_pairs={{0,4},{1,5},{2,6},{3,7},{4,0},{5,1},{6,2},{7,3},{8,12},{9,13},{10,... | collective-permute-start | bytes 1916936 | tf_op jit(solution)/shard_map/ppermute | solution.py:412
  99.8 25.4 %collective-permute-start.13 = (bf16[2,624,1024]{2,1,0:T(8,128)(2,1)}, bf16[2,624,1024]{2,1,0:T(8,128)(2,1)S(1)}, u32[]{:S(2)}, u32[]{:S(2)}) collective-permute-start(bf16[2,624,1024]{2,1,0:T(8,128)(2,1)} %shard_map.124.refs_4_), channel_id=1, source_target_pairs={{0,1},{1,0},{2,3},{3,2},{4,5},{5,4},{6,7},{7,6},{8,9},{9,8},{10,11... | collective-permute-start | bytes 7667720 | tf_op jit(solution)/shard_map/ppermute | solution.py:412
  100.3 24.9 %collective-permute-start.12 = (bf16[128,4096]{1,0:T(8,128)(2,1)}, bf16[128,4096]{1,0:T(8,128)(2,1)S(1)}, u32[]{:S(2)}, u32[]{:S(2)}) collective-permute-start(bf16[128,4096]{1,0:T(8,128)(2,1)} %copy-done.14), channel_id=1, source_target_pairs={{0,2},{1,3},{2,0},{3,1},{4,6},{5,7},{6,4},{7,5},{8,10},{9,11},{10,... | collective-permute-start | bytes 3145736 | tf_op jit(solution)/shard_map/ppermute | solution.py:412
  104.2 20.9 %collective-permute-start.15 = (bf16[240,2048]{1,0:T(8,128)(2,1)}, bf16[240,2048]{1,0:T(8,128)(2,1)}, u32[]{:S(2)}, u32[]{:S(2)}) collective-permute-start(bf16[240,2048]{1,0:T(8,128)(2,1)} %get-tuple-element.288), channel_id=1, source_target_pairs={{3,7},{4,0},{11,15},{12,8},{19,23},{20,16},{27,31},{28,24}} | collective-permute-start | bytes 2949128 | tf_op jit(solution)/shard_map/ppermute | solution.py:422
  126.7 35.2 %collective-permute-start.16 = (bf16[128,4096]{1,0:T(8,128)(2,1)S(1)}, bf16[128,4096]{1,0:T(8,128)(2,1)S(1)}, u32[]{:S(2)}, u32[]{:S(2)}) collective-permute-start(bf16[128,4096]{1,0:T(8,128)(2,1)S(1)} %collective-permute-done.12.refs_5_), channel_id=1, source_target_pairs={{0,4},{1,5},{2,6},{3,7},{4,0},{5,1},{6,2},{7,3},{8,12},{9,13},{10,... | collective-permute-start | bytes 3145736 | tf_op jit(solution)/shard_map/ppermute | solution.py:412
  128.6 33.3 %collective-permute-start.17 = (bf16[128,4096]{1,0:T(8,128)(2,1)S(1)}, bf16[128,4096]{1,0:T(8,128)(2,1)S(1)}, u32[]{:S(2)}, u32[]{:S(2)}) collective-permute-start(bf16[128,4096]{1,0:T(8,128)(2,1)S(1)} %collective-permute-done.12.refs_5_), channel_id=1, source_target_pairs={{0,8},{8,0},{16,24},{24,16},{1,9},{9,1},{17,25},{25,17},{2,10},{10... | collective-permute-start | bytes 3145736 | tf_op jit(solution)/shard_map/ppermute | solution.py:466
  128.6 25.8 %collective-permute-start.18 = (bf16[240,2048]{1,0:T(8,128)(2,1)S(1)}, bf16[240,2048]{1,0:T(8,128)(2,1)S(1)}, u32[]{:S(2)}, u32[]{:S(2)}) collective-permute-start(bf16[240,2048]{1,0:T(8,128)(2,1)S(1)} %copy-done.24), channel_id=1, source_target_pairs={{1,2},{2,1},{3,4},{4,3},{5,6},{6,5},{9,10},{10,9},{11,12},{12,11},... | collective-permute-start | bytes 2949128 | tf_op jit(solution)/shard_map/ppermute | solution.py:418
  161.9 23.5 %collective-permute-start.20 = (bf16[128,4096]{1,0:T(8,128)(2,1)S(1)}, bf16[128,4096]{1,0:T(8,128)(2,1)S(1)}, u32[]{:S(2)}, u32[]{:S(2)}) collective-permute-start(bf16[128,4096]{1,0:T(8,128)(2,1)S(1)} %collective-permute-done.16.refs_8_), channel_id=1, source_target_pairs={{0,8},{8,0},{16,24},{24,16},{1,9},{9,1},{17,25},{25,17},{2,10},{10... | collective-permute-start | bytes 3145736 | tf_op jit(solution)/shard_map/ppermute | solution.py:466
  162.6 24.0 %collective-permute-start.22 = (bf16[2,4,256,256]{3,2,1,0:T(8,128)(2,1)}, bf16[2,4,256,256]{3,2,1,0:T(8,128)(2,1)}, u32[]{:S(2)}, u32[]{:S(2)}) collective-permute-start(bf16[2,4,256,256]{3,2,1,0:T(8,128)(2,1)} %get-tuple-element.253), channel_id=1, source_target_pairs={{0,4},{1,5},{2,6},{3,7},{4,0},{5,1},{6,2},{7,3},{8,12},{9,13},{10,... | collective-permute-start | bytes 3145736 | tf_op jit(solution)/shard_map/ppermute | solution.py:412
  186.6 40.6 %collective-permute-start.24 = (bf16[2,4,256,256]{3,2,1,0:T(8,128)(2,1)}, bf16[2,4,256,256]{3,2,1,0:T(8,128)(2,1)S(1)}, u32[]{:S(2)}, u32[]{:S(2)}) collective-permute-start(bf16[2,4,256,256]{3,2,1,0:T(8,128)(2,1)} %get-tuple-element.270), channel_id=1, source_target_pairs={{0,4},{1,5},{2,6},{3,7},{4,0},{5,1},{6,2},{7,3},{8,12},{9,13},{10,... | collective-permute-start | bytes 3145736 | tf_op jit(solution)/shard_map/ppermute | solution.py:412
  186.9 39.3 %collective-permute-start.23 = (bf16[240,2048]{1,0:T(8,128)(2,1)}, bf16[240,2048]{1,0:T(8,128)(2,1)}, u32[]{:S(2)}, u32[]{:S(2)}) collective-permute-start(bf16[240,2048]{1,0:T(8,128)(2,1)} %get-tuple-element.265), channel_id=1, source_target_pairs={{1,2},{2,1},{3,4},{4,3},{5,6},{6,5},{9,10},{10,9},{11,12},{12,11},... | collective-permute-start | bytes 2949128 | tf_op jit(solution)/shard_map/ppermute | solution.py:418
  189.2 37.1 %collective-permute-start.26 = (bf16[240,2048]{1,0:T(8,128)(2,1)}, bf16[240,2048]{1,0:T(8,128)(2,1)S(1)}, u32[]{:S(2)}, u32[]{:S(2)}) collective-permute-start(bf16[240,2048]{1,0:T(8,128)(2,1)} %collective-permute-done.15), channel_id=1, source_target_pairs={{7,4},{0,3},{15,12},{8,11},{23,20},{16,19},{31,28},{24,27}} | collective-permute-start | bytes 2949128 | tf_op jit(solution)/shard_map/ppermute | solution.py:426
  191.6 33.2 %collective-permute-start.25 = (bf16[4,256,256]{2,1,0:T(8,128)(2,1)S(1)}, bf16[4,256,256]{2,1,0:T(8,128)(2,1)}, u32[]{:S(2)}, u32[]{:S(2)}) collective-permute-start(bf16[4,256,256]{2,1,0:T(8,128)(2,1)S(1)} %fusion), channel_id=1, source_target_pairs={{0,2},{1,3},{2,0},{3,1},{4,6},{5,7},{6,4},{7,5},{8,10},{9,11},{10,... | collective-permute-start | bytes 1572872 | tf_op jit(solution)/shard_map/ppermute | solution.py:412
  228.1 30.3 %collective-permute-start.30 = (bf16[624,2048]{1,0:T(8,128)(2,1)}, bf16[624,2048]{1,0:T(8,128)(2,1)S(1)}, u32[]{:S(2)}, u32[]{:S(2)}) collective-permute-start(bf16[624,2048]{1,0:T(8,128)(2,1)} %shard_map.133), channel_id=1, source_target_pairs={{0,1},{1,0},{2,3},{3,2},{4,5},{5,4},{6,7},{7,6},{8,9},{9,8},{10,11... | collective-permute-start | bytes 7667720 | tf_op jit(solution)/shard_map/ppermute | solution.py:412
  229.6 54.3 %collective-permute-start.31 = (bf16[624,2048]{1,0:T(8,128)(2,1)}, bf16[624,2048]{1,0:T(8,128)(2,1)S(1)}, u32[]{:S(2)}, u32[]{:S(2)}) collective-permute-start(bf16[624,2048]{1,0:T(8,128)(2,1)} %shard_map.134), channel_id=1, source_target_pairs={{0,1},{1,0},{2,3},{3,2},{4,5},{5,4},{6,7},{7,6},{8,9},{9,8},{10,11... | collective-permute-start | bytes 7667720 | tf_op jit(solution)/shard_map/ppermute | solution.py:412
  229.6 54.3 %collective-permute-start.28 = (bf16[2,4,256,256]{3,2,1,0:T(8,128)(2,1)}, bf16[2,4,256,256]{3,2,1,0:T(8,128)(2,1)}, u32[]{:S(2)}, u32[]{:S(2)}) collective-permute-start(bf16[2,4,256,256]{3,2,1,0:T(8,128)(2,1)} %get-tuple-element.290), channel_id=1, source_target_pairs={{0,4},{1,5},{2,6},{3,7},{4,0},{5,1},{6,2},{7,3},{8,12},{9,13},{10,... | collective-permute-start | bytes 3145736 | tf_op jit(solution)/shard_map/ppermute | solution.py:412
  229.6 54.3 %collective-permute-start.27 = (bf16[240,2048]{1,0:T(8,128)(2,1)}, bf16[240,2048]{1,0:T(8,128)(2,1)}, u32[]{:S(2)}, u32[]{:S(2)}) collective-permute-start(bf16[240,2048]{1,0:T(8,128)(2,1)} %get-tuple-element.288), channel_id=1, source_target_pairs={{1,2},{2,1},{5,6},{6,5},{9,10},{10,9},{13,14},{14,13},{17,18},{18,... | collective-permute-start | bytes 2949128 | tf_op jit(solution)/shard_map/ppermute | solution.py:418
  232.6 23.7 %collective-permute-start.29 = (bf16[4,256,256]{2,1,0:T(8,128)(2,1)S(1)}, bf16[4,256,256]{2,1,0:T(8,128)(2,1)S(1)}, u32[]{:S(2)}, u32[]{:S(2)}) collective-permute-start(bf16[4,256,256]{2,1,0:T(8,128)(2,1)S(1)} %fusion.1), channel_id=1, source_target_pairs={{0,2},{1,3},{2,0},{3,1},{4,6},{5,7},{6,4},{7,5},{8,10},{9,11},{10,... | collective-permute-start | bytes 1572872 | tf_op jit(solution)/shard_map/ppermute | solution.py:412
  283.9 34.2 %collective-permute-start.38 = (bf16[2,4,256,256]{3,2,1,0:T(8,128)(2,1)}, bf16[2,4,256,256]{3,2,1,0:T(8,128)(2,1)S(1)}, u32[]{:S(2)}, u32[]{:S(2)}) collective-permute-start(bf16[2,4,256,256]{3,2,1,0:T(8,128)(2,1)} %get-tuple-element.309), channel_id=1, source_target_pairs={{0,4},{1,5},{2,6},{3,7},{4,0},{5,1},{6,2},{7,3},{8,12},{9,13},{10,... | collective-permute-start | bytes 3145736 | tf_op jit(solution)/shard_map/ppermute | solution.py:412
  287.7 28.1 %collective-permute-start.39 = (bf16[4,256,256]{2,1,0:T(8,128)(2,1)}, bf16[4,256,256]{2,1,0:T(8,128)(2,1)S(1)}, u32[]{:S(2)}, u32[]{:S(2)}) collective-permute-start(bf16[4,256,256]{2,1,0:T(8,128)(2,1)} %fusion.2), channel_id=1, source_target_pairs={{0,2},{1,3},{2,0},{3,1},{4,6},{5,7},{6,4},{7,5},{8,10},{9,11},{10,... | collective-permute-start | bytes 1572872 | tf_op jit(solution)/shard_map/ppermute | solution.py:412
  288.5 33.0 %collective-permute-start.32 = (bf16[256,256]{1,0:T(8,128)(2,1)}, bf16[256,256]{1,0:T(8,128)(2,1)}, u32[]{:S(2)}, u32[]{:S(2)}) collective-permute-start(bf16[256,256]{1,0:T(8,128)(2,1)} %get-tuple-element.332), channel_id=1, source_target_pairs={{0,8},{8,16},{16,24},{24,0},{1,9},{9,17},{17,25},{25,1},{2,10},{10... | collective-permute-start | bytes 393224 | tf_op jit(solution)/shard_map/ppermute | solution.py:431
  290.4 31.2 %collective-permute-start.33 = (bf16[256,256]{1,0:T(8,128)(2,1)}, bf16[256,256]{1,0:T(8,128)(2,1)}, u32[]{:S(2)}, u32[]{:S(2)}) collective-permute-start(bf16[256,256]{1,0:T(8,128)(2,1)} %get-tuple-element.334), channel_id=1, source_target_pairs={{0,16},{8,24},{16,0},{24,8},{1,17},{9,25},{17,1},{25,9},{2,18},{10... | collective-permute-start | bytes 393224 | tf_op jit(solution)/shard_map/ppermute | solution.py:431
  291.4 31.7 %collective-permute-start.34 = (bf16[256,256]{1,0:T(8,128)(2,1)}, bf16[256,256]{1,0:T(8,128)(2,1)}, u32[]{:S(2)}, u32[]{:S(2)}) collective-permute-start(bf16[256,256]{1,0:T(8,128)(2,1)} %get-tuple-element.333), channel_id=1, source_target_pairs={{0,24},{8,0},{16,8},{24,16},{1,25},{9,1},{17,9},{25,17},{2,26},{10... | collective-permute-start | bytes 393224 | tf_op jit(solution)/shard_map/ppermute | solution.py:431
  (40 other events, 532.2 us)

commit v3 on v2

--- a/solution.py
+++ b/solution.py
@@ -45,40 +45,55 @@
     return jnp.where(sublane < 8 - rem, y[:-1], y[1:]).reshape(rows, lanes)
 
 
-def place_groups(y, rem):
-    before = jnp.concatenate([y[:1], y])
-    here = jnp.concatenate([y, y[-1:]])
-    sublane = lax.broadcasted_iota(jnp.int32, (1, 8, y.shape[2]), 1)
-    return jnp.where(sublane < rem, before, here)
+def piece_rows(rows, sizes=(48, 32, 24, 16, 8)):
+    return next(size for size in sizes if rows % size == 0)
 
 
 def rolled(x, rem):
     return pltpu.roll(x.reshape(x.shape[0] // 8, 8, x.shape[1]), rem, 1)
 
 
-def relayout(tab, n, own, inner, outer, dst):
-    slot, mv = own.shape[0], inner.shape[0]
-    lanes = own.shape[1]
+def place_rows(parts, dst, start, keep):
+    base = pl.multiple_of((start // 8) * 8, 8)
+    rem = start - base
+    last = None
+    at = 0
+    for load, rows in parts:
+        size = piece_rows(rows)
+        for first in range(0, rows, size):
+            y = rolled(load(first, size), rem)
+            lanes = y.shape[2]
+            if last is None:
+                last = dst[pl.ds(base, 8), :].reshape(1, 8, lanes) if keep else y[:1]
+            before = jnp.concatenate([last, y[:-1]]) if size > 8 else last
+            sublane = lax.broadcasted_iota(jnp.int32, y.shape, 1)
+            out = jnp.where(sublane < rem, before, y)
+            dst[pl.ds(pl.multiple_of(base + at, 8), size), :] = out.reshape(size, lanes)
+            last = y[-1:]
+            at += size
+    dst[pl.ds(pl.multiple_of(base + at, 8), 8), :] = last.reshape(8, last.shape[2])
+
+
+def relayout(tab, n, own, left, right, slot, mv, dst):
     q = tab[3 * n + 1]
-    odd = lax.rem(q, 2) == 1
     old_start, old_end = old_range(tab, n, q)
     new_start, _ = new_range(tab, n, q)
     start = slot + jnp.clip(old_start - new_start, -slot, mv)
-    base = pl.multiple_of((start // 8) * 8, 8)
-    rem = start - base
-    left = jnp.where(odd, inner, outer).astype(F32)
-    y = jnp.concatenate([rolled(left, rem), rolled(own, rem)])
-    dst[pl.ds(base, mv + slot + 8), :] = place_groups(y, rem).reshape(mv + slot + 8, lanes)
+    place_rows([(left, mv), (own, slot)], dst, start, False)
     start = mv + slot + jnp.clip(old_end - new_start, -mv, slot)
-    base = pl.multiple_of((start // 8) * 8, 8)
-    rem = start - base
-    right = place_groups(rolled(jnp.where(odd, outer, inner).astype(F32), rem), rem).reshape(mv + 8, lanes)
-    row = lax.broadcasted_iota(jnp.int32, (mv + 8, lanes), 0)
-    dst[pl.ds(base, mv + 8), :] = jnp.where(row >= rem, right, dst[pl.ds(base, mv + 8), :])
+    place_rows([(right, mv)], dst, start, True)
+
+
+def from_ref(ref, columns=slice(None)):
+    return lambda first, rows: ref[first : first + rows, columns]
+
+
+def chosen(flag, a, b):
+    return lambda first, rows: jnp.where(flag, a(first, rows), b(first, rows)).astype(F32)
 
 
 def relayout_rows(slot, mv):
-    return 2 * slot + 2 * mv + 16
+    return 2 * slot + 2 * mv + 32
 
 
 def hidden_kernel(n, rows, tab, gate, up, *refs):
@@ -91,10 +106,12 @@
         scratch[first:last, :] = h.T
     scratch[width:, :] = jnp.zeros((scratch.shape[0] - width, tokens), F32)
     q = tab[3 * n + 1]
+    piece = piece_rows(rows, (48, 16))
     for rel, out in enumerate(outs):
         for other in range(2):
             start, _ = new_range(tab, n, q ^ (2 * rel + other))
-            out[other] = shifted_rows(scratch, start, rows).astype(BF16)
+            for row in range(0, rows, piece):
+                out[other, row : row + piece, :] = shifted_rows(scratch, start + row, piece).astype(BF16)
 
 
 def hidden_windows(tab, gate, up, n, rows):
@@ -128,18 +145,21 @@
     for copy in copies:
         copy.start()
     size = len(starts[0]) * count * block
+    piece = piece_rows(mv, (48, 32, 16))
     for i in range(count):
         copies[2 * i].wait()
         copies[2 * i + 1].wait()
         for part, blocks in enumerate(starts):
             for at, start in enumerate(blocks):
                 columns = slice(start, start + block)
-                first = head[i, :, columns].astype(BF16)
-                last = shifted_rows(tail.at[i, :, columns], live + 8 - base, mv).astype(BF16)
                 place = (at * count + i) * block
-                outers[part][:, place : place + block] = jnp.where(odd, last, first)
-                place += part * size
-                inner[:, place : place + block] = jnp.where(odd, first, last)
+                for row in range(0, mv, piece):
+                    rows = slice(row, row + piece)
+                    first = head[i, rows, columns]
+                    last = shifted_rows(tail.at[i, :, columns], live + 8 - base + row, piece)
+                    outers[part][rows, place : place + block] = jnp.where(odd, last, first).astype(BF16)
+                    inner_place = place + part * size
+                    inner[rows, inner_place : inner_place + block] = jnp.where(odd, first, last).astype(BF16)
 
 
 def edges(tab, arrays, n, mv, block, starts):
@@ -163,15 +183,20 @@
 
 def weights_kernel(n, tab, own, inner, outer, out, dst):
     slot, mv = own.shape[0], inner.shape[0]
-    relayout(tab, n, own[...], inner[...], outer[...], dst)
-    start, end = new_range(tab, n, tab[3 * n + 1])
-    row = lax.broadcasted_iota(jnp.int32, own.shape, 0)
-    kept = jnp.where(row < end - start, dst[mv + slot : mv + 2 * slot, :], 0.0).astype(BF16)
-    if out.shape[1] > slot:
-        kept = jnp.concatenate([kept, jnp.zeros((out.shape[1] - slot, kept.shape[1]), BF16)])
+    q = tab[3 * n + 1]
+    odd = lax.rem(q, 2) == 1
+    left = chosen(odd, from_ref(inner), from_ref(outer))
+    right = chosen(odd, from_ref(outer), from_ref(inner))
+    relayout(tab, n, from_ref(own), left, right, slot, mv, dst)
+    start, end = new_range(tab, n, q)
     block = out.shape[2]
-    for i in range(out.shape[0]):
-        out[i] = kept[:, i * block : (i + 1) * block]
+    size = piece_rows(out.shape[1], (48, 32, 16))
+    for first in range(0, out.shape[1], size):
+        kept = dst[mv + slot + first : mv + slot + first + size, :]
+        row = lax.broadcasted_iota(jnp.int32, kept.shape, 0) + first
+        kept = jnp.where(row < end - start, kept, 0.0).astype(BF16)
+        for i in range(out.shape[0]):
+            out[i, first : first + size, :] = kept[:, i * block : (i + 1) * block]
 
 
 def new_weights(tab, own, inner, outer, n, n_dp, rows, half):
@@ -219,9 +244,11 @@
 
 
 def forward_kernel(sent, tab, *refs):
-    pieces, (mine, other, send, keep, hid, weights) = refs[:-6], refs[-6:]
+    outs = refs[-4:-2] if sent else refs[-3:-2]
+    pieces, (mine, other) = refs[: -4 - len(outs)], refs[-4 - len(outs) : -2 - len(outs)]
+    hid, weights = refs[-2:]
     rows = mine.shape[1]
-    tokens = send.shape[2]
+    tokens = pieces[0].shape[0]
 
     @pl.when(pl.program_id(0) == 0)
     def _():
@@ -233,35 +260,34 @@
     part = jnp.dot(hid[...], weights[...], preferred_element_type=F32).astype(BF16)
     for i in range(len(pieces)):
         block = part[i * tokens : (i + 1) * tokens, :]
-        if i < sent:
-            send[i, 0] = block
+        if not sent:
+            outs[0][0, i] = block
+        elif i < sent:
+            outs[0][i, 0] = block
         else:
-            keep[i - sent, 0] = block
+            outs[1][i - sent, 0] = block
 
 
 def forward_chunk(tab, pieces, mine, other, sent, n_dp, at):
     tokens = pieces[0].shape[0]
     rows = mine.shape[1]
     block = mine.shape[2] // n_dp
-    kept = len(pieces) - sent
-
-    def out_block(s):
-        return 0, s, 0, 0
+    count = len(pieces)
+    if sent:
+        out_shape = [(sent, n_dp, tokens, block), (count - sent, n_dp, tokens, block)]
+        out_specs = [pl.BlockSpec((shape[0], 1, tokens, block), lambda s: (0, s, 0, 0)) for shape in out_shape]
+    else:
+        out_shape = [(n_dp, count, tokens, block)]
+        out_specs = [pl.BlockSpec((1, count, tokens, block), lambda s: (s, 0, 0, 0))]
 
     return pl.pallas_call(
         functools.partial(forward_kernel, sent),
-        out_shape=[
-            jax.ShapeDtypeStruct((sent, n_dp, tokens, block), BF16),
-            jax.ShapeDtypeStruct((kept, n_dp, tokens, block), BF16),
-        ],
+        out_shape=[jax.ShapeDtypeStruct(shape, BF16) for shape in out_shape],
         grid=(n_dp,),
         in_specs=[SMEM]
         + [pl.BlockSpec(pieces[0].shape, lambda s: (0, 0))] * len(pieces)
         + [pl.BlockSpec((1, rows, block), lambda s: (at, 0, s))] * 2,
-        out_specs=[
-            pl.BlockSpec((sent, 1, tokens, block), out_block),
-            pl.BlockSpec((kept, 1, tokens, block), out_block),
-        ],
+        out_specs=out_specs,
         scratch_shapes=[
             pltpu.VMEM((len(pieces) * tokens, 2 * rows), BF16),
             pltpu.VMEM((2 * rows, block), BF16),
@@ -298,19 +324,19 @@
     out[...] = jnp.dot(ht[...], og[...], preferred_element_type=F32).astype(BF16)
 
 
-def partner_grad(tab, pieces, grads, places, n, part, parts):
+def partner_grad(tab, pieces, grads, places, n):
     rows, tokens = pieces[0].shape[1:]
     width = grads[0].shape[1]
-    block = min(width // parts, 512)
-    steps = width // parts // block
+    block = min(width, 512)
+    steps = width // block
     total = sum(g.shape[0] for g in grads)
     return pl.pallas_call(
         functools.partial(partner_kernel, n, len(pieces), places),
-        out_shape=jax.ShapeDtypeStruct((rows, width // parts), BF16),
+        out_shape=jax.ShapeDtypeStruct((rows, width), BF16),
         grid=(steps,),
         in_specs=[SMEM]
         + [pl.BlockSpec((1, rows, tokens), lambda i: (1, 0, 0))] * len(pieces)
-        + [pl.BlockSpec((g.shape[0], block), lambda i: (0, part * steps + i)) for g in grads],
+        + [pl.BlockSpec((g.shape[0], block), lambda i: (0, i)) for g in grads],
         out_specs=pl.BlockSpec((rows, block), lambda i: (0, i)),
         scratch_shapes=[pltpu.VMEM((rows, total), BF16), pltpu.VMEM((total, block), BF16)],
         compiler_params=params(),
@@ -324,58 +350,61 @@
     rest, own, (inner0, inner1, outer0, outer1, inner_both, outer_both) = refs[0], refs[1:4], refs[4:10]
     refs = refs[10:]
     relay, refs = refs[:relayed], refs[relayed + aliased :]
-    outs, ht, og, moved = refs[0:3], refs[3], refs[4], refs[5:8]
+    outs, ht, og, gradient, moved = refs[0:3], refs[3], refs[4], refs[5], refs[6:9]
     slot, mv = own[0].shape[0], inner0.shape[0]
     block = og.shape[1]
-    even = lax.rem(pl.program_id(0), 2) == 0
+    even = lax.rem(pl.program_id(0) // 2, 2) == 0
 
     @pl.when(pl.program_id(0) == 0)
     def _():
         fill_tokens(ht_refs, ht)
 
     fill_grads(lax.rem(tab[3 * n + 2], 2), og_refs, places, og)
-    inner = jnp.where(even, inner0[...], inner1[...])
-    outer = jnp.where(even, outer0[...], outer1[...])
-    relayout(tab, n, own[0][...], inner, outer, moved[0])
+    odd = lax.rem(tab[3 * n + 1], 2) == 1
+    middle = (tab[3 * n + 1] == n // 2 - 1) | (tab[3 * n + 1] == n // 2)
+    inner = chosen(even, from_ref(inner0), from_ref(inner1))
+    outer = chosen(even, from_ref(outer0), from_ref(outer1))
+    relayout(tab, n, from_ref(own[0]), chosen(odd, inner, outer), chosen(odd, outer, inner), slot, mv, moved[0])
     for i in range(2):
         columns = slice(i * block, (i + 1) * block)
-        outer = outer_both[:, columns]
-        for ref in relay:
-            outer = outer + ref[:, columns]
-        relayout(tab, n, own[i + 1][...], inner_both[:, columns], outer, moved[i + 1])
+        inner, outer = from_ref(inner_both, columns), from_ref(outer_both, columns)
+        if relay:
+            outer = chosen(middle, from_ref(relay[0], columns), outer)
+            inner = chosen(True, inner, inner)
+        relayout(tab, n, from_ref(own[i + 1]), chosen(odd, inner, outer), chosen(odd, outer, inner), slot, mv, moved[i + 1])
     start, end = new_range(tab, n, tab[3 * n + 1])
-    step = slot // 2 if slot % 16 == 0 else slot
-    for base in range(0, slot, step):
-        grad = jnp.dot(ht[base : base + step, :], og[...], preferred_element_type=F32)
-        grad = (grad + rest[base : base + step, :].astype(F32)) * scale
-        rows = slice(mv + slot + base, mv + slot + base + step)
-        master, first_old, second_old = (ref[rows, :] for ref in moved)
+    gradient[...] = jnp.dot(ht[...], og[...], preferred_element_type=F32)
+    gradient[...] = (gradient[...] + rest[...].astype(F32)) * scale
+    size = piece_rows(slot, (24, 16, 8))
+    for first in range(0, slot, size):
+        grad = gradient[first : first + size, :]
+        at = mv + slot + first
+        master, first_old, second_old = (ref[at : at + size, :] for ref in moved)
         first_next = 0.9 * first_old + 0.1 * grad
         second_next = 0.95 * second_old + 0.05 * grad * grad
         master_next = master - 0.001 * (first_next / (jnp.sqrt(second_next) + 1e-08) + 0.1 * master)
-        live = lax.broadcasted_iota(jnp.int32, grad.shape, 0) + base < end - start
+        live = lax.broadcasted_iota(jnp.int32, grad.shape, 0) + first < end - start
         for out, value in zip(outs, (master_next, first_next, second_next)):
-            out[base : base + step, :] = jnp.where(live, value, 0.0)
+            out[first : first + size, :] = jnp.where(live, value, 0.0)
 
 
 def adam_part(tab, pieces, grads, places, rest, own, edge, both, outs, n, n_dp, scale, part, parts):
     rows, tokens = pieces[0].shape[1:]
     slot, width = own[0].shape
     mv = both[0].shape[0]
-    block = width // (2 * n_dp)
+    block = width // (4 * n_dp)
     steps = width // parts // block
     total = sum(g.shape[0] for g in grads)
     inner, outers = edge
-    split = parts // (width // rest.shape[1])
 
     def column(i):
         return 0, part * steps + i
 
     def first(i):
-        return 0, (part * steps + i) // 2
+        return 0, (part * steps + i) // 4 * 2 + i % 2
 
     def second(i):
-        return 0, n_dp + (part * steps + i) // 2
+        return 0, 2 * n_dp + (part * steps + i) // 4 * 2 + i % 2
 
     def inner_both(i):
         return 0, part * steps + i
@@ -388,7 +417,7 @@
         in_specs=[SMEM]
         + [pl.BlockSpec((1, rows, tokens), lambda i: (0, 0, 0))] * len(pieces)
         + [pl.BlockSpec((g.shape[0], block), column) for g in grads]
-        + [pl.BlockSpec((rows, block), lambda i: (0, part % split * steps + i))]
+        + [pl.BlockSpec((rows, block), column)]
         + [pl.BlockSpec((slot, block), column)] * 3
         + [pl.BlockSpec((mv, block), first), pl.BlockSpec((mv, block), second)]
         + [pl.BlockSpec((mv, block), first)] * 2
@@ -399,6 +428,7 @@
         scratch_shapes=[
             pltpu.VMEM((rows, total), BF16),
             pltpu.VMEM((total, block), BF16),
+            pltpu.VMEM((rows, block), F32),
         ]
         + [pltpu.VMEM((relayout_rows(slot, mv), block), F32)] * 3,
         input_output_aliases={len(operands) - 3 + i: i for i in range(3)} if outs else {},
@@ -457,8 +487,8 @@
     mine_grad = lax.dynamic_slice_in_dim(out_grad, parity * half, half, 0)
 
     block = width // (2 * n_dp)
-    steps = width // parts // block
-    halves = 2
+    small = block // 2
+    steps = width // parts // small
     order = [2, 3, 0, 1] if square else list(range(1, groups)) + [0]
     sent = 2 if square else groups - 1
 
@@ -467,7 +497,8 @@
 
     def forward(chunk):
         mine, other = weights[chunk // 2]
-        return forward_chunk(tab, [tokens_first[i] for i in order], mine, other, sent, n_dp, chunk % 2)
+        by_dp = square and chunk == 1
+        return forward_chunk(tab, [tokens_first[i] for i in order], mine, other, 0 if by_dp else sent, n_dp, chunk % 2)
 
     def first_sum(chunk):
         send = sends[chunk]
@@ -476,32 +507,36 @@
         return [swap(send[rel - 1], 2 * rel) for rel in range(1, groups)]
 
     def second_sum(chunk):
+        return swap(add(keeps[chunk][1], came[chunk][0][1]), 2) if square else tab
+
+    def summed(chunk, passed):
         total = keeps[chunk][0].astype(F32)
         if square:
-            passed = swap(add(keeps[chunk][1], came[chunk][0][1]), 2)
             return total + came[chunk][0][0].astype(F32) + passed.astype(F32)
         for value in came[chunk]:
             total = total + value.astype(F32)
         return total
 
-    def over_dp(chunk):
-        low = totals[chunk].astype(BF16)
-        out = totals[chunk][0]
+    def over_dp(total):
+        low = total.astype(BF16)
+        out = total[0]
         for turned_by in range(1, n_dp):
             out = out + turn(low[turned_by], turned_by).astype(F32)
         return out
 
     def step(part, outs):
         moved = (moving_inner, *moved_outer[part])
-        value = partner[part // (parts // halves)]
         return list(
-            adam_part(tab, pieces, grads, places, value, own, (inner, outers), moved, outs, n, n_dp, scale, part, parts)
+            adam_part(tab, pieces, grads, places, partner, own, (inner, outers), moved, outs, n, n_dp, scale, part, parts)
         )
 
     inner, *outers = edges(
         tab, own[:1], n, mv, block, [[(2 * j + h) * block for j in range(n_dp)] for h in range(2)]
     )
-    tab, inner, outers, mine_grad = stage(tab, inner, outers, mine_grad)
+    quarter = half // 2
+    tab, inner, outers, mine_grad, quarters = stage(
+        tab, inner, outers, mine_grad, [mine_grad[:quarter], mine_grad[quarter:]]
+    )
     outers = list(outers)
     inner, outers[0] = swap(inner, 1), swap_outer(outers[0])
     windows = list(hidden_windows(tab, gate, up, n, rows))
@@ -511,12 +546,11 @@
             own[1:],
             n,
             mv,
-            block,
-            [[(part * steps + i) * block for i in range(steps)] for part in range(parts)],
+            small,
+            [[(part * steps + i) * small for i in range(steps)] for part in range(parts)],
         )
     )
-    quarter = half // 2
-    grad_y = [swap(mine_grad[:quarter], 4)] if square else []
+    grad_y = [swap(quarters[0], 4)] if square else []
     tab, inner, outers, mine_grad, grad_y, windows, moving = stage(
         tab, inner, outers, mine_grad, grad_y, windows, moving
     )
@@ -525,7 +559,7 @@
     outers[1] = swap_outer(outers[1])
     flips_y = []
     if square:
-        grad_y.append(swap(mine_grad[quarter:], 4))
+        grad_y.append(swap(quarters[1], 4))
         flips_y.append(flip(grad_y[0]))
     moving_inner = swap(moving[0], 1)
     mine = new_weights(tab, own[0], inner, outers[0], n, n_dp, rows, 0)
@@ -549,10 +583,15 @@
     tokens_first = list(tokens_first) + [turned(piece) for piece in pieces[1:]]
     sends, keeps, came, totals = [None] * chunks, [None] * chunks, [None] * chunks, [None] * chunks
     sends[0], keeps[0] = forward(0)
+    if square:
+        (last,) = forward(1)
+    else:
+        sends[1], keeps[1] = forward(1)
+        last = tab
     grad_x = swap(mine_grad, 2) if square else mine_grad
     relays = [relay_first(moving[2]), relay_first(moving[4])] if square else []
-    tab, grad_x, moving, weights, sends, keeps, tokens_first, relays = stage(
-        tab, grad_x, moving, weights, sends, keeps, tokens_first, relays
+    tab, grad_x, moving, weights, sends, keeps, tokens_first, relays, last = stage(
+        tab, grad_x, moving, weights, sends, keeps, tokens_first, relays, last
     )
 
     sends, keeps, relays = list(sends), list(keeps), list(relays)
@@ -562,22 +601,24 @@
         grad_g, flip_x = swap(grad_x, 4), flip(grad_x)
     else:
         grad_g, flip_x = grad_x, grad_x
-    sends[1], keeps[1] = forward(1)
-    tab, grad_x, grad_g, flip_x, moving, moved_outer, sends, keeps, relays = stage(
-        tab, grad_x, grad_g, flip_x, moving, moved_outer, sends, keeps, relays
-    )
-
-    sends, keeps, moved_outer = list(sends), list(keeps), list(moved_outer)
+    turns = [turn(last[i], i) for i in range(2, n_dp, 2)] if square else []
+    sends[2], keeps[2] = forward(2)
+    sends[3], keeps[3] = forward(3)
+    tab, grad_x, grad_g, flip_x, moving, moved_outer, sends, keeps, relays, turns, last = stage(
+        tab, grad_x, grad_g, flip_x, moving, moved_outer, sends, keeps, relays, turns, last
+    )
+
+    sends, keeps, moved_outer, relays = list(sends), list(keeps), list(moved_outer), list(relays)
     moved_outer.append((swap_outer(moving[2], not square), *relays[:1]))
     came[0] = first_sum(0)
+    if square:
+        relays[1] = relay_second(relays[1])
     flip_g = flip(grad_g) if square else grad_g
-    sends[2], keeps[2] = forward(2)
-    sends[3], keeps[3] = forward(3)
-    tab, flip_g, moving, moved_outer, sends, keeps, came, relays = stage(
-        tab, flip_g, moving, moved_outer, sends, keeps, came, relays
-    )
-
-    keeps, came, moved_outer, relays = list(keeps), list(came), list(moved_outer), list(relays)
+    tab, flip_g, moving, moved_outer, sends, keeps, came, relays, last = stage(
+        tab, flip_g, moving, moved_outer, sends, keeps, came, relays, last
+    )
+
+    keeps, came, moved_outer = list(keeps), list(came), list(moved_outer)
     if square:
         grads = [out_grad, grad_x, *grad_y, grad_g, flip_x, *flips_y, flip_g]
         places = [(0, None, tokens)]
@@ -588,36 +629,43 @@
         grads = [out_grad] + [swap(out_grad, 2 * rel) for rel in range(1, groups)]
         places = [(i * tokens, None, tokens) for i in range(groups)]
     moved_outer.append((swap_outer(moving[3]),))
-    if square:
-        relays[1] = relay_second(relays[1])
-    came[1] = first_sum(1)
+    came[2] = first_sum(2)
     totals[0] = second_sum(0)
-    partner = [partner_grad(tab, pieces, grads, places, n, i, halves) for i in range(halves)]
-    tab, moving, moved_outer, sends, came, totals, partner, relays = stage(
-        tab, moving, moved_outer, sends, came, totals, partner, relays
+    turns = list(turns)
+    if square:
+        turns += [turn(last[i], i) for i in range(1, n_dp, 2)]
+    partner = partner_grad(tab, pieces, grads, places, n)
+    tab, moving, moved_outer, sends, came, totals, partner, turns, last = stage(
+        tab, moving, moved_outer, sends, came, totals, partner, turns, last
     )
 
     came, totals, moved_outer = list(came), list(totals), list(moved_outer)
     moved_outer.append((swap_outer(moving[4], not square), *relays[1:]))
-    came[2] = first_sum(2)
-    totals[1] = second_sum(1)
-    partner = [swap(value, 1) for value in partner]
-    outs = step(1, step(0, []))
-    tab, moved_outer, sends, came, totals, partner, outs = stage(
-        tab, moved_outer, sends, came, totals, partner, outs
-    )
-
-    came, totals = list(came), list(totals)
     came[3] = first_sum(3)
     totals[2] = second_sum(2)
-    results = [over_dp(0), over_dp(1)]
+    partner, tab = stage(swap(partner, 1), tab)
+    outs = step(1, step(0, []))
+    tab, moved_outer, sends, came, totals, outs, turns = stage(
+        tab, moved_outer, sends, came, totals, outs, turns
+    )
+
+    came, totals = list(came), list(totals)
+    totals[3] = second_sum(3)
+    if square:
+        total = last[0].astype(F32)
+        for value in turns:
+            total = total + value.astype(F32)
+        came[1] = [swap(total[:2].astype(BF16), 4)]
+        keeps[1] = total[2:]
+    else:
+        came[1] = first_sum(1)
+    both = over_dp(jnp.stack([summed(i, totals[i]) for i in (0, 2)], axis=1))
     outs = step(3, step(2, list(outs)))
     tab, came, totals, outs = stage(tab, came, totals, list(outs))
 
     totals = list(totals)
-    totals[3] = second_sum(3)
-    results.append(over_dp(2))
-    results.append(over_dp(3))
+    total = summed(1, second_sum(1))
+    results = [both[0], total if square else over_dp(total), both[1], over_dp(summed(3, totals[3]))]
     mlp_out = jnp.concatenate(results, axis=1)
     return mlp_out, outs[0][None], outs[1][None], outs[2][None]
 

time: 361 us -> 322 us (0.89)
  waiting for transfers between devices: 146 us -> 111 us
    ppermute x21 -> x20, waiting for transfers between devices: 89.6 us -> 58.9 us  [swap(): return lax.ppermute(value, 'fsdp', [(i, i ^ mask) for i in range(n)])]
    ppermute x2, waiting for transfers between devices: 0.07 us -> 24 us  [relay_second(): return lax.ppermute(value, 'fsdp', [(7, 4), (0, 3)])]
    ppermute x6, waiting for transfers between devices: 12.5 us -> 0.02 us  [swap_outer(): lax.ppermute(value, 'fsdp', [(i, j) for i, j in pairs if middle or {i, j}...]
    ppermute x4, waiting for transfers between devices: 12.1 us -> 4.25 us  [flip(): return lax.ppermute(value, 'dp', [(i, i ^ 1) for i in range(n_dp)])]
    ppermute x2, waiting for transfers between devices: 4.82 us -> 0.01 us  [relay_first(): return lax.ppermute(value, 'fsdp', [(3, 7), (4, 0)])]
    ppermute x12 -> x9, waiting for transfers between devices: 26.4 us -> 23.9 us  [turn(): return lax.ppermute(value, 'dp', [(i, (i + steps) % n) for i in range(n)])]
    pallas_call x2 -> x1, Pallas kernels: 14.1 us -> 11.9 us  [partner_grad(): pl.pallas_call(functools.partial(partner_kernel, n, len(pieces), places),...]
    ppermute x12 -> x9, starting transfers between devices: 13.5 us -> 11.8 us  [turn(): return lax.ppermute(value, 'dp', [(i, (i + steps) % n) for i in range(n)])]
  transfers between devices with their start and end apart: 47 -> 43, of which waited for: 21 -> 12; matrix products, arithmetic and copies ran while one was open for 4% -> 3% of each run, Pallas kernels for 35% -> 38%
where the time goes in v3:
time: 322 us; the launch traced here: 319 us
  Pallas kernels  129 us (40%)
  waiting for transfers between devices  111 us (34%)
  starting transfers between devices  53.6 us (17%)
  local copies, waits for them, and re-layouts  12.8 us (4%)
  other arithmetic  11.2 us (3%)
    ppermute x20, waiting for transfers between devices, swap(): return lax.ppermute(value, 'fsdp', [(i, i ^ mask) for i in range(n)])  58.9 us
    pallas_call x4, Pallas kernels, adam_part(): pl.pallas_call(functools.partial(adam_kernel, n, len(pieces), places, sca...  46.8 us
    pallas_call x4, Pallas kernels, forward_chunk(): pl.pallas_call(functools.partial(forward_kernel, sent), out_shape=[jax.Sh...  27.4 us
    ppermute x2, waiting for transfers between devices, relay_second(): return lax.ppermute(value, 'fsdp', [(7, 4), (0, 3)])  24 us
    ppermute x9, waiting for transfers between devices, turn(): return lax.ppermute(value, 'dp', [(i, (i + steps) % n) for i in range(n)])  23.9 us
    ppermute x6, starting transfers between devices, swap_outer(): lax.ppermute(value, 'fsdp', [(i, j) for i, j in pairs if middle or {i, j}...  16.6 us
    pallas_call x2, Pallas kernels, edges(): pl.pallas_call(functools.partial(edges_kernel, n, mv, count, block, start...  16.4 us
    ppermute x20, starting transfers between devices, swap(): return lax.ppermute(value, 'fsdp', [(i, i ^ mask) for i in range(n)])  15.8 us
  transfers between devices with their start and end apart: 43, of which 12 were waited for; matrix products, arithmetic and copies ran while one was open for 3% of the time, Pallas kernels for 38%

profile of v3, /device:TPU:11, one launch (start us, length us, event | category | flops | bytes accessed | tf_op | source)
XLA Modules:
  0.0 318.8 jit_solution(12483703135669021781)
XLA Ops:
  5.7 6.6 %shard_map.120 = (bf16[240,4096]{1,0:T(8,128)(2,1)}, bf16[240,2048]{1,0:T(8,128)(2,1)}, bf16[240,2048]{1,0:T(8,128)(2,1)}) custom-call(s32[27]{0:T(128)} %concatenate.6.tab, f32[624,4096]{1,0:T(8,128)} %bitcast.79), custom_call_target="tpu_custom_call" | custom-call | flops 1 | bytes 1 | tf_op jit(solution)/shard_map/pallas_call | solution.py:168
  13.1 3.0 collective-permute-start.1
  16.2 9.7 %shard_map.122 = (bf16[240,8192]{1,0:T(8,128)(2,1)}, bf16[240,2048]{1,0:T(8,128)(2,1)}, bf16[240,2048]{1,0:T(8,128)(2,1)}, bf16[240,2048]{1,0:T(8,128)(2,1)}, bf16[240,2048]{1,0:T(8,128)(2,1)}) custom-call(s32[27]{0:T(128)} %concatenate.6.tab, f32[624,4096]{1,0:T(8,128)} %bitcast.86, f32[624,4096]{1,0:T(8,128)} %bitcast.91), custom_call_target="tpu_custom_call" | custom-call | flops 1 | bytes 1 | tf_op jit(solution)/shard_map/pallas_call | solution.py:168
  26.0 5.1 %shard_map.121 = (bf16[2,624,256]{2,1,0:T(8,128)(2,1)}, bf16[2,624,256]{2,1,0:T(8,128)(2,1)}, bf16[2,624,256]{2,1,0:T(8,128)(2,1)}, bf16[2,624,256]{2,1,0:T(8,128)(2,1)}) custom-call(s32[27]{0:T(128)} %concatenate.6.tab, bf16[256,3712]{1,0:T(8,128)(2,1)} %gate.1, bf16[256,3712]{1,0:T(8,128)(2,1)} %up.1), custom_call_target="tpu_custom_call" | custom-call | flops 1 | bytes 1 | tf_op jit(solution)/shard_map/pallas_call | solution.py:120
  31.0 9.6 %collective-permute-done.2.refs_6_ = bf16[64,4096]{1,0:T(8,128)(2,1)S(1)} collective-permute-done((bf16[64,4096]{1,0:T(8,128)(2,1)S(1)}, bf16[64,4096]{1,0:T(8,128)(2,1)S(1)}, u32[]{:S(2)}, u32[]{:S(2)}) %collective-permute-start.2) | collective-permute-done | bytes 524320 | tf_op jit(solution)/shard_map/ppermute | solution.py:442
  42.2 2.9 collective-permute-start.3
  45.5 6.1 %shard_map.123.refs_4_ = bf16[2,624,1024]{2,1,0:T(8,128)(2,1)} custom-call(s32[27]{0:T(128)} %concatenate.6.tab, f32[624,4096]{1,0:T(8,128)} %bitcast.80, bf16[240,4096]{1,0:T(8,128)(2,1)} %copy-done, bf16[240,2048]{1,0:T(8,128)(2,1)} %copy-done.7), custom_call_target="tpu_custom_call" | custom-call | flops 1 | bytes 1 | tf_op jit(solution)/shard_map/pallas_call | solution.py:210
  51.6 17.7 %collective-permute-done.4.refs_7_ = bf16[64,4096]{1,0:T(8,128)(2,1)} collective-permute-done((bf16[64,4096]{1,0:T(8,128)(2,1)}, bf16[64,4096]{1,0:T(8,128)(2,1)}, u32[]{:S(2)}, u32[]{:S(2)}) %collective-permute-start.4) | collective-permute-done | bytes 524320 | tf_op jit(solution)/shard_map/ppermute | solution.py:442
  74.7 6.1 %shard_map.124.refs_4_ = bf16[2,624,1024]{2,1,0:T(8,128)(2,1)} custom-call(s32[27]{0:T(128)} %concatenate.6.tab, f32[624,4096]{1,0:T(8,128)} %bitcast.81, bf16[240,4096]{1,0:T(8,128)(2,1)} %copy-done, bf16[240,2048]{1,0:T(8,128)(2,1)} %collective-permute-done.3.outer.refs_20_), custom_call_target="tpu_custom_call" | custom-call | flops 1 | bytes 1 | tf_op jit(solution)/shard_map/pallas_call | solution.py:210
  80.8 4.2 %collective-permute-done.7.refs_11_ = bf16[64,4096]{1,0:T(8,128)(2,1)} collective-permute-done((bf16[64,4096]{1,0:T(8,128)(2,1)}, bf16[64,4096]{1,0:T(8,128)(2,1)}, u32[]{:S(2)}, u32[]{:S(2)}) %collective-permute-start.7) | collective-permute-done | bytes 524320 | tf_op jit(solution)/shard_map/ppermute | solution.py:496
  86.7 11.8 %collective-permute-done.8.piece.refs_1_ = bf16[2,624,256]{2,1,0:T(8,128)(2,1)S(1)} collective-permute-done((bf16[2,624,256]{2,1,0:T(8,128)(2,1)}, bf16[2,624,256]{2,1,0:T(8,128)(2,1)S(1)}, u32[]{:S(2)}, u32[]{:S(2)}) %collective-permute-start.8) | collective-permute-done | bytes 639008 | tf_op jit(solution)/shard_map/ppermute | solution.py:442
  98.5 2.3 collective-permute-done.9.piece.refs_2_
  101.5 3.9 %collective-permute-start.14 = (bf16[240,2048]{1,0:T(8,128)(2,1)}, bf16[240,2048]{1,0:T(8,128)(2,1)}, u32[]{:S(2)}, u32[]{:S(2)}) collective-permute-start(bf16[240,2048]{1,0:T(8,128)(2,1)} %get-tuple-element.263), channel_id=1, source_target_pairs={{3,7},{4,0},{11,15},{12,8},{19,23},{20,16},{27,31},{28,24}} | collective-permute-start | bytes 2949128 | tf_op jit(solution)/shard_map/ppermute | solution.py:452
  110.0 2.3 shard_map.127.refs_1_
  114.6 6.8 %shard_map.130 = bf16[4,4,256,256]{3,2,1,0:T(8,128)(2,1)} custom-call(s32[27]{0:T(128)} %concatenate.6.tab, bf16[256,1248]{1,0:T(8,128)(2,1)} %shard_map.126.refs_0_, bf16[256,1248]{1,0:T(8,128)(2,1)} %shard_map.127.refs_1_, bf16[256,1248]{1,0:T(8,128)(2,1)} %shard_map.125.refs_2_, bf16[256,1248]{1,0:T(8,128)(2,1)} %shard_map.128.refs_3_, ...), custom_call_target="tpu_custom_call" | custom-call | flops 1 | bytes 1 | tf_op jit(solution)/shard_map/pallas_call | solution.py:283
  121.5 6.8 %shard_map.129 = (bf16[2,4,256,256]{3,2,1,0:T(8,128)(2,1)}, bf16[2,4,256,256]{3,2,1,0:T(8,128)(2,1)}) custom-call(s32[27]{0:T(128)} %concatenate.6.tab, bf16[256,1248]{1,0:T(8,128)(2,1)} %shard_map.126.refs_0_, bf16[256,1248]{1,0:T(8,128)(2,1)} %shard_map.127.refs_1_, bf16[256,1248]{1,0:T(8,128)(2,1)} %shard_map.125.refs_2_, ...), custom_call_target="tpu_custom_call" | custom-call | flops 1 | bytes 1 | tf_op jit(solution)/shard_map/pallas_call | solution.py:283
  128.6 5.0 %collective-permute-start.18 = (bf16[240,2048]{1,0:T(8,128)(2,1)}, bf16[240,2048]{1,0:T(8,128)(2,1)}, u32[]{:S(2)}, u32[]{:S(2)}) collective-permute-start(bf16[240,2048]{1,0:T(8,128)(2,1)} %get-tuple-element.242), channel_id=1, source_target_pairs={{1,2},{2,1},{3,4},{4,3},{5,6},{6,5},{9,10},{10,9},{11,12},{12,11},... | collective-permute-start | bytes 2949128 | tf_op jit(solution)/shard_map/ppermute | solution.py:448
  136.2 2.5 collective-permute-start.20
  138.7 6.8 %shard_map.132 = (bf16[2,4,256,256]{3,2,1,0:T(8,128)(2,1)}, bf16[2,4,256,256]{3,2,1,0:T(8,128)(2,1)}) custom-call(s32[27]{0:T(128)} %concatenate.6.tab, bf16[256,1248]{1,0:T(8,128)(2,1)} %shard_map.126.refs_0_, bf16[256,1248]{1,0:T(8,128)(2,1)} %shard_map.127.refs_1_, bf16[256,1248]{1,0:T(8,128)(2,1)} %shard_map.125.refs_2_, ...), custom_call_target="tpu_custom_call" | custom-call | flops 1 | bytes 1 | tf_op jit(solution)/shard_map/pallas_call | solution.py:283
  145.6 7.0 %shard_map.131 = (bf16[2,4,256,256]{3,2,1,0:T(8,128)(2,1)}, bf16[2,4,256,256]{3,2,1,0:T(8,128)(2,1)}) custom-call(s32[27]{0:T(128)} %concatenate.6.tab, bf16[256,1248]{1,0:T(8,128)(2,1)} %shard_map.126.refs_0_, bf16[256,1248]{1,0:T(8,128)(2,1)} %shard_map.127.refs_1_, bf16[256,1248]{1,0:T(8,128)(2,1)} %shard_map.125.refs_2_, ...), custom_call_target="tpu_custom_call" | custom-call | flops 1 | bytes 1 | tf_op jit(solution)/shard_map/pallas_call | solution.py:283
  152.5 13.2 %collective-permute-done.20 = bf16[4,256,256]{2,1,0:T(8,128)(2,1)} collective-permute-done((bf16[4,256,256]{2,1,0:T(8,128)(2,1)S(1)}, bf16[4,256,256]{2,1,0:T(8,128)(2,1)}, u32[]{:S(2)}, u32[]{:S(2)}) %collective-permute-start.20) | collective-permute-done | bytes 524320 | tf_op jit(solution)/shard_map/ppermute | solution.py:461
  168.8 23.9 %collective-permute-done.24.refs_23_ = bf16[240,2048]{1,0:T(8,128)(2,1)S(1)} collective-permute-done((bf16[240,2048]{1,0:T(8,128)(2,1)}, bf16[240,2048]{1,0:T(8,128)(2,1)S(1)}, u32[]{:S(2)}, u32[]{:S(2)}) %collective-permute-start.24) | collective-permute-done | bytes 983072 | tf_op jit(solution)/shard_map/ppermute | solution.py:456
  193.8 3.3 %collective-permute-start.25 = (bf16[240,2048]{1,0:T(8,128)(2,1)}, bf16[240,2048]{1,0:T(8,128)(2,1)}, u32[]{:S(2)}, u32[]{:S(2)}) collective-permute-start(bf16[240,2048]{1,0:T(8,128)(2,1)} %get-tuple-element.278), channel_id=1, source_target_pairs={{1,2},{2,1},{3,4},{4,3},{5,6},{6,5},{9,10},{10,9},{11,12},{12,11},... | collective-permute-start | bytes 2949128 | tf_op jit(solution)/shard_map/ppermute | solution.py:448
  202.2 11.9 %shard_map.133 = bf16[624,4096]{1,0:T(8,128)(2,1)} custom-call(s32[27]{0:T(128)} %concatenate.6.tab, bf16[2,624,256]{2,1,0:T(8,128)(2,1)} %get-tuple-element.286.piece.refs_0_, bf16[2,624,256]{2,1,0:T(8,128)(2,1)} %copy-done.9, bf16[2,624,256]{2,1,0:T(8,128)(2,1)} %copy-done.10, bf16[2,624,256]{2,1,0:T(8,128)(2,1)} %copy-done.8, bf16[256,4096]{1,0:T(8,128)(2,1)} %refs_4_.9, ...), custom_call_target="tpu_custom_call" | custom-call | flops 1 | bytes 1 | tf_op jit(solution)/shard_map/pallas_call | solution.py:333
  214.0 15.7 %collective-permute-done.27 = bf16[4,256,256]{2,1,0:T(8,128)(2,1)} collective-permute-done((bf16[4,256,256]{2,1,0:T(8,128)(2,1)}, bf16[4,256,256]{2,1,0:T(8,128)(2,1)}, u32[]{:S(2)}, u32[]{:S(2)}) %collective-permute-start.27) | collective-permute-done | bytes 524320 | tf_op jit(solution)/shard_map/ppermute | solution.py:442
  230.8 3.0 collective-permute-start.32
  241.7 11.4 %shard_map.134 = (f32[624,4096]{1,0:T(8,128)}, f32[624,4096]{1,0:T(8,128)}, f32[624,4096]{1,0:T(8,128)}) custom-call(s32[27]{0:T(128)} %concatenate.6.tab, bf16[2,624,256]{2,1,0:T(8,128)(2,1)} %get-tuple-element.286.piece.refs_0_, bf16[2,624,256]{2,1,0:T(8,128)(2,1)} %copy-done.9, bf16[2,624,256]{2,1,0:T(8,128)(2,1)} %copy-done.10, ...), custom_call_target="tpu_custom_call" | custom-call | flops 1 | bytes 1 | tf_op jit(solution)/shard_map/pallas_call | solution.py:413
  253.2 12.0 %shard_map.135 = (f32[624,4096]{1,0:T(8,128)}, f32[624,4096]{1,0:T(8,128)}, f32[624,4096]{1,0:T(8,128)}) custom-call(s32[27]{0:T(128)} %concatenate.6.tab, bf16[2,624,256]{2,1,0:T(8,128)(2,1)} %get-tuple-element.286.piece.refs_0_, bf16[2,624,256]{2,1,0:T(8,128)(2,1)} %copy-done.9, ...), custom_call_target="tpu_custom_call", output_to_operand_aliasing={{0}: (25, {}), {1}: (26, {}), {2}: (27, {})} | custom-call | flops 1 | bytes 1 | tf_op jit(solution)/shard_map/pallas_call | solution.py:413
  276.9 11.5 %shard_map.136 = (f32[624,4096]{1,0:T(8,128)}, f32[624,4096]{1,0:T(8,128)}, f32[624,4096]{1,0:T(8,128)}) custom-call(s32[27]{0:T(128)} %concatenate.6.tab, bf16[2,624,256]{2,1,0:T(8,128)(2,1)} %get-tuple-element.286.piece.refs_0_, bf16[2,624,256]{2,1,0:T(8,128)(2,1)} %copy-done.9, ...), custom_call_target="tpu_custom_call", output_to_operand_aliasing={{0}: (24, {}), {1}: (25, {}), {2}: (26, {})} | custom-call | flops 1 | bytes 1 | tf_op jit(solution)/shard_map/pallas_call | solution.py:413
  288.3 11.9 %shard_map.137 = (f32[624,4096]{1,0:T(8,128)}, f32[624,4096]{1,0:T(8,128)}, f32[624,4096]{1,0:T(8,128)}) custom-call(s32[27]{0:T(128)} %concatenate.6.tab, bf16[2,624,256]{2,1,0:T(8,128)(2,1)} %get-tuple-element.286.piece.refs_0_, bf16[2,624,256]{2,1,0:T(8,128)(2,1)} %copy-done.9, ...), custom_call_target="tpu_custom_call", output_to_operand_aliasing={{0}: (25, {}), {1}: (26, {}), {2}: (27, {})} | custom-call | flops 1 | bytes 1 | tf_op jit(solution)/shard_map/pallas_call | solution.py:413
  307.2 7.9 %collective-permute-done.41 = bf16[256,256]{1,0:T(8,128)(2,1)S(1)} collective-permute-done((bf16[256,256]{1,0:T(8,128)(2,1)S(1)}, bf16[256,256]{1,0:T(8,128)(2,1)S(1)}, u32[]{:S(2)}, u32[]{:S(2)}) %collective-permute-start.41) | collective-permute-done | bytes 131104 | tf_op jit(solution)/shard_map/ppermute | solution.py:461
  315.1 2.5 collective-permute-done.42
  (151 shorter events, 62.8 us)
Async XLA Ops:
  12.4 28.3 %collective-permute-start = (bf16[240,4096]{1,0:T(8,128)(2,1)}, bf16[240,4096]{1,0:T(8,128)(2,1)S(1)}, u32[]{:S(2)}, u32[]{:S(2)}) collective-permute-start(bf16[240,4096]{1,0:T(8,128)(2,1)} %get-tuple-element.181), channel_id=1, source_target_pairs={{0,1},{1,0},{2,3},{3,2},{4,5},{5,4},{6,7},{7,6},{8,9},{9,8},{10,11... | collective-permute-start | bytes 5898248 | tf_op jit(solution)/shard_map/ppermute | solution.py:442
  13.1 27.5 %collective-permute-start.1 = (bf16[240,2048]{1,0:T(8,128)(2,1)}, bf16[240,2048]{1,0:T(8,128)(2,1)S(1)}, u32[]{:S(2)}, u32[]{:S(2)}) collective-permute-start(bf16[240,2048]{1,0:T(8,128)(2,1)} %get-tuple-element.182), channel_id=1, source_target_pairs={{1,2},{2,1},{3,4},{4,3},{5,6},{6,5},{9,10},{10,9},{11,12},{12,11},... | collective-permute-start | bytes 2949128 | tf_op jit(solution)/shard_map/ppermute | solution.py:448
  16.1 24.5 %collective-permute-start.2 = (bf16[64,4096]{1,0:T(8,128)(2,1)S(1)}, bf16[64,4096]{1,0:T(8,128)(2,1)S(1)}, u32[]{:S(2)}, u32[]{:S(2)}) collective-permute-start(bf16[64,4096]{1,0:T(8,128)(2,1)S(1)} %get-tuple-element.185), channel_id=1, source_target_pairs={{0,4},{1,5},{2,6},{3,7},{4,0},{5,1},{6,2},{7,3},{8,12},{9,13},{10,... | collective-permute-start | bytes 1572872 | tf_op jit(solution)/shard_map/ppermute | solution.py:442
  41.9 27.5 %collective-permute-start.6 = (bf16[240,8192]{1,0:T(8,128)(2,1)}, bf16[240,8192]{1,0:T(8,128)(2,1)S(1)}, u32[]{:S(2)}, u32[]{:S(2)}) collective-permute-start(bf16[240,8192]{1,0:T(8,128)(2,1)} %get-tuple-element.205), channel_id=1, source_target_pairs={{0,1},{1,0},{2,3},{3,2},{4,5},{5,4},{6,7},{7,6},{8,9},{9,8},{10,11... | collective-permute-start | bytes 11796488 | tf_op jit(solution)/shard_map/ppermute | solution.py:442
  42.2 27.1 %collective-permute-start.3 = (bf16[240,2048]{1,0:T(8,128)(2,1)}, bf16[240,2048]{1,0:T(8,128)(2,1)}, u32[]{:S(2)}, u32[]{:S(2)}) collective-permute-start(bf16[240,2048]{1,0:T(8,128)(2,1)} %get-tuple-element.197), channel_id=1, source_target_pairs={{1,2},{2,1},{3,4},{4,3},{5,6},{6,5},{9,10},{10,9},{11,12},{12,11},... | collective-permute-start | bytes 2949128 | tf_op jit(solution)/shard_map/ppermute | solution.py:448
  69.3 31.5 %collective-permute-start.11 = (bf16[2,624,1024]{2,1,0:T(8,128)(2,1)}, bf16[2,624,1024]{2,1,0:T(8,128)(2,1)}, u32[]{:S(2)}, u32[]{:S(2)}) collective-permute-start(bf16[2,624,1024]{2,1,0:T(8,128)(2,1)} %shard_map.123.refs_4_), channel_id=1, source_target_pairs={{0,1},{1,0},{2,3},{3,2},{4,5},{5,4},{6,7},{7,6},{8,9},{9,8},{10,11... | collective-permute-start | bytes 7667720 | tf_op jit(solution)/shard_map/ppermute | solution.py:442
  70.7 27.8 %collective-permute-start.8 = (bf16[2,624,256]{2,1,0:T(8,128)(2,1)}, bf16[2,624,256]{2,1,0:T(8,128)(2,1)S(1)}, u32[]{:S(2)}, u32[]{:S(2)}) collective-permute-start(bf16[2,624,256]{2,1,0:T(8,128)(2,1)} %get-tuple-element.220), channel_id=1, source_target_pairs={{0,2},{1,3},{2,0},{3,1},{4,6},{5,7},{6,4},{7,5},{8,10},{9,11},{10,... | collective-permute-start | bytes 1916936 | tf_op jit(solution)/shard_map/ppermute | solution.py:442
  70.7 30.1 %collective-permute-start.9 = (bf16[2,624,256]{2,1,0:T(8,128)(2,1)}, bf16[2,624,256]{2,1,0:T(8,128)(2,1)S(1)}, u32[]{:S(2)}, u32[]{:S(2)}) collective-permute-start(bf16[2,624,256]{2,1,0:T(8,128)(2,1)} %get-tuple-element.221), channel_id=1, source_target_pairs={{0,4},{1,5},{2,6},{3,7},{4,0},{5,1},{6,2},{7,3},{8,12},{9,13},{10,... | collective-permute-start | bytes 1916936 | tf_op jit(solution)/shard_map/ppermute | solution.py:442
  100.8 27.5 %collective-permute-start.13 = (bf16[2,624,1024]{2,1,0:T(8,128)(2,1)}, bf16[2,624,1024]{2,1,0:T(8,128)(2,1)S(1)}, u32[]{:S(2)}, u32[]{:S(2)}) collective-permute-start(bf16[2,624,1024]{2,1,0:T(8,128)(2,1)} %shard_map.124.refs_4_), channel_id=1, source_target_pairs={{0,1},{1,0},{2,3},{3,2},{4,5},{5,4},{6,7},{7,6},{8,9},{9,8},{10,11... | collective-permute-start | bytes 7667720 | tf_op jit(solution)/shard_map/ppermute | solution.py:442
  101.3 27.0 %collective-permute-start.12 = (bf16[128,4096]{1,0:T(8,128)(2,1)}, bf16[128,4096]{1,0:T(8,128)(2,1)S(1)}, u32[]{:S(2)}, u32[]{:S(2)}) collective-permute-start(bf16[128,4096]{1,0:T(8,128)(2,1)} %constant_dynamic-slice_fusion.2), channel_id=1, source_target_pairs={{0,2},{1,3},{2,0},{3,1},{4,6},{5,7},{6,4},{7,5},{8,10},{9,11},{10,... | collective-permute-start | bytes 3145736 | tf_op jit(solution)/shard_map/ppermute | solution.py:442
  101.5 26.8 %collective-permute-start.14 = (bf16[240,2048]{1,0:T(8,128)(2,1)}, bf16[240,2048]{1,0:T(8,128)(2,1)}, u32[]{:S(2)}, u32[]{:S(2)}) collective-permute-start(bf16[240,2048]{1,0:T(8,128)(2,1)} %get-tuple-element.263), channel_id=1, source_target_pairs={{3,7},{4,0},{11,15},{12,8},{19,23},{20,16},{27,31},{28,24}} | collective-permute-start | bytes 2949128 | tf_op jit(solution)/shard_map/ppermute | solution.py:452
  128.4 37.3 %collective-permute-start.16 = (bf16[128,4096]{1,0:T(8,128)(2,1)S(1)}, bf16[128,4096]{1,0:T(8,128)(2,1)S(1)}, u32[]{:S(2)}, u32[]{:S(2)}) collective-permute-start(bf16[128,4096]{1,0:T(8,128)(2,1)S(1)} %collective-permute-done.12.refs_5_), channel_id=1, source_target_pairs={{0,4},{1,5},{2,6},{3,7},{4,0},{5,1},{6,2},{7,3},{8,12},{9,13},{10,... | collective-permute-start | bytes 3145736 | tf_op jit(solution)/shard_map/ppermute | solution.py:442
  128.4 37.3 %collective-permute-start.17 = (bf16[128,4096]{1,0:T(8,128)(2,1)S(1)}, bf16[128,4096]{1,0:T(8,128)(2,1)S(1)}, u32[]{:S(2)}, u32[]{:S(2)}) collective-permute-start(bf16[128,4096]{1,0:T(8,128)(2,1)S(1)} %collective-permute-done.12.refs_5_), channel_id=1, source_target_pairs={{0,8},{8,0},{16,24},{24,16},{1,9},{9,1},{17,25},{25,17},{2,10},{10... | collective-permute-start | bytes 3145736 | tf_op jit(solution)/shard_map/ppermute | solution.py:496
  128.6 37.1 %collective-permute-start.18 = (bf16[240,2048]{1,0:T(8,128)(2,1)}, bf16[240,2048]{1,0:T(8,128)(2,1)}, u32[]{:S(2)}, u32[]{:S(2)}) collective-permute-start(bf16[240,2048]{1,0:T(8,128)(2,1)} %get-tuple-element.242), channel_id=1, source_target_pairs={{1,2},{2,1},{3,4},{4,3},{5,6},{6,5},{9,10},{10,9},{11,12},{12,11},... | collective-permute-start | bytes 2949128 | tf_op jit(solution)/shard_map/ppermute | solution.py:448
  133.6 32.1 %collective-permute-start.19 = (bf16[240,2048]{1,0:T(8,128)(2,1)}, bf16[240,2048]{1,0:T(8,128)(2,1)}, u32[]{:S(2)}, u32[]{:S(2)}) collective-permute-start(bf16[240,2048]{1,0:T(8,128)(2,1)} %collective-permute-done.14), channel_id=1, source_target_pairs={{7,4},{0,3},{15,12},{8,11},{23,20},{16,19},{31,28},{24,27}} | collective-permute-start | bytes 2949128 | tf_op jit(solution)/shard_map/ppermute | solution.py:456
  136.2 29.5 %collective-permute-start.20 = (bf16[4,256,256]{2,1,0:T(8,128)(2,1)S(1)}, bf16[4,256,256]{2,1,0:T(8,128)(2,1)}, u32[]{:S(2)}, u32[]{:S(2)}) collective-permute-start(bf16[4,256,256]{2,1,0:T(8,128)(2,1)S(1)} %slice_bitcast_fusion.2), channel_id=1, source_target_pairs={{0,16},{8,24},{16,0},{24,8},{1,17},{9,25},{17,1},{25,9},{2,18},{10... | collective-permute-start | bytes 1572872 | tf_op jit(solution)/shard_map/ppermute | solution.py:461
  165.7 27.1 %collective-permute-start.21 = (bf16[128,4096]{1,0:T(8,128)(2,1)S(1)}, bf16[128,4096]{1,0:T(8,128)(2,1)S(1)}, u32[]{:S(2)}, u32[]{:S(2)}) collective-permute-start(bf16[128,4096]{1,0:T(8,128)(2,1)S(1)} %collective-permute-done.16.refs_8_), channel_id=1, source_target_pairs={{0,8},{8,0},{16,24},{24,16},{1,9},{9,1},{17,25},{25,17},{2,10},{10... | collective-permute-start | bytes 3145736 | tf_op jit(solution)/shard_map/ppermute | solution.py:496
  165.8 27.0 %collective-permute-start.23 = (bf16[2,4,256,256]{3,2,1,0:T(8,128)(2,1)}, bf16[2,4,256,256]{3,2,1,0:T(8,128)(2,1)S(1)}, u32[]{:S(2)}, u32[]{:S(2)}) collective-permute-start(bf16[2,4,256,256]{3,2,1,0:T(8,128)(2,1)} %get-tuple-element.268), channel_id=1, source_target_pairs={{0,4},{1,5},{2,6},{3,7},{4,0},{5,1},{6,2},{7,3},{8,12},{9,13},{10,... | collective-permute-start | bytes 3145736 | tf_op jit(solution)/shard_map/ppermute | solution.py:442
  167.5 25.3 %collective-permute-start.24 = (bf16[240,2048]{1,0:T(8,128)(2,1)}, bf16[240,2048]{1,0:T(8,128)(2,1)S(1)}, u32[]{:S(2)}, u32[]{:S(2)}) collective-permute-start(bf16[240,2048]{1,0:T(8,128)(2,1)} %collective-permute-done.15), channel_id=1, source_target_pairs={{7,4},{0,3},{15,12},{8,11},{23,20},{16,19},{31,28},{24,27}} | collective-permute-start | bytes 2949128 | tf_op jit(solution)/shard_map/ppermute | solution.py:456
  193.8 37.0 %collective-permute-start.26 = (bf16[2,4,256,256]{3,2,1,0:T(8,128)(2,1)}, bf16[2,4,256,256]{3,2,1,0:T(8,128)(2,1)}, u32[]{:S(2)}, u32[]{:S(2)}) collective-permute-start(bf16[2,4,256,256]{3,2,1,0:T(8,128)(2,1)} %get-tuple-element.283), channel_id=1, source_target_pairs={{0,4},{1,5},{2,6},{3,7},{4,0},{5,1},{6,2},{7,3},{8,12},{9,13},{10,... | collective-permute-start | bytes 3145736 | tf_op jit(solution)/shard_map/ppermute | solution.py:442
  193.8 36.0 %collective-permute-start.25 = (bf16[240,2048]{1,0:T(8,128)(2,1)}, bf16[240,2048]{1,0:T(8,128)(2,1)}, u32[]{:S(2)}, u32[]{:S(2)}) collective-permute-start(bf16[240,2048]{1,0:T(8,128)(2,1)} %get-tuple-element.278), channel_id=1, source_target_pairs={{1,2},{2,1},{3,4},{4,3},{5,6},{6,5},{9,10},{10,9},{11,12},{12,11},... | collective-permute-start | bytes 2949128 | tf_op jit(solution)/shard_map/ppermute | solution.py:448
  199.0 30.7 %collective-permute-start.27 = (bf16[4,256,256]{2,1,0:T(8,128)(2,1)}, bf16[4,256,256]{2,1,0:T(8,128)(2,1)}, u32[]{:S(2)}, u32[]{:S(2)}) collective-permute-start(bf16[4,256,256]{2,1,0:T(8,128)(2,1)} %fusion.5), channel_id=1, source_target_pairs={{0,2},{1,3},{2,0},{3,1},{4,6},{5,7},{6,4},{7,5},{8,10},{9,11},{10,... | collective-permute-start | bytes 1572872 | tf_op jit(solution)/shard_map/ppermute | solution.py:442
  200.2 29.6 %collective-permute-start.28 = (bf16[4,256,256]{2,1,0:T(8,128)(2,1)}, bf16[4,256,256]{2,1,0:T(8,128)(2,1)S(1)}, u32[]{:S(2)}, u32[]{:S(2)}) collective-permute-start(bf16[4,256,256]{2,1,0:T(8,128)(2,1)} %get-tuple-element.353), channel_id=1, source_target_pairs={{0,8},{8,16},{16,24},{24,0},{1,9},{9,17},{17,25},{25,1},{2,10},{10... | collective-permute-start | bytes 1572872 | tf_op jit(solution)/shard_map/ppermute | solution.py:461
  202.1 27.7 %collective-permute-start.29 = (bf16[4,256,256]{2,1,0:T(8,128)(2,1)}, bf16[4,256,256]{2,1,0:T(8,128)(2,1)S(1)}, u32[]{:S(2)}, u32[]{:S(2)}) collective-permute-start(bf16[4,256,256]{2,1,0:T(8,128)(2,1)} %get-tuple-element.352), channel_id=1, source_target_pairs={{0,24},{8,0},{16,8},{24,16},{1,25},{9,1},{17,9},{25,17},{2,26},{10... | collective-permute-start | bytes 1572872 | tf_op jit(solution)/shard_map/ppermute | solution.py:461
  230.8 34.4 %collective-permute-start.32 = (bf16[2,4,256,256]{3,2,1,0:T(8,128)(2,1)}, bf16[2,4,256,256]{3,2,1,0:T(8,128)(2,1)}, u32[]{:S(2)}, u32[]{:S(2)}) collective-permute-start(bf16[2,4,256,256]{3,2,1,0:T(8,128)(2,1)} %get-tuple-element.304), channel_id=1, source_target_pairs={{0,4},{1,5},{2,6},{3,7},{4,0},{5,1},{6,2},{7,3},{8,12},{9,13},{10,... | collective-permute-start | bytes 3145736 | tf_op jit(solution)/shard_map/ppermute | solution.py:442
  233.8 31.4 %collective-permute-start.31 = (bf16[240,2048]{1,0:T(8,128)(2,1)}, bf16[240,2048]{1,0:T(8,128)(2,1)}, u32[]{:S(2)}, u32[]{:S(2)}) collective-permute-start(bf16[240,2048]{1,0:T(8,128)(2,1)} %get-tuple-element.302), channel_id=1, source_target_pairs={{1,2},{2,1},{5,6},{6,5},{9,10},{10,9},{13,14},{14,13},{17,18},{18,... | collective-permute-start | bytes 2949128 | tf_op jit(solution)/shard_map/ppermute | solution.py:448
  237.5 27.8 %collective-permute-start.33 = (bf16[4,256,256]{2,1,0:T(8,128)(2,1)}, bf16[4,256,256]{2,1,0:T(8,128)(2,1)}, u32[]{:S(2)}, u32[]{:S(2)}) collective-permute-start(bf16[4,256,256]{2,1,0:T(8,128)(2,1)} %fusion.6), channel_id=1, source_target_pairs={{0,2},{1,3},{2,0},{3,1},{4,6},{5,7},{6,4},{7,5},{8,10},{9,11},{10,... | collective-permute-start | bytes 1572872 | tf_op jit(solution)/shard_map/ppermute | solution.py:442
  266.4 34.0 %collective-permute-start.38 = (bf16[4,256,256]{2,1,0:T(8,128)(2,1)S(1)}, bf16[4,256,256]{2,1,0:T(8,128)(2,1)}, u32[]{:S(2)}, u32[]{:S(2)}) collective-permute-start(bf16[4,256,256]{2,1,0:T(8,128)(2,1)S(1)} %fusion.7), channel_id=1, source_target_pairs={{0,2},{1,3},{2,0},{3,1},{4,6},{5,7},{6,4},{7,5},{8,10},{9,11},{10,... | collective-permute-start | bytes 1572872 | tf_op jit(solution)/shard_map/ppermute | solution.py:442
  270.3 29.9 %collective-permute-start.34 = (bf16[2,256,256]{2,1,0:T(8,128)(2,1)S(1)}, bf16[2,256,256]{2,1,0:T(8,128)(2,1)S(1)}, u32[]{:S(2)}, u32[]{:S(2)}) collective-permute-start(bf16[2,256,256]{2,1,0:T(8,128)(2,1)S(1)} %get-tuple-element.356), channel_id=1, source_target_pairs={{0,8},{8,16},{16,24},{24,0},{1,9},{9,17},{17,25},{25,1},{2,10},{10... | collective-permute-start | bytes 786440 | tf_op jit(solution)/shard_map/ppermute | solution.py:461
  271.8 28.4 %collective-permute-start.35 = (bf16[2,256,256]{2,1,0:T(8,128)(2,1)S(1)}, bf16[2,256,256]{2,1,0:T(8,128)(2,1)S(1)}, u32[]{:S(2)}, u32[]{:S(2)}) collective-permute-start(bf16[2,256,256]{2,1,0:T(8,128)(2,1)S(1)} %get-tuple-element.358), channel_id=1, source_target_pairs={{0,16},{8,24},{16,0},{24,8},{1,17},{9,25},{17,1},{25,9},{2,18},{10... | collective-permute-start | bytes 786440 | tf_op jit(solution)/shard_map/ppermute | solution.py:461
  274.1 26.1 %collective-permute-start.36 = (bf16[2,256,256]{2,1,0:T(8,128)(2,1)S(1)}, bf16[2,256,256]{2,1,0:T(8,128)(2,1)S(1)}, u32[]{:S(2)}, u32[]{:S(2)}) collective-permute-start(bf16[2,256,256]{2,1,0:T(8,128)(2,1)S(1)} %get-tuple-element.357), channel_id=1, source_target_pairs={{0,24},{8,0},{16,8},{24,16},{1,25},{9,1},{17,9},{25,17},{2,26},{10... | collective-permute-start | bytes 786440 | tf_op jit(solution)/shard_map/ppermute | solution.py:461
  275.7 24.8 %collective-permute-start.37 = (bf16[2,256,256]{2,1,0:T(8,128)(2,1)S(1)}, bf16[2,256,256]{2,1,0:T(8,128)(2,1)S(1)}, u32[]{:S(2)}, u32[]{:S(2)}) collective-permute-start(bf16[2,256,256]{2,1,0:T(8,128)(2,1)S(1)} %slice.208), channel_id=1, source_target_pairs={{0,4},{1,5},{2,6},{3,7},{4,0},{5,1},{6,2},{7,3},{8,12},{9,13},{10,... | collective-permute-start | bytes 786440 | tf_op jit(solution)/shard_map/ppermute | solution.py:442
  (40 other events, 508.2 us)

commit v4 on v3

--- a/solution.py
+++ b/solution.py
@@ -136,45 +136,48 @@
     live = old_end - old_start
     slot, width = ins[0].shape
     base = pl.multiple_of((jnp.clip(live - mv, 0, slot - mv - 8) // 8) * 8, 8)
-    copies = []
-    for i in range(count):
-        copies.append(pltpu.make_async_copy(ins[i].at[pl.ds(0, mv)], head.at[i], sems.at[i, 0]))
-        copies.append(
-            pltpu.make_async_copy(ins[i].at[pl.ds(base, mv + 8)], tail.at[i, pl.ds(mv + 8, mv + 8)], sems.at[i, 1])
-        )
-    for copy in copies:
-        copy.start()
     size = len(starts[0]) * count * block
     piece = piece_rows(mv, (48, 32, 16))
-    for i in range(count):
-        copies[2 * i].wait()
-        copies[2 * i + 1].wait()
-        for part, blocks in enumerate(starts):
-            for at, start in enumerate(blocks):
-                columns = slice(start, start + block)
-                place = (at * count + i) * block
-                for row in range(0, mv, piece):
-                    rows = slice(row, row + piece)
-                    first = head[i, rows, columns]
-                    last = shifted_rows(tail.at[i, :, columns], live + 8 - base + row, piece)
-                    outers[part][rows, place : place + block] = jnp.where(odd, last, first).astype(BF16)
-                    inner_place = place + part * size
-                    inner[rows, inner_place : inner_place + block] = jnp.where(odd, first, last).astype(BF16)
+    work = []
+    for part, blocks in enumerate(starts):
+        for at, start in enumerate(blocks):
+            for i in range(count):
+                k = len(work)
+                columns = pl.ds(start, block)
+                first = pltpu.make_async_copy(ins[i].at[pl.ds(0, mv), columns], head.at[k], sems.at[k, 0])
+                last = pltpu.make_async_copy(
+                    ins[i].at[pl.ds(base, mv + 8), columns], tail.at[k, pl.ds(mv + 8, mv + 8)], sems.at[k, 1]
+                )
+                work.append((first, last, part, (at * count + i) * block))
+    for first, last, _, _ in work:
+        first.start()
+        last.start()
+    for k, (first, last, part, place) in enumerate(work):
+        first.wait()
+        last.wait()
+        inner_place = place + part * size
+        for row in range(0, mv, piece):
+            rows = slice(row, row + piece)
+            top = head[k, rows, :]
+            end = shifted_rows(tail.at[k], live + 8 - base + row, piece)
+            outers[part][rows, place : place + block] = jnp.where(odd, end, top).astype(BF16)
+            inner[rows, inner_place : inner_place + block] = jnp.where(odd, top, end).astype(BF16)
 
 
 def edges(tab, arrays, n, mv, block, starts):
-    width = arrays[0].shape[1]
     count = len(arrays)
+    pieces = len(starts) * len(starts[0]) * count
+    width = pieces * block
     return pl.pallas_call(
         functools.partial(edges_kernel, n, mv, count, block, starts),
-        out_shape=[jax.ShapeDtypeStruct((mv, count * width), BF16)]
-        + [jax.ShapeDtypeStruct((mv, count * width // len(starts)), BF16)] * len(starts),
+        out_shape=[jax.ShapeDtypeStruct((mv, width), BF16)]
+        + [jax.ShapeDtypeStruct((mv, width // len(starts)), BF16)] * len(starts),
         in_specs=[SMEM] + [pl.BlockSpec(memory_space=pl.ANY)] * count,
         out_specs=[pl.BlockSpec(memory_space=pltpu.VMEM)] * (1 + len(starts)),
         scratch_shapes=[
-            pltpu.VMEM((count, mv, width), F32),
-            pltpu.VMEM((count, 2 * mv + 32, width), F32),
-            pltpu.SemaphoreType.DMA((count, 2)),
+            pltpu.VMEM((pieces, mv, block), F32),
+            pltpu.VMEM((pieces, 2 * mv + 32, block), F32),
+            pltpu.SemaphoreType.DMA((pieces, 2)),
         ],
         compiler_params=params(),
         cost_estimate=cost(),
@@ -215,7 +218,7 @@
             grid=(n_dp,),
             in_specs=[
                 pl.BlockSpec((slot, block), lambda s, tab: (0, 2 * group(s, tab) + half)),
-                pl.BlockSpec((mv, block), lambda s, tab: (0, half * n_dp + group(s, tab))),
+                pl.BlockSpec((mv, block), lambda s, tab: (0, group(s, tab))),
                 pl.BlockSpec((mv, block), lambda s, tab: (0, group(s, tab))),
             ],
             out_specs=pl.BlockSpec((2, rows, block // 2), lambda s, tab: (0, 0, s)),
@@ -304,13 +307,14 @@
 
 
 def fill_grads(parity, og_refs, places, og):
-    for ref, (at, flip, count, *more) in zip(og_refs, places):
-        rows = ref.shape[0]
+    refs = iter(og_refs)
+    for at, flip, half, more, filled, rows in places:
+        value = next(refs)[...] if filled else jnp.zeros((rows, og.shape[1]), og.dtype)
         if flip is None:
-            og[at : at + rows, :] = ref[...]
+            og[at : at + rows, :] = value
         else:
-            shift = (parity if flip == 0 else 1 - parity) * count + more[0]
-            og[pl.ds(pl.multiple_of(at + shift, rows), rows), :] = ref[...]
+            shift = (parity if flip == 0 else 1 - parity) * half + more
+            og[pl.ds(pl.multiple_of(at + shift, rows), rows), :] = value
 
 
 def partner_kernel(n, pieces, places, tab, *refs):
@@ -329,7 +333,7 @@
     width = grads[0].shape[1]
     block = min(width, 512)
     steps = width // block
-    total = sum(g.shape[0] for g in grads)
+    total = sum(place[5] for place in places)
     return pl.pallas_call(
         functools.partial(partner_kernel, n, len(pieces), places),
         out_shape=jax.ShapeDtypeStruct((rows, width), BF16),
@@ -344,9 +348,9 @@
     )(tab, *pieces, *grads)
 
 
-def adam_kernel(n, pieces, places, scale, aliased, relayed, tab, *refs):
+def adam_kernel(n, pieces, grads, places, scale, aliased, relayed, tab, *refs):
     ht_refs, refs = refs[:pieces], refs[pieces:]
-    og_refs, refs = refs[: len(places)], refs[len(places) :]
+    og_refs, refs = refs[:grads], refs[grads:]
     rest, own, (inner0, inner1, outer0, outer1, inner_both, outer_both) = refs[0], refs[1:4], refs[4:10]
     refs = refs[10:]
     relay, refs = refs[:relayed], refs[relayed + aliased :]
@@ -394,8 +398,8 @@
     mv = both[0].shape[0]
     block = width // (4 * n_dp)
     steps = width // parts // block
-    total = sum(g.shape[0] for g in grads)
-    inner, outers = edge
+    total = sum(place[5] for place in places)
+    inners, outers = edge
 
     def column(i):
         return 0, part * steps + i
@@ -403,15 +407,12 @@
     def first(i):
         return 0, (part * steps + i) // 4 * 2 + i % 2
 
-    def second(i):
-        return 0, 2 * n_dp + (part * steps + i) // 4 * 2 + i % 2
-
     def inner_both(i):
         return 0, part * steps + i
 
-    operands = [tab, *pieces, *grads, rest, *own, inner, inner, *outers, *both, *outs]
+    operands = [tab, *pieces, *grads, rest, *own, *inners, *outers, *both, *outs]
     return pl.pallas_call(
-        functools.partial(adam_kernel, n, len(pieces), places, scale, len(outs), len(both) - 2),
+        functools.partial(adam_kernel, n, len(pieces), len(grads), places, scale, len(outs), len(both) - 2),
         out_shape=[jax.ShapeDtypeStruct((slot, width), F32)] * 3,
         grid=(steps,),
         in_specs=[SMEM]
@@ -419,8 +420,7 @@
         + [pl.BlockSpec((g.shape[0], block), column) for g in grads]
         + [pl.BlockSpec((rows, block), column)]
         + [pl.BlockSpec((slot, block), column)] * 3
-        + [pl.BlockSpec((mv, block), first), pl.BlockSpec((mv, block), second)]
-        + [pl.BlockSpec((mv, block), first)] * 2
+        + [pl.BlockSpec((mv, block), first)] * 4
         + [pl.BlockSpec((mv, 2 * block), inner_both)]
         + [pl.BlockSpec((mv, 2 * block), lambda i: (0, i))] * (len(both) - 1)
         + [pl.BlockSpec(memory_space=pl.ANY)] * len(outs),
@@ -484,7 +484,6 @@
     own = [master_old[0], moment1_old[0], moment2_old[0]]
     half = tokens // 2
     parity = lax.rem(lax.axis_index("dp"), 2)
-    mine_grad = lax.dynamic_slice_in_dim(out_grad, parity * half, half, 0)
 
     block = width // (2 * n_dp)
     small = block // 2
@@ -527,18 +526,22 @@
     def step(part, outs):
         moved = (moving_inner, *moved_outer[part])
         return list(
-            adam_part(tab, pieces, grads, places, partner, own, (inner, outers), moved, outs, n, n_dp, scale, part, parts)
+            adam_part(tab, tokens_of, grads, places, partner, own, (inners, outers), moved, outs, n, n_dp, scale, part, parts)
         )
 
-    inner, *outers = edges(
-        tab, own[:1], n, mv, block, [[(2 * j + h) * block for j in range(n_dp)] for h in range(2)]
-    )
+    def master_edges(tab, h):
+        inner, outer = edges(tab, own[:1], n, mv, block, [[(2 * j + h) * block for j in range(n_dp)]])
+        return inner, outer
+
     quarter = half // 2
-    tab, inner, outers, mine_grad, quarters = stage(
-        tab, inner, outers, mine_grad, [mine_grad[:quarter], mine_grad[quarter:]]
-    )
-    outers = list(outers)
-    inner, outers[0] = swap(inner, 1), swap_outer(outers[0])
+    inner, outer = master_edges(tab, 0)
+    tab, inner, outer, out_grad = stage(tab, inner, outer, out_grad)
+    mine_grad = lax.dynamic_slice_in_dim(out_grad, parity * half, half, 0)
+    quarters = [lax.dynamic_slice_in_dim(out_grad, parity * half + at, quarter, 0) for at in (0, quarter)]
+    inners, outers = [swap(inner, 1)], [swap_outer(outer)]
+    inner, outer = master_edges(tab, 1)
+    inners.append(inner)
+    outers.append(outer)
     windows = list(hidden_windows(tab, gate, up, n, rows))
     moving = list(
         edges(
@@ -551,20 +554,21 @@
         )
     )
     grad_y = [swap(quarters[0], 4)] if square else []
-    tab, inner, outers, mine_grad, grad_y, windows, moving = stage(
-        tab, inner, outers, mine_grad, grad_y, windows, moving
-    )
-
-    outers, moving, grad_y = list(outers), list(moving), list(grad_y)
+    tab, inners, outers, mine_grad, quarters, grad_y, windows, moving = stage(
+        tab, inners, outers, mine_grad, quarters, grad_y, windows, moving
+    )
+
+    inners, outers, moving, grad_y = list(inners), list(outers), list(moving), list(grad_y)
     outers[1] = swap_outer(outers[1])
+    inners[1] = swap(inners[1], 1)
     flips_y = []
     if square:
         grad_y.append(swap(quarters[1], 4))
         flips_y.append(flip(grad_y[0]))
     moving_inner = swap(moving[0], 1)
-    mine = new_weights(tab, own[0], inner, outers[0], n, n_dp, rows, 0)
-    tab, outers, mine_grad, grad_y, flips_y, windows, moving, moving_inner, mine = stage(
-        tab, outers, mine_grad, grad_y, flips_y, windows, moving, moving_inner, mine
+    mine = new_weights(tab, own[0], inners[0], outers[0], n, n_dp, rows, 0)
+    tab, inners, outers, mine_grad, grad_y, flips_y, windows, moving, moving_inner, mine = stage(
+        tab, inners, outers, mine_grad, grad_y, flips_y, windows, moving, moving_inner, mine
     )
 
     pieces, flips_y = list(windows), list(flips_y)
@@ -573,7 +577,7 @@
     weights = [(mine, swap(mine, 1))]
     if square:
         flips_y.append(flip(grad_y[1]))
-    mine = new_weights(tab, own[0], inner, outers[1], n, n_dp, rows, 1)
+    mine = new_weights(tab, own[0], inners[1], outers[1], n, n_dp, rows, 1)
     tokens_first = [turned(pieces[0])]
     tab, mine_grad, flips_y, moving, pieces, weights, mine, tokens_first = stage(
         tab, mine_grad, flips_y, moving, pieces, weights, mine, tokens_first
@@ -614,37 +618,48 @@
     if square:
         relays[1] = relay_second(relays[1])
     flip_g = flip(grad_g) if square else grad_g
-    tab, flip_g, moving, moved_outer, sends, keeps, came, relays, last = stage(
-        tab, flip_g, moving, moved_outer, sends, keeps, came, relays, last
-    )
-
-    keeps, came, moved_outer = list(keeps), list(came), list(moved_outer)
-    if square:
-        grads = [out_grad, grad_x, *grad_y, grad_g, flip_x, *flips_y, flip_g]
-        places = [(0, None, tokens)]
+    tokens_of = pieces
+    if square:
+        grads = [out_grad, grad_x, *grad_y, grad_g, flip_x, *flips_y]
+        places = [(0, None, tokens, 0, True, tokens)]
         for which in range(2):
-            places += [(tokens, which, half, 0), (2 * tokens, which, half, 0), (2 * tokens, which, half, quarter)]
-            places += [(3 * tokens, which, half, 0)]
+            places += [(tokens, which, half, 0, True, half)]
+            places += [(2 * tokens, which, half, more, True, quarter) for more in (0, quarter)]
+            places += [(3 * tokens, which, half, 0, which == 0, half)]
+        tokens_of = pieces + [swap(pieces[3][1], 1)[None]]
     else:
         grads = [out_grad] + [swap(out_grad, 2 * rel) for rel in range(1, groups)]
-        places = [(i * tokens, None, tokens) for i in range(groups)]
+        places = [(i * tokens, None, tokens, 0, True, tokens) for i in range(groups)]
+    partner = partner_grad(tab, pieces, grads, places, n)
+    tab, flip_g, moving, moved_outer, sends, keeps, came, relays, tokens_of, partner = stage(
+        tab, flip_g, moving, moved_outer, sends, keeps, came, relays, tokens_of, partner
+    )
+
+    keeps, came, moved_outer = list(keeps), list(came), list(moved_outer)
     moved_outer.append((swap_outer(moving[3]),))
     came[2] = first_sum(2)
     totals[0] = second_sum(0)
-    turns = list(turns)
-    if square:
-        turns += [turn(last[i], i) for i in range(1, n_dp, 2)]
-    partner = partner_grad(tab, pieces, grads, places, n)
-    tab, moving, moved_outer, sends, came, totals, partner, turns, last = stage(
-        tab, moving, moved_outer, sends, came, totals, partner, turns, last
+    partner = swap(partner, 1)
+    if square:
+        partner, flip_core, tab = stage(partner, swap(flip_g, 1), tab)
+        grads = grads + [flip_g, flip_core]
+        places = places[:-1] + [(3 * tokens, 1, half, 0, True, half)]
+        places += [(4 * tokens, 0, half, 0, False, half), (4 * tokens, 1, half, 0, True, half)]
+    else:
+        partner, tab = stage(partner, tab)
+    outs = step(1, step(0, []))
+    tab, moving, moved_outer, sends, came, totals, outs, last = stage(
+        tab, moving, moved_outer, sends, came, totals, outs, last
     )
 
     came, totals, moved_outer = list(came), list(totals), list(moved_outer)
     moved_outer.append((swap_outer(moving[4], not square), *relays[1:]))
     came[3] = first_sum(3)
     totals[2] = second_sum(2)
-    partner, tab = stage(swap(partner, 1), tab)
-    outs = step(1, step(0, []))
+    turns = list(turns)
+    if square:
+        turns += [turn(last[i], i) for i in range(1, n_dp, 2)]
+    outs = step(2, list(outs))
     tab, moved_outer, sends, came, totals, outs, turns = stage(
         tab, moved_outer, sends, came, totals, outs, turns
     )
@@ -660,7 +675,7 @@
     else:
         came[1] = first_sum(1)
     both = over_dp(jnp.stack([summed(i, totals[i]) for i in (0, 2)], axis=1))
-    outs = step(3, step(2, list(outs)))
+    outs = step(3, list(outs))
     tab, came, totals, outs = stage(tab, came, totals, list(outs))
 
     totals = list(totals)

time: 322 us -> 315 us (0.978)
  waiting for transfers between devices: 111 us -> 97.9 us
    ppermute x2, waiting for transfers between devices: 24 us -> 10.4 us  [relay_second(): return lax.ppermute(value, 'fsdp', [(7, 4), (0, 3)])]
    ppermute x9, waiting for transfers between devices: 23.9 us -> 35.4 us  [turn(): return lax.ppermute(value, 'dp', [(i, (i + steps) % n) for i in range(n)])]
    ppermute x20 -> x23, waiting for transfers between devices: 58.9 us -> 47.9 us  [swap(): return lax.ppermute(value, 'fsdp', [(i, i ^ mask) for i in range(n)])]
    pallas_call x2 -> x3, Pallas kernels: 16.4 us -> 18.8 us  [edges(): pl.pallas_call(functools.partial(edges_kernel, n, mv, count, block, start...]
    unnamed x58 -> x50, local copies, waits for them, and re-layouts: 5.51 us -> 7.66 us
    ppermute x20 -> x23, starting transfers between devices: 15.8 us -> 15.8 us  [swap(): return lax.ppermute(value, 'fsdp', [(i, i ^ mask) for i in range(n)])]
  transfers between devices with their start and end apart: 43 -> 46, of which waited for: 12 -> 15; matrix products, arithmetic and copies ran while one was open for 3% -> 6% of each run, Pallas kernels for 38% -> 41%
where the time goes in v4:
time: 315 us; the launch traced here: 313 us
  Pallas kernels  132 us (42%)
  waiting for transfers between devices  97.9 us (31%)
  starting transfers between devices  52.2 us (17%)
  local copies, waits for them, and re-layouts  15.7 us (5%)
  other arithmetic  14.4 us (5%)
    pallas_call x4, Pallas kernels, adam_part(): pl.pallas_call(functools.partial(adam_kernel, n, len(pieces), len(grads),...  48 us
    ppermute x23, waiting for transfers between devices, swap(): return lax.ppermute(value, 'fsdp', [(i, i ^ mask) for i in range(n)])  47.9 us
    ppermute x9, waiting for transfers between devices, turn(): return lax.ppermute(value, 'dp', [(i, (i + steps) % n) for i in range(n)])  35.4 us
    pallas_call x4, Pallas kernels, forward_chunk(): pl.pallas_call(functools.partial(forward_kernel, sent), out_shape=[jax.Sh...  27.4 us
    pallas_call x3, Pallas kernels, edges(): pl.pallas_call(functools.partial(edges_kernel, n, mv, count, block, start...  18.8 us
    ppermute x6, starting transfers between devices, swap_outer(): lax.ppermute(value, 'fsdp', [(i, j) for i, j in pairs if middle or {i, j}...  16.5 us
    ppermute x23, starting transfers between devices, swap(): return lax.ppermute(value, 'fsdp', [(i, i ^ mask) for i in range(n)])  15.8 us
    pallas_call x2, Pallas kernels, new_weights(): pl.pallas_call(functools.partial(weights_kernel, n), out_shape=jax.ShapeD...  12.2 us
  transfers between devices with their start and end apart: 46, of which 15 were waited for; matrix products, arithmetic and copies ran while one was open for 6% of the time, Pallas kernels for 41%

profile of v4, /device:TPU:11, one launch (start us, length us, event | category | flops | bytes accessed | tf_op | source)
XLA Modules:
  0.0 313.4 jit_solution(1448075515907116746)
XLA Ops:
  1.9 4.3 %shard_map.120 = (bf16[240,2048]{1,0:T(8,128)(2,1)}, bf16[240,2048]{1,0:T(8,128)(2,1)}) custom-call(s32[27]{0:T(128)} %concatenate.6.tab, f32[624,4096]{1,0:T(8,128)} %bitcast.82), custom_call_target="tpu_custom_call" | custom-call | flops 1 | bytes 1 | tf_op jit(solution)/shard_map/pallas_call | solution.py:171
  10.9 4.2 %shard_map.121 = (bf16[240,2048]{1,0:T(8,128)(2,1)}, bf16[240,2048]{1,0:T(8,128)(2,1)}) custom-call(s32[27]{0:T(128)} %concatenate.6.tab, f32[624,4096]{1,0:T(8,128)} %bitcast.83), custom_call_target="tpu_custom_call" | custom-call | flops 1 | bytes 1 | tf_op jit(solution)/shard_map/pallas_call | solution.py:171
  15.1 10.3 %shard_map.123 = (bf16[240,8192]{1,0:T(8,128)(2,1)}, bf16[240,2048]{1,0:T(8,128)(2,1)}, bf16[240,2048]{1,0:T(8,128)(2,1)}, bf16[240,2048]{1,0:T(8,128)(2,1)}, bf16[240,2048]{1,0:T(8,128)(2,1)}) custom-call(s32[27]{0:T(128)} %concatenate.6.tab, f32[624,4096]{1,0:T(8,128)} %bitcast.90, f32[624,4096]{1,0:T(8,128)} %bitcast.95), custom_call_target="tpu_custom_call" | custom-call | flops 1 | bytes 1 | tf_op jit(solution)/shard_map/pallas_call | solution.py:171
  25.4 5.1 %shard_map.122 = (bf16[2,624,256]{2,1,0:T(8,128)(2,1)}, bf16[2,624,256]{2,1,0:T(8,128)(2,1)}, bf16[2,624,256]{2,1,0:T(8,128)(2,1)}, bf16[2,624,256]{2,1,0:T(8,128)(2,1)}) custom-call(s32[27]{0:T(128)} %concatenate.6.tab, bf16[256,3712]{1,0:T(8,128)(2,1)} %gate.1, bf16[256,3712]{1,0:T(8,128)(2,1)} %up.1), custom_call_target="tpu_custom_call" | custom-call | flops 1 | bytes 1 | tf_op jit(solution)/shard_map/pallas_call | solution.py:120
  31.5 3.8 %collective-permute-done.2.refs_6_.refs_7_ = bf16[64,4096]{1,0:T(8,128)(2,1)} collective-permute-done((bf16[64,4096]{1,0:T(8,128)(2,1)S(1)}, bf16[64,4096]{1,0:T(8,128)(2,1)}, u32[]{:S(2)}, u32[]{:S(2)}) %collective-permute-start.2) | collective-permute-done | bytes 524320 | tf_op jit(solution)/shard_map/ppermute | solution.py:442
  35.9 3.1 collective-permute-start.4
  39.3 6.1 %shard_map.124.refs_4_ = bf16[2,624,1024]{2,1,0:T(8,128)(2,1)} custom-call(s32[27]{0:T(128)} %concatenate.6.tab, f32[624,4096]{1,0:T(8,128)} %bitcast.84, bf16[240,2048]{1,0:T(8,128)(2,1)} %copy-done.8, bf16[240,2048]{1,0:T(8,128)(2,1)} %collective-permute-done.1.outer.refs_21_), custom_call_target="tpu_custom_call" | custom-call | flops 1 | bytes 1 | tf_op jit(solution)/shard_map/pallas_call | solution.py:213
  45.4 17.7 %collective-permute-done.5.refs_7_.refs_8_ = bf16[64,4096]{1,0:T(8,128)(2,1)S(1)} collective-permute-done((bf16[64,4096]{1,0:T(8,128)(2,1)}, bf16[64,4096]{1,0:T(8,128)(2,1)S(1)}, u32[]{:S(2)}, u32[]{:S(2)}) %collective-permute-start.5) | collective-permute-done | bytes 524320 | tf_op jit(solution)/shard_map/ppermute | solution.py:442
  69.3 6.1 %shard_map.125.refs_4_ = bf16[2,624,1024]{2,1,0:T(8,128)(2,1)} custom-call(s32[27]{0:T(128)} %concatenate.6.tab, f32[624,4096]{1,0:T(8,128)} %bitcast.85, bf16[240,2048]{1,0:T(8,128)(2,1)} %collective-permute-done.3.inner.refs_20_, bf16[240,2048]{1,0:T(8,128)(2,1)} %collective-permute-done.4.outer.refs_22_), custom_call_target="tpu_custom_call" | custom-call | flops 1 | bytes 1 | tf_op jit(solution)/shard_map/pallas_call | solution.py:213
  75.4 4.2 %collective-permute-done.8.refs_11_.refs_12_ = bf16[64,4096]{1,0:T(8,128)(2,1)S(1)} collective-permute-done((bf16[64,4096]{1,0:T(8,128)(2,1)}, bf16[64,4096]{1,0:T(8,128)(2,1)S(1)}, u32[]{:S(2)}, u32[]{:S(2)}) %collective-permute-start.8) | collective-permute-done | bytes 524320 | tf_op jit(solution)/shard_map/ppermute | solution.py:495
  79.6 14.6 %collective-permute-done.10.piece.refs_2_ = bf16[2,624,256]{2,1,0:T(8,128)(2,1)S(1)} collective-permute-done((bf16[2,624,256]{2,1,0:T(8,128)(2,1)}, bf16[2,624,256]{2,1,0:T(8,128)(2,1)S(1)}, u32[]{:S(2)}, u32[]{:S(2)}) %collective-permute-start.10) | collective-permute-done | bytes 639008 | tf_op jit(solution)/shard_map/ppermute | solution.py:442
  96.4 4.1 %collective-permute-start.15 = (bf16[240,2048]{1,0:T(8,128)(2,1)}, bf16[240,2048]{1,0:T(8,128)(2,1)}, u32[]{:S(2)}, u32[]{:S(2)}) collective-permute-start(bf16[240,2048]{1,0:T(8,128)(2,1)} %get-tuple-element.267), channel_id=1, source_target_pairs={{3,7},{4,0},{11,15},{12,8},{19,23},{20,16},{27,31},{28,24}} | collective-permute-start | bytes 2949128 | tf_op jit(solution)/shard_map/ppermute | solution.py:452
  109.7 6.8 %shard_map.131 = bf16[4,4,256,256]{3,2,1,0:T(8,128)(2,1)} custom-call(s32[27]{0:T(128)} %concatenate.6.tab, bf16[256,1248]{1,0:T(8,128)(2,1)} %shard_map.127.refs_0_, bf16[256,1248]{1,0:T(8,128)(2,1)} %shard_map.128.refs_1_, bf16[256,1248]{1,0:T(8,128)(2,1)} %shard_map.126.refs_2_, bf16[256,1248]{1,0:T(8,128)(2,1)} %shard_map.129.refs_3_, ...), custom_call_target="tpu_custom_call" | custom-call | flops 1 | bytes 1 | tf_op jit(solution)/shard_map/pallas_call | solution.py:286
  116.5 6.8 %shard_map.130 = (bf16[2,4,256,256]{3,2,1,0:T(8,128)(2,1)}, bf16[2,4,256,256]{3,2,1,0:T(8,128)(2,1)}) custom-call(s32[27]{0:T(128)} %concatenate.6.tab, bf16[256,1248]{1,0:T(8,128)(2,1)} %shard_map.127.refs_0_, bf16[256,1248]{1,0:T(8,128)(2,1)} %shard_map.128.refs_1_, bf16[256,1248]{1,0:T(8,128)(2,1)} %shard_map.126.refs_2_, ...), custom_call_target="tpu_custom_call" | custom-call | flops 1 | bytes 1 | tf_op jit(solution)/shard_map/pallas_call | solution.py:286
  124.9 4.8 %collective-permute-start.19 = (bf16[240,2048]{1,0:T(8,128)(2,1)}, bf16[240,2048]{1,0:T(8,128)(2,1)}, u32[]{:S(2)}, u32[]{:S(2)}) collective-permute-start(bf16[240,2048]{1,0:T(8,128)(2,1)} %get-tuple-element.246), channel_id=1, source_target_pairs={{1,2},{2,1},{3,4},{4,3},{5,6},{6,5},{9,10},{10,9},{11,12},{12,11},... | collective-permute-start | bytes 2949128 | tf_op jit(solution)/shard_map/ppermute | solution.py:448
  135.8 6.8 %shard_map.133 = (bf16[2,4,256,256]{3,2,1,0:T(8,128)(2,1)}, bf16[2,4,256,256]{3,2,1,0:T(8,128)(2,1)}) custom-call(s32[27]{0:T(128)} %concatenate.6.tab, bf16[256,1248]{1,0:T(8,128)(2,1)} %shard_map.127.refs_0_, bf16[256,1248]{1,0:T(8,128)(2,1)} %shard_map.128.refs_1_, bf16[256,1248]{1,0:T(8,128)(2,1)} %shard_map.126.refs_2_, ...), custom_call_target="tpu_custom_call" | custom-call | flops 1 | bytes 1 | tf_op jit(solution)/shard_map/pallas_call | solution.py:286
  142.6 6.9 %shard_map.132 = (bf16[2,4,256,256]{3,2,1,0:T(8,128)(2,1)}, bf16[2,4,256,256]{3,2,1,0:T(8,128)(2,1)}) custom-call(s32[27]{0:T(128)} %concatenate.6.tab, bf16[256,1248]{1,0:T(8,128)(2,1)} %shard_map.127.refs_0_, bf16[256,1248]{1,0:T(8,128)(2,1)} %shard_map.128.refs_1_, bf16[256,1248]{1,0:T(8,128)(2,1)} %shard_map.126.refs_2_, ...), custom_call_target="tpu_custom_call" | custom-call | flops 1 | bytes 1 | tf_op jit(solution)/shard_map/pallas_call | solution.py:286
  149.5 12.1 %collective-permute-done.21 = bf16[4,256,256]{2,1,0:T(8,128)(2,1)} collective-permute-done((bf16[4,256,256]{2,1,0:T(8,128)(2,1)}, bf16[4,256,256]{2,1,0:T(8,128)(2,1)}, u32[]{:S(2)}, u32[]{:S(2)}) %collective-permute-start.21) | collective-permute-done | bytes 524320 | tf_op jit(solution)/shard_map/ppermute | solution.py:461
  168.3 11.4 %shard_map.134 = bf16[624,4096]{1,0:T(8,128)(2,1)} custom-call(s32[27]{0:T(128)} %concatenate.6.tab, bf16[2,624,256]{2,1,0:T(8,128)(2,1)} %get-tuple-element.298.piece.refs_0_, bf16[2,624,256]{2,1,0:T(8,128)(2,1)} %collective-permute-done.9.piece.refs_1_, bf16[2,624,256]{2,1,0:T(8,128)(2,1)} %copy-done.9, bf16[2,624,256]{2,1,0:T(8,128)(2,1)} %copy-done.3, ...), custom_call_target="tpu_custom_call" | custom-call | flops 1 | bytes 1 | tf_op jit(solution)/shard_map/pallas_call | solution.py:337
  179.8 10.4 %collective-permute-done.25.refs_25_ = bf16[240,2048]{1,0:T(8,128)(2,1)} collective-permute-done((bf16[240,2048]{1,0:T(8,128)(2,1)}, bf16[240,2048]{1,0:T(8,128)(2,1)}, u32[]{:S(2)}, u32[]{:S(2)}) %collective-permute-start.25) | collective-permute-done | bytes 983072 | tf_op jit(solution)/shard_map/ppermute | solution.py:456
  191.7 3.2 %collective-permute-start.29 = (bf16[240,2048]{1,0:T(8,128)(2,1)}, bf16[240,2048]{1,0:T(8,128)(2,1)}, u32[]{:S(2)}, u32[]{:S(2)}) collective-permute-start(bf16[240,2048]{1,0:T(8,128)(2,1)} %get-tuple-element.290), channel_id=1, source_target_pairs={{1,2},{2,1},{3,4},{4,3},{5,6},{6,5},{9,10},{10,9},{11,12},{12,11},... | collective-permute-start | bytes 2949128 | tf_op jit(solution)/shard_map/ppermute | solution.py:448
  197.1 4.3 %collective-permute-done.28.refs_14_ = bf16[128,4096]{1,0:T(8,128)(2,1)S(1)} collective-permute-done((bf16[128,4096]{1,0:T(8,128)(2,1)}, bf16[128,4096]{1,0:T(8,128)(2,1)S(1)}, u32[]{:S(2)}, u32[]{:S(2)}) %collective-permute-start.28) | collective-permute-done | bytes 1048608 | tf_op jit(solution)/shard_map/ppermute | solution.py:442
  204.7 11.8 %shard_map.135 = (f32[624,4096]{1,0:T(8,128)}, f32[624,4096]{1,0:T(8,128)}, f32[624,4096]{1,0:T(8,128)}) custom-call(s32[27]{0:T(128)} %concatenate.6.tab, bf16[2,624,256]{2,1,0:T(8,128)(2,1)} %get-tuple-element.298.piece.refs_0_, bf16[2,624,256]{2,1,0:T(8,128)(2,1)} %collective-permute-done.9.piece.refs_1_, bf16[2,624,256]{2,1,0:T(8,128)(2,1)} %copy-done.9, ...), custom_call_target="tpu_custom_call" | custom-call | flops 1 | bytes 1 | tf_op jit(solution)/shard_map/pallas_call | solution.py:414
  216.5 12.3 %shard_map.136 = (f32[624,4096]{1,0:T(8,128)}, f32[624,4096]{1,0:T(8,128)}, f32[624,4096]{1,0:T(8,128)}) custom-call(s32[27]{0:T(128)} %concatenate.6.tab, bf16[2,624,256]{2,1,0:T(8,128)(2,1)} %get-tuple-element.298.piece.refs_0_, ...), custom_call_target="tpu_custom_call", output_to_operand_aliasing={{0}: (27, {}), {1}: (28, {}), {2}: (29, {})} | custom-call | flops 1 | bytes 1 | tf_op jit(solution)/shard_map/pallas_call | solution.py:414
  233.1 3.3 %collective-permute-start.34 = (bf16[4,256,256]{2,1,0:T(8,128)(2,1)}, bf16[4,256,256]{2,1,0:T(8,128)(2,1)}, u32[]{:S(2)}, u32[]{:S(2)}) collective-permute-start(bf16[4,256,256]{2,1,0:T(8,128)(2,1)} %fusion.6), channel_id=1, source_target_pairs={{0,2},{1,3},{2,0},{3,1},{4,6},{5,7},{6,4},{7,5},{8,10},{9,11},{10,... | collective-permute-start | bytes 1572872 | tf_op jit(solution)/shard_map/ppermute | solution.py:442
  239.4 11.8 %shard_map.137 = (f32[624,4096]{1,0:T(8,128)}, f32[624,4096]{1,0:T(8,128)}, f32[624,4096]{1,0:T(8,128)}) custom-call(s32[27]{0:T(128)} %concatenate.6.tab, bf16[2,624,256]{2,1,0:T(8,128)(2,1)} %get-tuple-element.298.piece.refs_0_, ...), custom_call_target="tpu_custom_call", output_to_operand_aliasing={{0}: (26, {}), {1}: (27, {}), {2}: (28, {})} | custom-call | flops 1 | bytes 1 | tf_op jit(solution)/shard_map/pallas_call | solution.py:414
  251.1 6.6 %collective-permute-done.34 = bf16[4,256,256]{2,1,0:T(8,128)(2,1)} collective-permute-done((bf16[4,256,256]{2,1,0:T(8,128)(2,1)}, bf16[4,256,256]{2,1,0:T(8,128)(2,1)}, u32[]{:S(2)}, u32[]{:S(2)}) %collective-permute-start.34) | collective-permute-done | bytes 524320 | tf_op jit(solution)/shard_map/ppermute | solution.py:442
  257.8 5.2 %collective-permute-done.36 = bf16[4,256,256]{2,1,0:T(8,128)(2,1)} collective-permute-done((bf16[4,256,256]{2,1,0:T(8,128)(2,1)}, bf16[4,256,256]{2,1,0:T(8,128)(2,1)}, u32[]{:S(2)}, u32[]{:S(2)}) %collective-permute-start.36) | collective-permute-done | bytes 524320 | tf_op jit(solution)/shard_map/ppermute | solution.py:461
  273.0 12.1 %shard_map.138 = (f32[624,4096]{1,0:T(8,128)}, f32[624,4096]{1,0:T(8,128)}, f32[624,4096]{1,0:T(8,128)}) custom-call(s32[27]{0:T(128)} %concatenate.6.tab, bf16[2,624,256]{2,1,0:T(8,128)(2,1)} %get-tuple-element.298.piece.refs_0_, ...), custom_call_target="tpu_custom_call", output_to_operand_aliasing={{0}: (27, {}), {1}: (28, {}), {2}: (29, {})} | custom-call | flops 1 | bytes 1 | tf_op jit(solution)/shard_map/pallas_call | solution.py:414
  285.1 5.3 %collective-permute-done.38 = bf16[2,256,256]{2,1,0:T(8,128)(2,1)} collective-permute-done((bf16[2,256,256]{2,1,0:T(8,128)(2,1)}, bf16[2,256,256]{2,1,0:T(8,128)(2,1)}, u32[]{:S(2)}, u32[]{:S(2)}) %collective-permute-start.38) | collective-permute-done | bytes 262176 | tf_op jit(solution)/shard_map/ppermute | solution.py:461
  302.5 6.6 %collective-permute-done.44 = bf16[256,256]{1,0:T(8,128)(2,1)S(1)} collective-permute-done((bf16[256,256]{1,0:T(8,128)(2,1)S(1)}, bf16[256,256]{1,0:T(8,128)(2,1)S(1)}, u32[]{:S(2)}, u32[]{:S(2)}) %collective-permute-start.44) | collective-permute-done | bytes 131104 | tf_op jit(solution)/shard_map/ppermute | solution.py:461
  309.1 3.1 %collective-permute-done.45 = bf16[256,256]{1,0:T(8,128)(2,1)S(1)} collective-permute-done((bf16[256,256]{1,0:T(8,128)(2,1)S(1)}, bf16[256,256]{1,0:T(8,128)(2,1)S(1)}, u32[]{:S(2)}, u32[]{:S(2)}) %collective-permute-start.45) | collective-permute-done | bytes 131104 | tf_op jit(solution)/shard_map/ppermute | solution.py:461
  (151 shorter events, 77.1 us)
Async XLA Ops:
  6.3 29.0 %collective-permute-start = (bf16[240,2048]{1,0:T(8,128)(2,1)}, bf16[240,2048]{1,0:T(8,128)(2,1)S(1)}, u32[]{:S(2)}, u32[]{:S(2)}) collective-permute-start(bf16[240,2048]{1,0:T(8,128)(2,1)} %get-tuple-element.183), channel_id=1, source_target_pairs={{0,1},{1,0},{2,3},{3,2},{4,5},{5,4},{6,7},{7,6},{8,9},{9,8},{10,11... | collective-permute-start | bytes 2949128 | tf_op jit(solution)/shard_map/ppermute | solution.py:442
  7.0 28.3 %collective-permute-start.1 = (bf16[240,2048]{1,0:T(8,128)(2,1)}, bf16[240,2048]{1,0:T(8,128)(2,1)}, u32[]{:S(2)}, u32[]{:S(2)}) collective-permute-start(bf16[240,2048]{1,0:T(8,128)(2,1)} %get-tuple-element.185), channel_id=1, source_target_pairs={{1,2},{2,1},{3,4},{4,3},{5,6},{6,5},{9,10},{10,9},{11,12},{12,11},... | collective-permute-start | bytes 2949128 | tf_op jit(solution)/shard_map/ppermute | solution.py:448
  10.9 24.4 %collective-permute-start.2 = (bf16[64,4096]{1,0:T(8,128)(2,1)S(1)}, bf16[64,4096]{1,0:T(8,128)(2,1)}, u32[]{:S(2)}, u32[]{:S(2)}) collective-permute-start(bf16[64,4096]{1,0:T(8,128)(2,1)S(1)} %get-tuple-element.361), channel_id=1, source_target_pairs={{0,4},{1,5},{2,6},{3,7},{4,0},{5,1},{6,2},{7,3},{8,12},{9,13},{10,... | collective-permute-start | bytes 1572872 | tf_op jit(solution)/shard_map/ppermute | solution.py:442
  35.3 27.8 %collective-permute-start.7 = (bf16[240,8192]{1,0:T(8,128)(2,1)}, bf16[240,8192]{1,0:T(8,128)(2,1)S(1)}, u32[]{:S(2)}, u32[]{:S(2)}) collective-permute-start(bf16[240,8192]{1,0:T(8,128)(2,1)} %get-tuple-element.209), channel_id=1, source_target_pairs={{0,1},{1,0},{2,3},{3,2},{4,5},{5,4},{6,7},{7,6},{8,9},{9,8},{10,11... | collective-permute-start | bytes 11796488 | tf_op jit(solution)/shard_map/ppermute | solution.py:442
  35.8 27.4 %collective-permute-start.3 = (bf16[240,2048]{1,0:T(8,128)(2,1)}, bf16[240,2048]{1,0:T(8,128)(2,1)}, u32[]{:S(2)}, u32[]{:S(2)}) collective-permute-start(bf16[240,2048]{1,0:T(8,128)(2,1)} %get-tuple-element.199), channel_id=1, source_target_pairs={{0,1},{1,0},{2,3},{3,2},{4,5},{5,4},{6,7},{7,6},{8,9},{9,8},{10,11... | collective-permute-start | bytes 2949128 | tf_op jit(solution)/shard_map/ppermute | solution.py:442
  35.9 27.2 %collective-permute-start.4 = (bf16[240,2048]{1,0:T(8,128)(2,1)}, bf16[240,2048]{1,0:T(8,128)(2,1)}, u32[]{:S(2)}, u32[]{:S(2)}) collective-permute-start(bf16[240,2048]{1,0:T(8,128)(2,1)} %get-tuple-element.201), channel_id=1, source_target_pairs={{1,2},{2,1},{3,4},{4,3},{5,6},{6,5},{9,10},{10,9},{11,12},{12,11},... | collective-permute-start | bytes 2949128 | tf_op jit(solution)/shard_map/ppermute | solution.py:448
  39.0 24.1 %collective-permute-start.5 = (bf16[64,4096]{1,0:T(8,128)(2,1)}, bf16[64,4096]{1,0:T(8,128)(2,1)S(1)}, u32[]{:S(2)}, u32[]{:S(2)}) collective-permute-start(bf16[64,4096]{1,0:T(8,128)(2,1)} %get-tuple-element.204), channel_id=1, source_target_pairs={{0,4},{1,5},{2,6},{3,7},{4,0},{5,1},{6,2},{7,3},{8,12},{9,13},{10,... | collective-permute-start | bytes 1572872 | tf_op jit(solution)/shard_map/ppermute | solution.py:442
  39.1 24.1 %collective-permute-start.6 = (bf16[64,4096]{1,0:T(8,128)(2,1)}, bf16[64,4096]{1,0:T(8,128)(2,1)}, u32[]{:S(2)}, u32[]{:S(2)}) collective-permute-start(bf16[64,4096]{1,0:T(8,128)(2,1)} %collective-permute-done.2.refs_6_.refs_7_), channel_id=1, source_target_pairs={{0,8},{8,0},{16,24},{24,16},{1,9},{9,1},{17,25},{25,17},{2,10},{10... | collective-permute-start | bytes 1572872 | tf_op jit(solution)/shard_map/ppermute | solution.py:495
  64.0 31.1 %collective-permute-start.12 = (bf16[2,624,1024]{2,1,0:T(8,128)(2,1)}, bf16[2,624,1024]{2,1,0:T(8,128)(2,1)}, u32[]{:S(2)}, u32[]{:S(2)}) collective-permute-start(bf16[2,624,1024]{2,1,0:T(8,128)(2,1)} %shard_map.124.refs_4_), channel_id=1, source_target_pairs={{0,1},{1,0},{2,3},{3,2},{4,5},{5,4},{6,7},{7,6},{8,9},{9,8},{10,11... | collective-permute-start | bytes 7667720 | tf_op jit(solution)/shard_map/ppermute | solution.py:442
  64.3 29.8 %collective-permute-start.10 = (bf16[2,624,256]{2,1,0:T(8,128)(2,1)}, bf16[2,624,256]{2,1,0:T(8,128)(2,1)S(1)}, u32[]{:S(2)}, u32[]{:S(2)}) collective-permute-start(bf16[2,624,256]{2,1,0:T(8,128)(2,1)} %get-tuple-element.224), channel_id=1, source_target_pairs={{0,4},{1,5},{2,6},{3,7},{4,0},{5,1},{6,2},{7,3},{8,12},{9,13},{10,... | collective-permute-start | bytes 1916936 | tf_op jit(solution)/shard_map/ppermute | solution.py:442
  64.3 29.8 %collective-permute-start.11 = (bf16[2,624,256]{2,1,0:T(8,128)(2,1)}, bf16[2,624,256]{2,1,0:T(8,128)(2,1)S(1)}, u32[]{:S(2)}, u32[]{:S(2)}) collective-permute-start(bf16[2,624,256]{2,1,0:T(8,128)(2,1)} %get-tuple-element.225), channel_id=1, source_target_pairs={{0,6},{1,7},{2,4},{3,5},{4,2},{5,3},{6,0},{7,1},{8,14},{9,15},{10,... | collective-permute-start | bytes 1916936 | tf_op jit(solution)/shard_map/ppermute | solution.py:442
  65.3 29.8 %collective-permute-start.9 = (bf16[2,624,256]{2,1,0:T(8,128)(2,1)}, bf16[2,624,256]{2,1,0:T(8,128)(2,1)}, u32[]{:S(2)}, u32[]{:S(2)}) collective-permute-start(bf16[2,624,256]{2,1,0:T(8,128)(2,1)} %get-tuple-element.223), channel_id=1, source_target_pairs={{0,2},{1,3},{2,0},{3,1},{4,6},{5,7},{6,4},{7,5},{8,10},{9,11},{10,... | collective-permute-start | bytes 1916936 | tf_op jit(solution)/shard_map/ppermute | solution.py:442
  95.1 28.3 %collective-permute-start.14 = (bf16[2,624,1024]{2,1,0:T(8,128)(2,1)}, bf16[2,624,1024]{2,1,0:T(8,128)(2,1)S(1)}, u32[]{:S(2)}, u32[]{:S(2)}) collective-permute-start(bf16[2,624,1024]{2,1,0:T(8,128)(2,1)} %shard_map.125.refs_4_), channel_id=1, source_target_pairs={{0,1},{1,0},{2,3},{3,2},{4,5},{5,4},{6,7},{7,6},{8,9},{9,8},{10,11... | collective-permute-start | bytes 7667720 | tf_op jit(solution)/shard_map/ppermute | solution.py:442
  96.3 27.0 %collective-permute-start.13 = (bf16[128,4096]{1,0:T(8,128)(2,1)}, bf16[128,4096]{1,0:T(8,128)(2,1)S(1)}, u32[]{:S(2)}, u32[]{:S(2)}) collective-permute-start(bf16[128,4096]{1,0:T(8,128)(2,1)} %constant_dynamic-slice_fusion.2), channel_id=1, source_target_pairs={{0,2},{1,3},{2,0},{3,1},{4,6},{5,7},{6,4},{7,5},{8,10},{9,11},{10,... | collective-permute-start | bytes 3145736 | tf_op jit(solution)/shard_map/ppermute | solution.py:442
  96.4 27.0 %collective-permute-start.15 = (bf16[240,2048]{1,0:T(8,128)(2,1)}, bf16[240,2048]{1,0:T(8,128)(2,1)}, u32[]{:S(2)}, u32[]{:S(2)}) collective-permute-start(bf16[240,2048]{1,0:T(8,128)(2,1)} %get-tuple-element.267), channel_id=1, source_target_pairs={{3,7},{4,0},{11,15},{12,8},{19,23},{20,16},{27,31},{28,24}} | collective-permute-start | bytes 2949128 | tf_op jit(solution)/shard_map/ppermute | solution.py:452
  100.4 22.9 %collective-permute-start.16 = (bf16[240,2048]{1,0:T(8,128)(2,1)}, bf16[240,2048]{1,0:T(8,128)(2,1)}, u32[]{:S(2)}, u32[]{:S(2)}) collective-permute-start(bf16[240,2048]{1,0:T(8,128)(2,1)} %get-tuple-element.317), channel_id=1, source_target_pairs={{3,7},{4,0},{11,15},{12,8},{19,23},{20,16},{27,31},{28,24}} | collective-permute-start | bytes 2949128 | tf_op jit(solution)/shard_map/ppermute | solution.py:452
  124.9 36.7 %collective-permute-start.17 = (bf16[128,4096]{1,0:T(8,128)(2,1)S(1)}, bf16[128,4096]{1,0:T(8,128)(2,1)S(1)}, u32[]{:S(2)}, u32[]{:S(2)}) collective-permute-start(bf16[128,4096]{1,0:T(8,128)(2,1)S(1)} %collective-permute-done.13.refs_5_.refs_6_), channel_id=1, source_target_pairs={{0,4},{1,5},{2,6},{3,7},{4,0},{5,1},{6,2},{7,3},{8,12},{9,13},{10,... | collective-permute-start | bytes 3145736 | tf_op jit(solution)/shard_map/ppermute | solution.py:442
  124.9 36.8 %collective-permute-start.18 = (bf16[128,4096]{1,0:T(8,128)(2,1)S(1)}, bf16[128,4096]{1,0:T(8,128)(2,1)S(1)}, u32[]{:S(2)}, u32[]{:S(2)}) collective-permute-start(bf16[128,4096]{1,0:T(8,128)(2,1)S(1)} %collective-permute-done.13.refs_5_.refs_6_), channel_id=1, source_target_pairs={{0,8},{8,0},{16,24},{24,16},{1,9},{9,1},{17,25},{25,17},{2,10},{10... | collective-permute-start | bytes 3145736 | tf_op jit(solution)/shard_map/ppermute | solution.py:495
  124.9 36.7 %collective-permute-start.19 = (bf16[240,2048]{1,0:T(8,128)(2,1)}, bf16[240,2048]{1,0:T(8,128)(2,1)}, u32[]{:S(2)}, u32[]{:S(2)}) collective-permute-start(bf16[240,2048]{1,0:T(8,128)(2,1)} %get-tuple-element.246), channel_id=1, source_target_pairs={{1,2},{2,1},{3,4},{4,3},{5,6},{6,5},{9,10},{10,9},{11,12},{12,11},... | collective-permute-start | bytes 2949128 | tf_op jit(solution)/shard_map/ppermute | solution.py:448
  129.7 31.9 %collective-permute-start.20 = (bf16[240,2048]{1,0:T(8,128)(2,1)}, bf16[240,2048]{1,0:T(8,128)(2,1)S(1)}, u32[]{:S(2)}, u32[]{:S(2)}) collective-permute-start(bf16[240,2048]{1,0:T(8,128)(2,1)} %collective-permute-done.15), channel_id=1, source_target_pairs={{7,4},{0,3},{15,12},{8,11},{23,20},{16,19},{31,28},{24,27}} | collective-permute-start | bytes 2949128 | tf_op jit(solution)/shard_map/ppermute | solution.py:456
  133.1 28.6 %collective-permute-start.21 = (bf16[4,256,256]{2,1,0:T(8,128)(2,1)}, bf16[4,256,256]{2,1,0:T(8,128)(2,1)}, u32[]{:S(2)}, u32[]{:S(2)}) collective-permute-start(bf16[4,256,256]{2,1,0:T(8,128)(2,1)} %slice_bitcast_fusion.2), channel_id=1, source_target_pairs={{0,16},{8,24},{16,0},{24,8},{1,17},{9,25},{17,1},{25,9},{2,18},{10... | collective-permute-start | bytes 1572872 | tf_op jit(solution)/shard_map/ppermute | solution.py:461
  162.6 27.6 %collective-permute-start.22 = (bf16[128,4096]{1,0:T(8,128)(2,1)S(1)}, bf16[128,4096]{1,0:T(8,128)(2,1)}, u32[]{:S(2)}, u32[]{:S(2)}) collective-permute-start(bf16[128,4096]{1,0:T(8,128)(2,1)S(1)} %collective-permute-done.17.refs_8_.refs_9_), channel_id=1, source_target_pairs={{0,8},{8,0},{16,24},{24,16},{1,9},{9,1},{17,25},{25,17},{2,10},{10... | collective-permute-start | bytes 3145736 | tf_op jit(solution)/shard_map/ppermute | solution.py:495
  162.6 27.6 %collective-permute-start.24 = (bf16[2,4,256,256]{3,2,1,0:T(8,128)(2,1)}, bf16[2,4,256,256]{3,2,1,0:T(8,128)(2,1)S(1)}, u32[]{:S(2)}, u32[]{:S(2)}) collective-permute-start(bf16[2,4,256,256]{3,2,1,0:T(8,128)(2,1)} %get-tuple-element.272), channel_id=1, source_target_pairs={{0,4},{1,5},{2,6},{3,7},{4,0},{5,1},{6,2},{7,3},{8,12},{9,13},{10,... | collective-permute-start | bytes 3145736 | tf_op jit(solution)/shard_map/ppermute | solution.py:442
  165.7 24.4 %collective-permute-start.25 = (bf16[240,2048]{1,0:T(8,128)(2,1)}, bf16[240,2048]{1,0:T(8,128)(2,1)}, u32[]{:S(2)}, u32[]{:S(2)}) collective-permute-start(bf16[240,2048]{1,0:T(8,128)(2,1)} %collective-permute-done.16), channel_id=1, source_target_pairs={{7,4},{0,3},{15,12},{8,11},{23,20},{16,19},{31,28},{24,27}} | collective-permute-start | bytes 2949128 | tf_op jit(solution)/shard_map/ppermute | solution.py:456
  191.7 37.1 %collective-permute-start.30 = (bf16[2,4,256,256]{3,2,1,0:T(8,128)(2,1)}, bf16[2,4,256,256]{3,2,1,0:T(8,128)(2,1)}, u32[]{:S(2)}, u32[]{:S(2)}) collective-permute-start(bf16[2,4,256,256]{3,2,1,0:T(8,128)(2,1)} %get-tuple-element.295), channel_id=1, source_target_pairs={{0,4},{1,5},{2,6},{3,7},{4,0},{5,1},{6,2},{7,3},{8,12},{9,13},{10,... | collective-permute-start | bytes 3145736 | tf_op jit(solution)/shard_map/ppermute | solution.py:442
  191.7 37.1 %collective-permute-start.29 = (bf16[240,2048]{1,0:T(8,128)(2,1)}, bf16[240,2048]{1,0:T(8,128)(2,1)}, u32[]{:S(2)}, u32[]{:S(2)}) collective-permute-start(bf16[240,2048]{1,0:T(8,128)(2,1)} %get-tuple-element.290), channel_id=1, source_target_pairs={{1,2},{2,1},{3,4},{4,3},{5,6},{6,5},{9,10},{10,9},{11,12},{12,11},... | collective-permute-start | bytes 2949128 | tf_op jit(solution)/shard_map/ppermute | solution.py:448
  197.0 31.8 %collective-permute-start.31 = (bf16[4,256,256]{2,1,0:T(8,128)(2,1)}, bf16[4,256,256]{2,1,0:T(8,128)(2,1)}, u32[]{:S(2)}, u32[]{:S(2)}) collective-permute-start(bf16[4,256,256]{2,1,0:T(8,128)(2,1)} %fusion.5), channel_id=1, source_target_pairs={{0,2},{1,3},{2,0},{3,1},{4,6},{5,7},{6,4},{7,5},{8,10},{9,11},{10,... | collective-permute-start | bytes 1572872 | tf_op jit(solution)/shard_map/ppermute | solution.py:442
  228.8 34.1 %collective-permute-start.33 = (bf16[2,4,256,256]{3,2,1,0:T(8,128)(2,1)}, bf16[2,4,256,256]{3,2,1,0:T(8,128)(2,1)S(1)}, u32[]{:S(2)}, u32[]{:S(2)}) collective-permute-start(bf16[2,4,256,256]{3,2,1,0:T(8,128)(2,1)} %get-tuple-element.319), channel_id=1, source_target_pairs={{0,4},{1,5},{2,6},{3,7},{4,0},{5,1},{6,2},{7,3},{8,12},{9,13},{10,... | collective-permute-start | bytes 3145736 | tf_op jit(solution)/shard_map/ppermute | solution.py:442
  230.4 32.5 %collective-permute-start.32 = (bf16[240,2048]{1,0:T(8,128)(2,1)}, bf16[240,2048]{1,0:T(8,128)(2,1)S(1)}, u32[]{:S(2)}, u32[]{:S(2)}) collective-permute-start(bf16[240,2048]{1,0:T(8,128)(2,1)} %get-tuple-element.317), channel_id=1, source_target_pairs={{1,2},{2,1},{5,6},{6,5},{9,10},{10,9},{13,14},{14,13},{17,18},{18,... | collective-permute-start | bytes 2949128 | tf_op jit(solution)/shard_map/ppermute | solution.py:448
  233.1 24.7 %collective-permute-start.34 = (bf16[4,256,256]{2,1,0:T(8,128)(2,1)}, bf16[4,256,256]{2,1,0:T(8,128)(2,1)}, u32[]{:S(2)}, u32[]{:S(2)}) collective-permute-start(bf16[4,256,256]{2,1,0:T(8,128)(2,1)} %fusion.6), channel_id=1, source_target_pairs={{0,2},{1,3},{2,0},{3,1},{4,6},{5,7},{6,4},{7,5},{8,10},{9,11},{10,... | collective-permute-start | bytes 1572872 | tf_op jit(solution)/shard_map/ppermute | solution.py:442
  238.3 24.6 %collective-permute-start.36 = (bf16[4,256,256]{2,1,0:T(8,128)(2,1)}, bf16[4,256,256]{2,1,0:T(8,128)(2,1)}, u32[]{:S(2)}, u32[]{:S(2)}) collective-permute-start(bf16[4,256,256]{2,1,0:T(8,128)(2,1)} %get-tuple-element.358), channel_id=1, source_target_pairs={{0,24},{8,0},{16,8},{24,16},{1,25},{9,1},{17,9},{25,17},{2,26},{10... | collective-permute-start | bytes 1572872 | tf_op jit(solution)/shard_map/ppermute | solution.py:461
  264.1 30.5 %collective-permute-start.41 = (bf16[4,256,256]{2,1,0:T(8,128)(2,1)}, bf16[4,256,256]{2,1,0:T(8,128)(2,1)}, u32[]{:S(2)}, u32[]{:S(2)}) collective-permute-start(bf16[4,256,256]{2,1,0:T(8,128)(2,1)} %fusion.7), channel_id=1, source_target_pairs={{0,2},{1,3},{2,0},{3,1},{4,6},{5,7},{6,4},{7,5},{8,10},{9,11},{10,... | collective-permute-start | bytes 1572872 | tf_op jit(solution)/shard_map/ppermute | solution.py:442
  (39 other events, 513.2 us)

commit v5 on v4

--- a/solution.py
+++ b/solution.py
@@ -631,8 +631,9 @@
         grads = [out_grad] + [swap(out_grad, 2 * rel) for rel in range(1, groups)]
         places = [(i * tokens, None, tokens, 0, True, tokens) for i in range(groups)]
     partner = partner_grad(tab, pieces, grads, places, n)
-    tab, flip_g, moving, moved_outer, sends, keeps, came, relays, tokens_of, partner = stage(
-        tab, flip_g, moving, moved_outer, sends, keeps, came, relays, tokens_of, partner
+    odd_turns = [last[i] for i in range(1, n_dp, 2)] if square else []
+    tab, flip_g, moving, moved_outer, sends, keeps, came, relays, tokens_of, partner, odd_turns = stage(
+        tab, flip_g, moving, moved_outer, sends, keeps, came, relays, tokens_of, partner, odd_turns
     )
 
     keeps, came, moved_outer = list(keeps), list(came), list(moved_outer)
@@ -658,7 +659,7 @@
     totals[2] = second_sum(2)
     turns = list(turns)
     if square:
-        turns += [turn(last[i], i) for i in range(1, n_dp, 2)]
+        turns += [turn(value, 2 * i + 1) for i, value in enumerate(odd_turns)]
     outs = step(2, list(outs))
     tab, moved_outer, sends, came, totals, outs, turns = stage(
         tab, moved_outer, sends, came, totals, outs, turns

time: 315 us -> 308 us (0.978)
  waiting for transfers between devices: 97.9 us -> 93.8 us
    ppermute x23, waiting for transfers between devices: 47.9 us -> 42.4 us  [swap(): return lax.ppermute(value, 'fsdp', [(i, i ^ mask) for i in range(n)])]
    unnamed x50 -> x48, local copies, waits for them, and re-layouts: 7.66 us -> 5.9 us
  transfers between devices with their start and end apart: 46 -> 46, of which waited for: 15 -> 15; matrix products, arithmetic and copies ran while one was open for 6% -> 6% of each run, Pallas kernels for 41% -> 42%
where the time goes in v5:
time: 308 us; the launch traced here: 306 us
  Pallas kernels  132 us (43%)
  waiting for transfers between devices  93.8 us (30%)
  starting transfers between devices  51.7 us (17%)
  local copies, waits for them, and re-layouts  13.8 us (4%)
  other arithmetic  13.6 us (4%)
    pallas_call x4, Pallas kernels, adam_part(): pl.pallas_call(functools.partial(adam_kernel, n, len(pieces), len(grads),...  47.9 us
    ppermute x23, waiting for transfers between devices, swap(): return lax.ppermute(value, 'fsdp', [(i, i ^ mask) for i in range(n)])  42.4 us
    ppermute x9, waiting for transfers between devices, turn(): return lax.ppermute(value, 'dp', [(i, (i + steps) % n) for i in range(n)])  37.7 us
    pallas_call x4, Pallas kernels, forward_chunk(): pl.pallas_call(functools.partial(forward_kernel, sent), out_shape=[jax.Sh...  27.3 us
    pallas_call x3, Pallas kernels, edges(): pl.pallas_call(functools.partial(edges_kernel, n, mv, count, block, start...  18.8 us
    ppermute x6, starting transfers between devices, swap_outer(): lax.ppermute(value, 'fsdp', [(i, j) for i, j in pairs if middle or {i, j}...  16.5 us
    ppermute x23, starting transfers between devices, swap(): return lax.ppermute(value, 'fsdp', [(i, i ^ mask) for i in range(n)])  16.5 us
    pallas_call x2, Pallas kernels, new_weights(): pl.pallas_call(functools.partial(weights_kernel, n), out_shape=jax.ShapeD...  12.2 us
  transfers between devices with their start and end apart: 46, of which 15 were waited for; matrix products, arithmetic and copies ran while one was open for 6% of the time, Pallas kernels for 42%

profile of v5, /device:TPU:11, one launch (start us, length us, event | category | flops | bytes accessed | tf_op | source)
XLA Modules:
  0.0 306.0 jit_solution(7377542094046917257)
XLA Ops:
  2.0 4.3 %shard_map.120 = (bf16[240,2048]{1,0:T(8,128)(2,1)}, bf16[240,2048]{1,0:T(8,128)(2,1)}) custom-call(s32[27]{0:T(128)} %concatenate.6.tab, f32[624,4096]{1,0:T(8,128)} %bitcast.82), custom_call_target="tpu_custom_call" | custom-call | flops 1 | bytes 1 | tf_op jit(solution)/shard_map/pallas_call | solution.py:171
  7.1 3.0 collective-permute-start.1
  11.0 4.2 %shard_map.121 = (bf16[240,2048]{1,0:T(8,128)(2,1)}, bf16[240,2048]{1,0:T(8,128)(2,1)}) custom-call(s32[27]{0:T(128)} %concatenate.6.tab, f32[624,4096]{1,0:T(8,128)} %bitcast.83), custom_call_target="tpu_custom_call" | custom-call | flops 1 | bytes 1 | tf_op jit(solution)/shard_map/pallas_call | solution.py:171
  15.2 10.3 %shard_map.123 = (bf16[240,8192]{1,0:T(8,128)(2,1)}, bf16[240,2048]{1,0:T(8,128)(2,1)}, bf16[240,2048]{1,0:T(8,128)(2,1)}, bf16[240,2048]{1,0:T(8,128)(2,1)}, bf16[240,2048]{1,0:T(8,128)(2,1)}) custom-call(s32[27]{0:T(128)} %concatenate.6.tab, f32[624,4096]{1,0:T(8,128)} %bitcast.90, f32[624,4096]{1,0:T(8,128)} %bitcast.95), custom_call_target="tpu_custom_call" | custom-call | flops 1 | bytes 1 | tf_op jit(solution)/shard_map/pallas_call | solution.py:171
  25.5 5.0 %shard_map.122 = (bf16[2,624,256]{2,1,0:T(8,128)(2,1)}, bf16[2,624,256]{2,1,0:T(8,128)(2,1)}, bf16[2,624,256]{2,1,0:T(8,128)(2,1)}, bf16[2,624,256]{2,1,0:T(8,128)(2,1)}) custom-call(s32[27]{0:T(128)} %concatenate.6.tab, bf16[256,3712]{1,0:T(8,128)(2,1)} %gate.1, bf16[256,3712]{1,0:T(8,128)(2,1)} %up.1), custom_call_target="tpu_custom_call" | custom-call | flops 1 | bytes 1 | tf_op jit(solution)/shard_map/pallas_call | solution.py:120
  31.6 3.8 %collective-permute-done.2.refs_6_.refs_7_ = bf16[64,4096]{1,0:T(8,128)(2,1)} collective-permute-done((bf16[64,4096]{1,0:T(8,128)(2,1)S(1)}, bf16[64,4096]{1,0:T(8,128)(2,1)}, u32[]{:S(2)}, u32[]{:S(2)}) %collective-permute-start.2) | collective-permute-done | bytes 524320 | tf_op jit(solution)/shard_map/ppermute | solution.py:442
  35.9 3.1 %collective-permute-start.4 = (bf16[240,2048]{1,0:T(8,128)(2,1)}, bf16[240,2048]{1,0:T(8,128)(2,1)}, u32[]{:S(2)}, u32[]{:S(2)}) collective-permute-start(bf16[240,2048]{1,0:T(8,128)(2,1)} %get-tuple-element.203), channel_id=1, source_target_pairs={{1,2},{2,1},{3,4},{4,3},{5,6},{6,5},{9,10},{10,9},{11,12},{12,11},... | collective-permute-start | bytes 2949128 | tf_op jit(solution)/shard_map/ppermute | solution.py:448
  39.4 6.1 %shard_map.124.refs_4_ = bf16[2,624,1024]{2,1,0:T(8,128)(2,1)} custom-call(s32[27]{0:T(128)} %concatenate.6.tab, f32[624,4096]{1,0:T(8,128)} %bitcast.84, bf16[240,2048]{1,0:T(8,128)(2,1)} %copy-done.8, bf16[240,2048]{1,0:T(8,128)(2,1)} %collective-permute-done.1.outer.refs_21_), custom_call_target="tpu_custom_call" | custom-call | flops 1 | bytes 1 | tf_op jit(solution)/shard_map/pallas_call | solution.py:213
  45.5 17.7 %collective-permute-done.5.refs_7_.refs_8_ = bf16[64,4096]{1,0:T(8,128)(2,1)S(1)} collective-permute-done((bf16[64,4096]{1,0:T(8,128)(2,1)}, bf16[64,4096]{1,0:T(8,128)(2,1)S(1)}, u32[]{:S(2)}, u32[]{:S(2)}) %collective-permute-start.5) | collective-permute-done | bytes 524320 | tf_op jit(solution)/shard_map/ppermute | solution.py:442
  69.3 6.1 %shard_map.125.refs_4_ = bf16[2,624,1024]{2,1,0:T(8,128)(2,1)} custom-call(s32[27]{0:T(128)} %concatenate.6.tab, f32[624,4096]{1,0:T(8,128)} %bitcast.85, bf16[240,2048]{1,0:T(8,128)(2,1)} %collective-permute-done.3.inner.refs_20_, bf16[240,2048]{1,0:T(8,128)(2,1)} %collective-permute-done.4.outer.refs_22_), custom_call_target="tpu_custom_call" | custom-call | flops 1 | bytes 1 | tf_op jit(solution)/shard_map/pallas_call | solution.py:213
  75.4 4.2 %collective-permute-done.8.refs_11_.refs_12_ = bf16[64,4096]{1,0:T(8,128)(2,1)S(1)} collective-permute-done((bf16[64,4096]{1,0:T(8,128)(2,1)}, bf16[64,4096]{1,0:T(8,128)(2,1)S(1)}, u32[]{:S(2)}, u32[]{:S(2)}) %collective-permute-start.8) | collective-permute-done | bytes 524320 | tf_op jit(solution)/shard_map/ppermute | solution.py:495
  79.6 14.6 %collective-permute-done.10.piece.refs_2_ = bf16[2,624,256]{2,1,0:T(8,128)(2,1)S(1)} collective-permute-done((bf16[2,624,256]{2,1,0:T(8,128)(2,1)}, bf16[2,624,256]{2,1,0:T(8,128)(2,1)S(1)}, u32[]{:S(2)}, u32[]{:S(2)}) %collective-permute-start.10) | collective-permute-done | bytes 639008 | tf_op jit(solution)/shard_map/ppermute | solution.py:442
  96.4 4.1 %collective-permute-start.15 = (bf16[240,2048]{1,0:T(8,128)(2,1)}, bf16[240,2048]{1,0:T(8,128)(2,1)}, u32[]{:S(2)}, u32[]{:S(2)}) collective-permute-start(bf16[240,2048]{1,0:T(8,128)(2,1)} %get-tuple-element.269), channel_id=1, source_target_pairs={{3,7},{4,0},{11,15},{12,8},{19,23},{20,16},{27,31},{28,24}} | collective-permute-start | bytes 2949128 | tf_op jit(solution)/shard_map/ppermute | solution.py:452
  109.7 6.8 %shard_map.131 = bf16[4,4,256,256]{3,2,1,0:T(8,128)(2,1)} custom-call(s32[27]{0:T(128)} %concatenate.6.tab, bf16[256,1248]{1,0:T(8,128)(2,1)} %shard_map.127.refs_0_, bf16[256,1248]{1,0:T(8,128)(2,1)} %shard_map.128.refs_1_, bf16[256,1248]{1,0:T(8,128)(2,1)} %shard_map.126.refs_2_, bf16[256,1248]{1,0:T(8,128)(2,1)} %shard_map.129.refs_3_, ...), custom_call_target="tpu_custom_call" | custom-call | flops 1 | bytes 1 | tf_op jit(solution)/shard_map/pallas_call | solution.py:286
  116.5 6.8 %shard_map.130 = (bf16[2,4,256,256]{3,2,1,0:T(8,128)(2,1)}, bf16[2,4,256,256]{3,2,1,0:T(8,128)(2,1)}) custom-call(s32[27]{0:T(128)} %concatenate.6.tab, bf16[256,1248]{1,0:T(8,128)(2,1)} %shard_map.127.refs_0_, bf16[256,1248]{1,0:T(8,128)(2,1)} %shard_map.128.refs_1_, bf16[256,1248]{1,0:T(8,128)(2,1)} %shard_map.126.refs_2_, ...), custom_call_target="tpu_custom_call" | custom-call | flops 1 | bytes 1 | tf_op jit(solution)/shard_map/pallas_call | solution.py:286
  124.9 4.9 %collective-permute-start.19 = (bf16[240,2048]{1,0:T(8,128)(2,1)}, bf16[240,2048]{1,0:T(8,128)(2,1)}, u32[]{:S(2)}, u32[]{:S(2)}) collective-permute-start(bf16[240,2048]{1,0:T(8,128)(2,1)} %get-tuple-element.248), channel_id=1, source_target_pairs={{1,2},{2,1},{3,4},{4,3},{5,6},{6,5},{9,10},{10,9},{11,12},{12,11},... | collective-permute-start | bytes 2949128 | tf_op jit(solution)/shard_map/ppermute | solution.py:448
  135.8 6.8 %shard_map.133 = (bf16[2,4,256,256]{3,2,1,0:T(8,128)(2,1)}, bf16[2,4,256,256]{3,2,1,0:T(8,128)(2,1)}) custom-call(s32[27]{0:T(128)} %concatenate.6.tab, bf16[256,1248]{1,0:T(8,128)(2,1)} %shard_map.127.refs_0_, bf16[256,1248]{1,0:T(8,128)(2,1)} %shard_map.128.refs_1_, bf16[256,1248]{1,0:T(8,128)(2,1)} %shard_map.126.refs_2_, ...), custom_call_target="tpu_custom_call" | custom-call | flops 1 | bytes 1 | tf_op jit(solution)/shard_map/pallas_call | solution.py:286
  142.6 6.9 %shard_map.132 = (bf16[2,4,256,256]{3,2,1,0:T(8,128)(2,1)}, bf16[2,4,256,256]{3,2,1,0:T(8,128)(2,1)}) custom-call(s32[27]{0:T(128)} %concatenate.6.tab, bf16[256,1248]{1,0:T(8,128)(2,1)} %shard_map.127.refs_0_, bf16[256,1248]{1,0:T(8,128)(2,1)} %shard_map.128.refs_1_, bf16[256,1248]{1,0:T(8,128)(2,1)} %shard_map.126.refs_2_, ...), custom_call_target="tpu_custom_call" | custom-call | flops 1 | bytes 1 | tf_op jit(solution)/shard_map/pallas_call | solution.py:286
  149.5 12.1 %collective-permute-done.21 = bf16[4,256,256]{2,1,0:T(8,128)(2,1)} collective-permute-done((bf16[4,256,256]{2,1,0:T(8,128)(2,1)}, bf16[4,256,256]{2,1,0:T(8,128)(2,1)}, u32[]{:S(2)}, u32[]{:S(2)}) %collective-permute-start.21) | collective-permute-done | bytes 524320 | tf_op jit(solution)/shard_map/ppermute | solution.py:461
  167.6 11.4 %shard_map.134 = bf16[624,4096]{1,0:T(8,128)(2,1)} custom-call(s32[27]{0:T(128)} %concatenate.6.tab, bf16[2,624,256]{2,1,0:T(8,128)(2,1)} %get-tuple-element.301.piece.refs_0_, bf16[2,624,256]{2,1,0:T(8,128)(2,1)} %collective-permute-done.9.piece.refs_1_, bf16[2,624,256]{2,1,0:T(8,128)(2,1)} %copy-done.9, bf16[2,624,256]{2,1,0:T(8,128)(2,1)} %copy-done.3, ...), custom_call_target="tpu_custom_call" | custom-call | flops 1 | bytes 1 | tf_op jit(solution)/shard_map/pallas_call | solution.py:337
  180.1 9.4 %collective-permute-done.25.refs_25_ = bf16[240,2048]{1,0:T(8,128)(2,1)} collective-permute-done((bf16[240,2048]{1,0:T(8,128)(2,1)}, bf16[240,2048]{1,0:T(8,128)(2,1)}, u32[]{:S(2)}, u32[]{:S(2)}) %collective-permute-start.25) | collective-permute-done | bytes 983072 | tf_op jit(solution)/shard_map/ppermute | solution.py:456
  190.1 3.2 %collective-permute-start.29 = (bf16[240,2048]{1,0:T(8,128)(2,1)}, bf16[240,2048]{1,0:T(8,128)(2,1)}, u32[]{:S(2)}, u32[]{:S(2)}) collective-permute-start(bf16[240,2048]{1,0:T(8,128)(2,1)} %get-tuple-element.293), channel_id=1, source_target_pairs={{1,2},{2,1},{3,4},{4,3},{5,6},{6,5},{9,10},{10,9},{11,12},{12,11},... | collective-permute-start | bytes 2949128 | tf_op jit(solution)/shard_map/ppermute | solution.py:448
  195.6 4.2 %collective-permute-done.28.refs_14_ = bf16[128,4096]{1,0:T(8,128)(2,1)S(1)} collective-permute-done((bf16[128,4096]{1,0:T(8,128)(2,1)}, bf16[128,4096]{1,0:T(8,128)(2,1)S(1)}, u32[]{:S(2)}, u32[]{:S(2)}) %collective-permute-start.28) | collective-permute-done | bytes 1048608 | tf_op jit(solution)/shard_map/ppermute | solution.py:442
  203.0 11.7 %shard_map.135 = (f32[624,4096]{1,0:T(8,128)}, f32[624,4096]{1,0:T(8,128)}, f32[624,4096]{1,0:T(8,128)}) custom-call(s32[27]{0:T(128)} %concatenate.6.tab, bf16[2,624,256]{2,1,0:T(8,128)(2,1)} %get-tuple-element.301.piece.refs_0_, bf16[2,624,256]{2,1,0:T(8,128)(2,1)} %collective-permute-done.9.piece.refs_1_, bf16[2,624,256]{2,1,0:T(8,128)(2,1)} %copy-done.9, ...), custom_call_target="tpu_custom_call" | custom-call | flops 1 | bytes 1 | tf_op jit(solution)/shard_map/pallas_call | solution.py:414
  214.8 12.2 %shard_map.136 = (f32[624,4096]{1,0:T(8,128)}, f32[624,4096]{1,0:T(8,128)}, f32[624,4096]{1,0:T(8,128)}) custom-call(s32[27]{0:T(128)} %concatenate.6.tab, bf16[2,624,256]{2,1,0:T(8,128)(2,1)} %get-tuple-element.301.piece.refs_0_, ...), custom_call_target="tpu_custom_call", output_to_operand_aliasing={{0}: (27, {}), {1}: (28, {}), {2}: (29, {})} | custom-call | flops 1 | bytes 1 | tf_op jit(solution)/shard_map/pallas_call | solution.py:414
  232.6 3.3 %collective-permute-start.34 = (bf16[4,256,256]{2,1,0:T(8,128)(2,1)S(1)}, bf16[4,256,256]{2,1,0:T(8,128)(2,1)S(1)}, u32[]{:S(2)}, u32[]{:S(2)}) collective-permute-start(bf16[4,256,256]{2,1,0:T(8,128)(2,1)S(1)} %fusion.6), channel_id=1, source_target_pairs={{0,2},{1,3},{2,0},{3,1},{4,6},{5,7},{6,4},{7,5},{8,10},{9,11},{10,... | collective-permute-start | bytes 1572872 | tf_op jit(solution)/shard_map/ppermute | solution.py:442
  236.0 11.8 %shard_map.137 = (f32[624,4096]{1,0:T(8,128)}, f32[624,4096]{1,0:T(8,128)}, f32[624,4096]{1,0:T(8,128)}) custom-call(s32[27]{0:T(128)} %concatenate.6.tab, bf16[2,624,256]{2,1,0:T(8,128)(2,1)} %get-tuple-element.301.piece.refs_0_, ...), custom_call_target="tpu_custom_call", output_to_operand_aliasing={{0}: (26, {}), {1}: (27, {}), {2}: (28, {})} | custom-call | flops 1 | bytes 1 | tf_op jit(solution)/shard_map/pallas_call | solution.py:414
  247.8 8.1 %collective-permute-done.36 = bf16[4,256,256]{2,1,0:T(8,128)(2,1)} collective-permute-done((bf16[4,256,256]{2,1,0:T(8,128)(2,1)}, bf16[4,256,256]{2,1,0:T(8,128)(2,1)}, u32[]{:S(2)}, u32[]{:S(2)}) %collective-permute-start.36) | collective-permute-done | bytes 524320 | tf_op jit(solution)/shard_map/ppermute | solution.py:461
  267.4 12.1 %shard_map.138 = (f32[624,4096]{1,0:T(8,128)}, f32[624,4096]{1,0:T(8,128)}, f32[624,4096]{1,0:T(8,128)}) custom-call(s32[27]{0:T(128)} %concatenate.6.tab, bf16[2,624,256]{2,1,0:T(8,128)(2,1)} %get-tuple-element.301.piece.refs_0_, ...), custom_call_target="tpu_custom_call", output_to_operand_aliasing={{0}: (27, {}), {1}: (28, {}), {2}: (29, {})} | custom-call | flops 1 | bytes 1 | tf_op jit(solution)/shard_map/pallas_call | solution.py:414
  279.6 4.8 %collective-permute-done.38 = bf16[2,256,256]{2,1,0:T(8,128)(2,1)} collective-permute-done((bf16[2,256,256]{2,1,0:T(8,128)(2,1)}, bf16[2,256,256]{2,1,0:T(8,128)(2,1)}, u32[]{:S(2)}, u32[]{:S(2)}) %collective-permute-start.38) | collective-permute-done | bytes 262176 | tf_op jit(solution)/shard_map/ppermute | solution.py:461
  284.4 3.4 %collective-permute-done.39 = bf16[2,256,256]{2,1,0:T(8,128)(2,1)} collective-permute-done((bf16[2,256,256]{2,1,0:T(8,128)(2,1)}, bf16[2,256,256]{2,1,0:T(8,128)(2,1)}, u32[]{:S(2)}, u32[]{:S(2)}) %collective-permute-start.39) | collective-permute-done | bytes 262176 | tf_op jit(solution)/shard_map/ppermute | solution.py:461
  297.3 7.5 %collective-permute-done.45 = bf16[256,256]{1,0:T(8,128)(2,1)S(1)} collective-permute-done((bf16[256,256]{1,0:T(8,128)(2,1)S(1)}, bf16[256,256]{1,0:T(8,128)(2,1)S(1)}, u32[]{:S(2)}, u32[]{:S(2)}) %collective-permute-start.45) | collective-permute-done | bytes 131104 | tf_op jit(solution)/shard_map/ppermute | solution.py:461
  (149 shorter events, 70.7 us)
Async XLA Ops:
  6.3 29.0 %collective-permute-start = (bf16[240,2048]{1,0:T(8,128)(2,1)}, bf16[240,2048]{1,0:T(8,128)(2,1)S(1)}, u32[]{:S(2)}, u32[]{:S(2)}) collective-permute-start(bf16[240,2048]{1,0:T(8,128)(2,1)} %get-tuple-element.185), channel_id=1, source_target_pairs={{0,1},{1,0},{2,3},{3,2},{4,5},{5,4},{6,7},{7,6},{8,9},{9,8},{10,11... | collective-permute-start | bytes 2949128 | tf_op jit(solution)/shard_map/ppermute | solution.py:442
  7.1 28.3 %collective-permute-start.1 = (bf16[240,2048]{1,0:T(8,128)(2,1)}, bf16[240,2048]{1,0:T(8,128)(2,1)}, u32[]{:S(2)}, u32[]{:S(2)}) collective-permute-start(bf16[240,2048]{1,0:T(8,128)(2,1)} %get-tuple-element.187), channel_id=1, source_target_pairs={{1,2},{2,1},{3,4},{4,3},{5,6},{6,5},{9,10},{10,9},{11,12},{12,11},... | collective-permute-start | bytes 2949128 | tf_op jit(solution)/shard_map/ppermute | solution.py:448
  11.0 24.3 %collective-permute-start.2 = (bf16[64,4096]{1,0:T(8,128)(2,1)S(1)}, bf16[64,4096]{1,0:T(8,128)(2,1)}, u32[]{:S(2)}, u32[]{:S(2)}) collective-permute-start(bf16[64,4096]{1,0:T(8,128)(2,1)S(1)} %get-tuple-element.365), channel_id=1, source_target_pairs={{0,4},{1,5},{2,6},{3,7},{4,0},{5,1},{6,2},{7,3},{8,12},{9,13},{10,... | collective-permute-start | bytes 1572872 | tf_op jit(solution)/shard_map/ppermute | solution.py:442
  35.4 27.8 %collective-permute-start.7 = (bf16[240,8192]{1,0:T(8,128)(2,1)}, bf16[240,8192]{1,0:T(8,128)(2,1)S(1)}, u32[]{:S(2)}, u32[]{:S(2)}) collective-permute-start(bf16[240,8192]{1,0:T(8,128)(2,1)} %get-tuple-element.211), channel_id=1, source_target_pairs={{0,1},{1,0},{2,3},{3,2},{4,5},{5,4},{6,7},{7,6},{8,9},{9,8},{10,11... | collective-permute-start | bytes 11796488 | tf_op jit(solution)/shard_map/ppermute | solution.py:442
  35.8 27.4 %collective-permute-start.3 = (bf16[240,2048]{1,0:T(8,128)(2,1)}, bf16[240,2048]{1,0:T(8,128)(2,1)}, u32[]{:S(2)}, u32[]{:S(2)}) collective-permute-start(bf16[240,2048]{1,0:T(8,128)(2,1)} %get-tuple-element.201), channel_id=1, source_target_pairs={{0,1},{1,0},{2,3},{3,2},{4,5},{5,4},{6,7},{7,6},{8,9},{9,8},{10,11... | collective-permute-start | bytes 2949128 | tf_op jit(solution)/shard_map/ppermute | solution.py:442
  35.9 27.2 %collective-permute-start.4 = (bf16[240,2048]{1,0:T(8,128)(2,1)}, bf16[240,2048]{1,0:T(8,128)(2,1)}, u32[]{:S(2)}, u32[]{:S(2)}) collective-permute-start(bf16[240,2048]{1,0:T(8,128)(2,1)} %get-tuple-element.203), channel_id=1, source_target_pairs={{1,2},{2,1},{3,4},{4,3},{5,6},{6,5},{9,10},{10,9},{11,12},{12,11},... | collective-permute-start | bytes 2949128 | tf_op jit(solution)/shard_map/ppermute | solution.py:448
  39.0 24.1 %collective-permute-start.5 = (bf16[64,4096]{1,0:T(8,128)(2,1)}, bf16[64,4096]{1,0:T(8,128)(2,1)S(1)}, u32[]{:S(2)}, u32[]{:S(2)}) collective-permute-start(bf16[64,4096]{1,0:T(8,128)(2,1)} %get-tuple-element.206), channel_id=1, source_target_pairs={{0,4},{1,5},{2,6},{3,7},{4,0},{5,1},{6,2},{7,3},{8,12},{9,13},{10,... | collective-permute-start | bytes 1572872 | tf_op jit(solution)/shard_map/ppermute | solution.py:442
  39.1 24.0 %collective-permute-start.6 = (bf16[64,4096]{1,0:T(8,128)(2,1)}, bf16[64,4096]{1,0:T(8,128)(2,1)}, u32[]{:S(2)}, u32[]{:S(2)}) collective-permute-start(bf16[64,4096]{1,0:T(8,128)(2,1)} %collective-permute-done.2.refs_6_.refs_7_), channel_id=1, source_target_pairs={{0,8},{8,0},{16,24},{24,16},{1,9},{9,1},{17,25},{25,17},{2,10},{10... | collective-permute-start | bytes 1572872 | tf_op jit(solution)/shard_map/ppermute | solution.py:495
  64.0 31.1 %collective-permute-start.12 = (bf16[2,624,1024]{2,1,0:T(8,128)(2,1)}, bf16[2,624,1024]{2,1,0:T(8,128)(2,1)}, u32[]{:S(2)}, u32[]{:S(2)}) collective-permute-start(bf16[2,624,1024]{2,1,0:T(8,128)(2,1)} %shard_map.124.refs_4_), channel_id=1, source_target_pairs={{0,1},{1,0},{2,3},{3,2},{4,5},{5,4},{6,7},{7,6},{8,9},{9,8},{10,11... | collective-permute-start | bytes 7667720 | tf_op jit(solution)/shard_map/ppermute | solution.py:442
  64.4 29.8 %collective-permute-start.10 = (bf16[2,624,256]{2,1,0:T(8,128)(2,1)}, bf16[2,624,256]{2,1,0:T(8,128)(2,1)S(1)}, u32[]{:S(2)}, u32[]{:S(2)}) collective-permute-start(bf16[2,624,256]{2,1,0:T(8,128)(2,1)} %get-tuple-element.226), channel_id=1, source_target_pairs={{0,4},{1,5},{2,6},{3,7},{4,0},{5,1},{6,2},{7,3},{8,12},{9,13},{10,... | collective-permute-start | bytes 1916936 | tf_op jit(solution)/shard_map/ppermute | solution.py:442
  64.4 29.8 %collective-permute-start.11 = (bf16[2,624,256]{2,1,0:T(8,128)(2,1)}, bf16[2,624,256]{2,1,0:T(8,128)(2,1)S(1)}, u32[]{:S(2)}, u32[]{:S(2)}) collective-permute-start(bf16[2,624,256]{2,1,0:T(8,128)(2,1)} %get-tuple-element.227), channel_id=1, source_target_pairs={{0,6},{1,7},{2,4},{3,5},{4,2},{5,3},{6,0},{7,1},{8,14},{9,15},{10,... | collective-permute-start | bytes 1916936 | tf_op jit(solution)/shard_map/ppermute | solution.py:442
  65.3 29.8 %collective-permute-start.9 = (bf16[2,624,256]{2,1,0:T(8,128)(2,1)}, bf16[2,624,256]{2,1,0:T(8,128)(2,1)}, u32[]{:S(2)}, u32[]{:S(2)}) collective-permute-start(bf16[2,624,256]{2,1,0:T(8,128)(2,1)} %get-tuple-element.225), channel_id=1, source_target_pairs={{0,2},{1,3},{2,0},{3,1},{4,6},{5,7},{6,4},{7,5},{8,10},{9,11},{10,... | collective-permute-start | bytes 1916936 | tf_op jit(solution)/shard_map/ppermute | solution.py:442
  95.1 28.2 %collective-permute-start.14 = (bf16[2,624,1024]{2,1,0:T(8,128)(2,1)}, bf16[2,624,1024]{2,1,0:T(8,128)(2,1)S(1)}, u32[]{:S(2)}, u32[]{:S(2)}) collective-permute-start(bf16[2,624,1024]{2,1,0:T(8,128)(2,1)} %shard_map.125.refs_4_), channel_id=1, source_target_pairs={{0,1},{1,0},{2,3},{3,2},{4,5},{5,4},{6,7},{7,6},{8,9},{9,8},{10,11... | collective-permute-start | bytes 7667720 | tf_op jit(solution)/shard_map/ppermute | solution.py:442
  96.4 26.9 %collective-permute-start.13 = (bf16[128,4096]{1,0:T(8,128)(2,1)}, bf16[128,4096]{1,0:T(8,128)(2,1)S(1)}, u32[]{:S(2)}, u32[]{:S(2)}) collective-permute-start(bf16[128,4096]{1,0:T(8,128)(2,1)} %constant_dynamic-slice_fusion.2), channel_id=1, source_target_pairs={{0,2},{1,3},{2,0},{3,1},{4,6},{5,7},{6,4},{7,5},{8,10},{9,11},{10,... | collective-permute-start | bytes 3145736 | tf_op jit(solution)/shard_map/ppermute | solution.py:442
  96.4 26.9 %collective-permute-start.15 = (bf16[240,2048]{1,0:T(8,128)(2,1)}, bf16[240,2048]{1,0:T(8,128)(2,1)}, u32[]{:S(2)}, u32[]{:S(2)}) collective-permute-start(bf16[240,2048]{1,0:T(8,128)(2,1)} %get-tuple-element.269), channel_id=1, source_target_pairs={{3,7},{4,0},{11,15},{12,8},{19,23},{20,16},{27,31},{28,24}} | collective-permute-start | bytes 2949128 | tf_op jit(solution)/shard_map/ppermute | solution.py:452
  124.9 36.8 %collective-permute-start.17 = (bf16[128,4096]{1,0:T(8,128)(2,1)S(1)}, bf16[128,4096]{1,0:T(8,128)(2,1)S(1)}, u32[]{:S(2)}, u32[]{:S(2)}) collective-permute-start(bf16[128,4096]{1,0:T(8,128)(2,1)S(1)} %collective-permute-done.13.refs_5_.refs_6_), channel_id=1, source_target_pairs={{0,4},{1,5},{2,6},{3,7},{4,0},{5,1},{6,2},{7,3},{8,12},{9,13},{10,... | collective-permute-start | bytes 3145736 | tf_op jit(solution)/shard_map/ppermute | solution.py:442
  124.9 36.8 %collective-permute-start.18 = (bf16[128,4096]{1,0:T(8,128)(2,1)S(1)}, bf16[128,4096]{1,0:T(8,128)(2,1)S(1)}, u32[]{:S(2)}, u32[]{:S(2)}) collective-permute-start(bf16[128,4096]{1,0:T(8,128)(2,1)S(1)} %collective-permute-done.13.refs_5_.refs_6_), channel_id=1, source_target_pairs={{0,8},{8,0},{16,24},{24,16},{1,9},{9,1},{17,25},{25,17},{2,10},{10... | collective-permute-start | bytes 3145736 | tf_op jit(solution)/shard_map/ppermute | solution.py:495
  124.9 36.8 %collective-permute-start.19 = (bf16[240,2048]{1,0:T(8,128)(2,1)}, bf16[240,2048]{1,0:T(8,128)(2,1)}, u32[]{:S(2)}, u32[]{:S(2)}) collective-permute-start(bf16[240,2048]{1,0:T(8,128)(2,1)} %get-tuple-element.248), channel_id=1, source_target_pairs={{1,2},{2,1},{3,4},{4,3},{5,6},{6,5},{9,10},{10,9},{11,12},{12,11},... | collective-permute-start | bytes 2949128 | tf_op jit(solution)/shard_map/ppermute | solution.py:448
  129.7 31.9 %collective-permute-start.20 = (bf16[240,2048]{1,0:T(8,128)(2,1)}, bf16[240,2048]{1,0:T(8,128)(2,1)S(1)}, u32[]{:S(2)}, u32[]{:S(2)}) collective-permute-start(bf16[240,2048]{1,0:T(8,128)(2,1)} %collective-permute-done.15), channel_id=1, source_target_pairs={{7,4},{0,3},{15,12},{8,11},{23,20},{16,19},{31,28},{24,27}} | collective-permute-start | bytes 2949128 | tf_op jit(solution)/shard_map/ppermute | solution.py:456
  133.1 28.6 %collective-permute-start.21 = (bf16[4,256,256]{2,1,0:T(8,128)(2,1)}, bf16[4,256,256]{2,1,0:T(8,128)(2,1)}, u32[]{:S(2)}, u32[]{:S(2)}) collective-permute-start(bf16[4,256,256]{2,1,0:T(8,128)(2,1)} %slice_bitcast_fusion.2), channel_id=1, source_target_pairs={{0,16},{8,24},{16,0},{24,8},{1,17},{9,25},{17,1},{25,9},{2,18},{10... | collective-permute-start | bytes 1572872 | tf_op jit(solution)/shard_map/ppermute | solution.py:461
  161.7 27.8 %collective-permute-start.22 = (bf16[128,4096]{1,0:T(8,128)(2,1)S(1)}, bf16[128,4096]{1,0:T(8,128)(2,1)}, u32[]{:S(2)}, u32[]{:S(2)}) collective-permute-start(bf16[128,4096]{1,0:T(8,128)(2,1)S(1)} %collective-permute-done.17.refs_8_.refs_9_), channel_id=1, source_target_pairs={{0,8},{8,0},{16,24},{24,16},{1,9},{9,1},{17,25},{25,17},{2,10},{10... | collective-permute-start | bytes 3145736 | tf_op jit(solution)/shard_map/ppermute | solution.py:495
  161.8 27.7 %collective-permute-start.24 = (bf16[2,4,256,256]{3,2,1,0:T(8,128)(2,1)}, bf16[2,4,256,256]{3,2,1,0:T(8,128)(2,1)}, u32[]{:S(2)}, u32[]{:S(2)}) collective-permute-start(bf16[2,4,256,256]{3,2,1,0:T(8,128)(2,1)} %get-tuple-element.274), channel_id=1, source_target_pairs={{0,4},{1,5},{2,6},{3,7},{4,0},{5,1},{6,2},{7,3},{8,12},{9,13},{10,... | collective-permute-start | bytes 3145736 | tf_op jit(solution)/shard_map/ppermute | solution.py:442
  165.0 24.5 %collective-permute-start.25 = (bf16[240,2048]{1,0:T(8,128)(2,1)}, bf16[240,2048]{1,0:T(8,128)(2,1)}, u32[]{:S(2)}, u32[]{:S(2)}) collective-permute-start(bf16[240,2048]{1,0:T(8,128)(2,1)} %collective-permute-done.16), channel_id=1, source_target_pairs={{7,4},{0,3},{15,12},{8,11},{23,20},{16,19},{31,28},{24,27}} | collective-permute-start | bytes 2949128 | tf_op jit(solution)/shard_map/ppermute | solution.py:456
  190.1 37.0 %collective-permute-start.30 = (bf16[2,4,256,256]{3,2,1,0:T(8,128)(2,1)}, bf16[2,4,256,256]{3,2,1,0:T(8,128)(2,1)}, u32[]{:S(2)}, u32[]{:S(2)}) collective-permute-start(bf16[2,4,256,256]{3,2,1,0:T(8,128)(2,1)} %get-tuple-element.298), channel_id=1, source_target_pairs={{0,4},{1,5},{2,6},{3,7},{4,0},{5,1},{6,2},{7,3},{8,12},{9,13},{10,... | collective-permute-start | bytes 3145736 | tf_op jit(solution)/shard_map/ppermute | solution.py:442
  190.1 37.0 %collective-permute-start.29 = (bf16[240,2048]{1,0:T(8,128)(2,1)}, bf16[240,2048]{1,0:T(8,128)(2,1)}, u32[]{:S(2)}, u32[]{:S(2)}) collective-permute-start(bf16[240,2048]{1,0:T(8,128)(2,1)} %get-tuple-element.293), channel_id=1, source_target_pairs={{1,2},{2,1},{3,4},{4,3},{5,6},{6,5},{9,10},{10,9},{11,12},{12,11},... | collective-permute-start | bytes 2949128 | tf_op jit(solution)/shard_map/ppermute | solution.py:448
  195.4 31.6 %collective-permute-start.31 = (bf16[4,256,256]{2,1,0:T(8,128)(2,1)}, bf16[4,256,256]{2,1,0:T(8,128)(2,1)}, u32[]{:S(2)}, u32[]{:S(2)}) collective-permute-start(bf16[4,256,256]{2,1,0:T(8,128)(2,1)} %fusion.5), channel_id=1, source_target_pairs={{0,2},{1,3},{2,0},{3,1},{4,6},{5,7},{6,4},{7,5},{8,10},{9,11},{10,... | collective-permute-start | bytes 1572872 | tf_op jit(solution)/shard_map/ppermute | solution.py:442
  227.1 29.2 %collective-permute-start.33 = (bf16[2,4,256,256]{3,2,1,0:T(8,128)(2,1)}, bf16[2,4,256,256]{3,2,1,0:T(8,128)(2,1)S(1)}, u32[]{:S(2)}, u32[]{:S(2)}) collective-permute-start(bf16[2,4,256,256]{3,2,1,0:T(8,128)(2,1)} %get-tuple-element.321), channel_id=1, source_target_pairs={{0,4},{1,5},{2,6},{3,7},{4,0},{5,1},{6,2},{7,3},{8,12},{9,13},{10,... | collective-permute-start | bytes 3145736 | tf_op jit(solution)/shard_map/ppermute | solution.py:442
  229.0 27.3 %collective-permute-start.32 = (bf16[240,2048]{1,0:T(8,128)(2,1)}, bf16[240,2048]{1,0:T(8,128)(2,1)S(1)}, u32[]{:S(2)}, u32[]{:S(2)}) collective-permute-start(bf16[240,2048]{1,0:T(8,128)(2,1)} %get-tuple-element.319), channel_id=1, source_target_pairs={{1,2},{2,1},{5,6},{6,5},{9,10},{10,9},{13,14},{14,13},{17,18},{18,... | collective-permute-start | bytes 2949128 | tf_op jit(solution)/shard_map/ppermute | solution.py:448
  231.3 24.6 %collective-permute-start.36 = (bf16[4,256,256]{2,1,0:T(8,128)(2,1)}, bf16[4,256,256]{2,1,0:T(8,128)(2,1)}, u32[]{:S(2)}, u32[]{:S(2)}) collective-permute-start(bf16[4,256,256]{2,1,0:T(8,128)(2,1)} %get-tuple-element.334), channel_id=1, source_target_pairs={{0,24},{8,0},{16,8},{24,16},{1,25},{9,1},{17,9},{25,17},{2,26},{10... | collective-permute-start | bytes 1572872 | tf_op jit(solution)/shard_map/ppermute | solution.py:461
  232.6 23.6 %collective-permute-start.34 = (bf16[4,256,256]{2,1,0:T(8,128)(2,1)S(1)}, bf16[4,256,256]{2,1,0:T(8,128)(2,1)S(1)}, u32[]{:S(2)}, u32[]{:S(2)}) collective-permute-start(bf16[4,256,256]{2,1,0:T(8,128)(2,1)S(1)} %fusion.6), channel_id=1, source_target_pairs={{0,2},{1,3},{2,0},{3,1},{4,6},{5,7},{6,4},{7,5},{8,10},{9,11},{10,... | collective-permute-start | bytes 1572872 | tf_op jit(solution)/shard_map/ppermute | solution.py:442
  257.6 31.5 %collective-permute-start.41 = (bf16[4,256,256]{2,1,0:T(8,128)(2,1)}, bf16[4,256,256]{2,1,0:T(8,128)(2,1)}, u32[]{:S(2)}, u32[]{:S(2)}) collective-permute-start(bf16[4,256,256]{2,1,0:T(8,128)(2,1)} %fusion.7), channel_id=1, source_target_pairs={{0,2},{1,3},{2,0},{3,1},{4,6},{5,7},{6,4},{7,5},{8,10},{9,11},{10,... | collective-permute-start | bytes 1572872 | tf_op jit(solution)/shard_map/ppermute | solution.py:442
  263.9 24.0 %collective-permute-start.39 = (bf16[2,256,256]{2,1,0:T(8,128)(2,1)}, bf16[2,256,256]{2,1,0:T(8,128)(2,1)}, u32[]{:S(2)}, u32[]{:S(2)}) collective-permute-start(bf16[2,256,256]{2,1,0:T(8,128)(2,1)} %get-tuple-element.367), channel_id=1, source_target_pairs={{0,24},{8,0},{16,8},{24,16},{1,25},{9,1},{17,9},{25,17},{2,26},{10... | collective-permute-start | bytes 786440 | tf_op jit(solution)/shard_map/ppermute | solution.py:461
  (38 other events, 492.0 us)
